TPU v7x, 32 devices: a whole 2x2x4 slice. The times are simulated.
32 devices in a mesh: lat: 4 (over x, core), lon: 8 (over z, y).
Axes of the slice: x: 2, y: 2, z: 4, core: 2. Of those that a mesh axis runs over, the one named last changes fastest.
Arguments:
- fields: bfloat16 [128, 1024, 128], P('lat', 'lon'), may hold values from -6 to 6
- cotangent: bfloat16 [128, 1024, 128], P('lat', 'lon'), may hold values from -6 to 6
- kernel_bank: bfloat16 [256, 9, 128, 128], P(('lat', 'lon')), may hold values from -0.1875 to 0.1875
- block_expert: int32 [8, 64], P('lat', 'lon'), may hold values from 0 to 255, as said below
- owner: int32 [256], replicated, may hold values from 0 to 255, as said below
Outputs:
- outputs: bfloat16 [128, 1024, 128], P('lat', 'lon')
- grad_fields: bfloat16 [128, 1024, 128], P('lat', 'lon')
- grad_bank: float32 [256, 9, 128, 128], P(('lat', 'lon'))
Inputs may be any that keep to these rules, and one draw needn't show every extreme that they name: owner is a permutation: each expert is stored in exactly one row of kernel_bank. `block_expert`: call the lon column of expert e the value (owner[e] // 8) modulo the number of devices along lon. Among the 2 x 8 blocks of one device, at most 2 name experts of any one lon column; in every latitude band of devices one column is named by exactly 2 blocks of each device of that band.
All inputs are finite; a program needn't handle non-finite values.
Results may differ from a plain program's by a relative error of at most 0.0032.
Values may be sent and summed in bfloat16 or wider, within the bound.
No kernel may reach another device: no remote copies, remote signals or barrier semaphores. Data moves between devices by JAX's collectives and lax.ppermute only.
A program may use at most 192 MiB of HBM per device.

v0:
```python
import jax
import jax.numpy as jnp
from jax import lax
from jax.sharding import PartitionSpec as P

BS = 16
CAP = 2


def padded_2(array, sides, width):
    for axis, dim in sides:
        count, length = (lax.axis_size(axis), array.shape[dim])
        up = [(i, (i + 1) % count) for i in range(count)]
        down = [(j, i) for i, j in up]
        last = lax.slice_in_dim(array, length - width, length, axis=dim)
        initial = lax.slice_in_dim(array, 0, width, axis=dim)
        before = lax.ppermute(last, axis, up)
        after = lax.ppermute(initial, axis, down)
        array = jnp.concatenate([before, array, after], axis=dim)
    return array


def windows(source, along):
    blocks_n = (source.shape[along] - 2) // BS
    leading = lax.slice_in_dim(source, 0, BS * blocks_n, axis=along)
    trailing = lax.slice_in_dim(source, BS, BS * blocks_n + 2, axis=along)
    padding = [(0, 0)] * source.ndim
    padding[along] = (0, BS - 2)
    trailing = jnp.pad(trailing, padding)
    new_shape = source.shape[:along] + (blocks_n, BS) + source.shape[along + 1 :]
    leading = leading.reshape(new_shape)
    trailing = lax.slice_in_dim(trailing.reshape(new_shape), 0, 2, axis=along + 1)
    return jnp.concatenate([leading, trailing], axis=along + 1)


def tiles_to_grid(blocks):
    lat_blocks, lon_blocks, tile_rows, tile_cols, chans = blocks.shape
    return blocks.transpose(0, 2, 1, 3, 4).reshape(
        lat_blocks * tile_rows, lon_blocks * tile_cols, chans
    )


def place_portion(portion, row_shift, col_shift):
    padded = jnp.pad(
        portion, ((0, 0), (0, 0), (0, BS - portion.shape[2]), (0, BS - portion.shape[3]), (0, 0))
    )
    grid = tiles_to_grid(padded)
    return jnp.pad(grid, ((row_shift, BS - row_shift), (col_shift, BS - col_shift), (0, 0)))


def place_blocks(blocks):
    row_total = blocks.shape[0] * BS
    col_total = blocks.shape[1] * BS
    canvas = place_portion(blocks[:, :, :BS, :BS], 0, 0)
    canvas = canvas + place_portion(blocks[:, :, :BS, BS:], 0, BS)
    canvas = canvas + place_portion(blocks[:, :, BS:, :BS], BS, 0)
    canvas = canvas + place_portion(blocks[:, :, BS:, BS:], BS, BS)
    return canvas[: row_total + 2, : col_total + 2]


def expert_forward(patch_in, kernel_in):
    slot_total = patch_in.shape[0]
    total = jnp.zeros((slot_total, BS, BS, kernel_in.shape[3]), jnp.float32)
    for tap_index in range(9):
        row_off = tap_index // 3
        col_off = tap_index % 3
        window = patch_in[:, row_off : row_off + BS, col_off : col_off + BS]
        total = total + jnp.einsum(
            "sxyc,scd->sxyd", window, kernel_in[:, tap_index], preferred_element_type=jnp.float32
        )
    return total


def expert_backward(patch_in, cot_in, kernel_in, selector):
    edge = BS + 2
    cot_wide = jnp.pad(cot_in, ((0, 0), (2, 2), (2, 2), (0, 0)))
    spread = jnp.zeros(patch_in.shape, jnp.float32)
    grads = []
    for tap_index in range(9):
        row_off = tap_index // 3
        col_off = tap_index % 3
        window = patch_in[:, row_off : row_off + BS, col_off : col_off + BS]
        shifted = cot_wide[:, 2 - row_off : 2 - row_off + edge, 2 - col_off : 2 - col_off + edge]
        spread = spread + jnp.einsum(
            "sxyd,scd->sxyc", shifted, kernel_in[:, tap_index], preferred_element_type=jnp.float32
        )
        per_slot = jnp.einsum("sxyc,sxyd->scd", window, cot_in, preferred_element_type=jnp.float32)
        grads.append(jnp.einsum("su,scd->ucd", selector, per_slot, precision=lax.Precision.HIGHEST))
    return (spread, jnp.stack(grads, axis=1))


def local(fields, cotangent, kernel_bank, block_expert, owner):
    lon_count = lax.axis_size("lon")
    lat_count = lax.axis_size("lat")
    lat_index = lax.axis_index("lat")
    lat_blocks, lon_blocks = block_expert.shape
    height, width, chans = fields.shape
    per_device = kernel_bank.shape[0]
    block_total = lat_blocks * lon_blocks
    slot_total = lon_count * CAP
    edge = BS + 2
    extended = padded_2(fields, (("lat", 0), ("lon", 1)), 1)
    row_ids = jnp.arange(height + 2)
    keep_rows = ((row_ids > 0) | (lat_index > 0)) & (
        (row_ids < height + 1) | (lat_index < lat_count - 1)
    )
    extended = jnp.where(keep_rows[:, None, None], extended, jnp.zeros((), extended.dtype))
    patches = (
        windows(windows(extended, 0), 2)
        .transpose(0, 2, 1, 3, 4)
        .reshape(block_total, edge, edge, chans)
    )
    cot_blocks = cotangent.reshape(lat_blocks, BS, lon_blocks, BS, chans).transpose(0, 2, 1, 3, 4)
    cot_blocks = cot_blocks.reshape(block_total, BS, BS, chans)
    storage = owner[block_expert.reshape(-1)]
    group_ids = storage // per_device
    column = group_ids % lon_count
    local_ids = group_ids // lon_count * per_device + storage % per_device
    hits = (column[:, None] == jnp.arange(lon_count)[None, :]).astype(jnp.int32)
    rank_ids = jnp.sum(jnp.cumsum(hits, axis=0) * hits, axis=1) - 1
    target = column * CAP + rank_ids
    placing = (target[None, :] == jnp.arange(slot_total)[:, None]).astype(jnp.bfloat16)
    sent_patches = jnp.einsum(
        "sb,bxyc->sxyc", placing, patches, preferred_element_type=jnp.float32
    ).astype(jnp.bfloat16)
    sent_patches = sent_patches.reshape(lon_count, CAP, edge, edge, chans)
    sent_cot = jnp.einsum(
        "sb,bxyc->sxyc", placing, cot_blocks, preferred_element_type=jnp.float32
    ).astype(jnp.bfloat16)
    sent_cot = sent_cot.reshape(lon_count, CAP, BS, BS, chans)
    sent_ids = jnp.dot(
        placing, local_ids.astype(jnp.bfloat16), preferred_element_type=jnp.float32
    ).astype(jnp.bfloat16)
    sent_ids = sent_ids.reshape(lon_count, CAP)
    column_kernels = lax.all_gather(kernel_bank, "lat", axis=0, tiled=True)
    column_size = column_kernels.shape[0]
    arrived_patches, arrived_ids = (
        lax.all_to_all(sent_patches, "lon", split_axis=0, concat_axis=0, tiled=True),
        lax.all_to_all(sent_ids, "lon", split_axis=0, concat_axis=0, tiled=True),
    )
    patch_in = arrived_patches.reshape(slot_total, edge, edge, chans)
    slot_ids = arrived_ids.reshape(slot_total).astype(jnp.int32)
    kernel_in = jnp.take(column_kernels, slot_ids, axis=0)
    result = expert_forward(patch_in, kernel_in).astype(jnp.bfloat16)
    returned_out = lax.all_to_all(
        result.reshape(lon_count, CAP, BS, BS, chans),
        "lon",
        split_axis=0,
        concat_axis=0,
        tiled=True,
    )
    arrived_cot = lax.all_to_all(sent_cot, "lon", split_axis=0, concat_axis=0, tiled=True)
    cot_in = arrived_cot.reshape(slot_total, BS, BS, chans)
    selector = (slot_ids[:, None] == jnp.arange(column_size)[None, :]).astype(jnp.float32)
    spread, grads = expert_backward(patch_in, cot_in, kernel_in, selector)
    spread_send = spread.astype(jnp.bfloat16).reshape(lon_count, CAP, edge, edge, chans)
    returned_spread = lax.all_to_all(spread_send, "lon", split_axis=0, concat_axis=0, tiled=True)
    grad_bank = lax.psum_scatter(grads, "lat", scatter_dimension=0, tiled=True)
    out_blocks = jnp.einsum(
        "sb,sxyc->bxyc",
        placing,
        returned_out.reshape(slot_total, BS, BS, chans),
        preferred_element_type=jnp.float32,
    )
    outputs = tiles_to_grid(out_blocks.reshape(lat_blocks, lon_blocks, BS, BS, chans)).astype(
        jnp.bfloat16
    )
    spread_blocks = jnp.einsum(
        "sb,sxyc->bxyc",
        placing,
        returned_spread.reshape(slot_total, edge, edge, chans),
        preferred_element_type=jnp.float32,
    )
    canvas = place_blocks(spread_blocks.reshape(lat_blocks, lon_blocks, edge, edge, chans))
    framed = padded_2(canvas.astype(jnp.bfloat16), (("lat", 0), ("lon", 1)), 1).astype(canvas.dtype)
    result_grid = canvas[1 : height + 1, 1 : width + 1]
    result_grid = result_grid.at[:, 0].add(framed[2 : height + 2, 0])
    result_grid = result_grid.at[:, width - 1].add(framed[2 : height + 2, width + 3])
    upper_line = (
        framed[0, 2 : width + 2].at[0].add(framed[0, 0]).at[width - 1].add(framed[0, width + 3])
    )
    lower_line = (
        framed[height + 3, 2 : width + 2]
        .at[0]
        .add(framed[height + 3, 0])
        .at[width - 1]
        .add(framed[height + 3, width + 3])
    )
    upper_keep = jnp.where(lat_index > 0, 1.0, 0.0).astype(jnp.float32)
    lower_keep = jnp.where(lat_index < lat_count - 1, 1.0, 0.0).astype(jnp.float32)
    result_grid = result_grid.at[0].add(upper_line * upper_keep)
    result_grid = result_grid.at[height - 1].add(lower_line * lower_keep)
    return (outputs, result_grid.astype(jnp.bfloat16), grad_bank)


def solution(mesh):
    return jax.shard_map(
        local,
        mesh=mesh,
        in_specs=(
            P("lat", "lon", None),
            P("lat", "lon", None),
            P(("lat", "lon"), None, None, None),
            P("lat", "lon"),
            P(),
        ),
        out_specs=(
            P("lat", "lon", None),
            P("lat", "lon", None),
            P(("lat", "lon"), None, None, None),
        ),
        check_vma=False,
    )
```

profile of v0, /device:TPU:0, one launch (start us, length us, event | category | flops | bytes accessed | tf_op | source)
XLA Modules:
  0.0 276.3 jit_solution(3106196975117636467)
XLA Ops:
  9.9 7.3 %all-to-all-start.1 = ((bf16[8,1,2]{2,1,0:T(2,128)(2,1)}), bf16[8,1,2]{2,1,0:T(2,128)(2,1)S(1)}, u32[]{:S(2)}, u32[]{:S(2)}) async-start(bf16[8,1,2]{2,1,0:T(2,128)(2,1)} %all_to_all.24), calls=%async_computation.1 | async-start | bytes 8192 | tf_op jit(solution)/shard_map/all_to_all | solution.py:139
  19.4 4.2 %all-to-all-done.1 = bf16[8,1,2]{2,1,0:T(2,128)(2,1)S(1)} async-done(((bf16[8,1,2]{2,1,0:T(2,128)(2,1)}), bf16[8,1,2]{2,1,0:T(2,128)(2,1)S(1)}, u32[]{:S(2)}, u32[]{:S(2)}) %all-to-all-start.1) | async-done | bytes 64 | tf_op jit(solution)/shard_map/all_to_all | solution.py:139
  23.5 3.6 %all-to-all-start.3 = ((bf16[8,2,16,16,128]{4,1,3,2,0:T(2,128)(2,1)}), bf16[8,2,16,16,128]{4,1,3,2,0:T(2,128)(2,1)S(1)}, u32[]{:S(2)}, u32[]{:S(2)}) async-start(bf16[8,2,16,16,128]{4,1,3,2,0:T(2,128)(2,1)} %copy.35), calls=%async_computation.3 | async-start | bytes 2097152 | tf_op jit(solution)/shard_map/all_to_all | solution.py:152
  36.2 12.1 %collective-permute-done.2 = bf16[34,1,128]{2,1,0:T(2,128)(2,1)S(1)} collective-permute-done((bf16[34,1,128]{2,1,0:T(2,128)(2,1)S(1)}, bf16[34,1,128]{2,1,0:T(2,128)(2,1)S(1)}, u32[]{:S(2)}, u32[]{:S(2)}) %collective-permute-start.2) | collective-permute-done | bytes 8736 | tf_op jit(solution)/shard_map/ppermute | solution.py:17
  52.8 6.6 %all-to-all-start = ((bf16[8,2,18,18,128]{4,1,3,2,0:T(2,128)(2,1)}), bf16[8,2,18,18,128]{4,1,3,2,0:T(2,128)(2,1)}, u32[]{:S(2)}, u32[]{:S(2)}) async-start(bf16[8,2,18,18,128]{4,1,3,2,0:T(2,128)(2,1)} %copy.28), calls=%async_computation | async-start | bytes 2654208 | tf_op jit(solution)/shard_map/all_to_all | solution.py:138
  60.3 31.8 %all-to-all-done = bf16[8,2,18,18,128]{4,1,3,2,0:T(2,128)(2,1)} async-done(((bf16[8,2,18,18,128]{4,1,3,2,0:T(2,128)(2,1)}), bf16[8,2,18,18,128]{4,1,3,2,0:T(2,128)(2,1)}, u32[]{:S(2)}, u32[]{:S(2)}) %all-to-all-start) | async-done | bytes 1327136 | tf_op jit(solution)/shard_map/all_to_all | solution.py:138
  94.1 2.9 %bitcast_dynamic-update-slice_fusion.8 = f32[32,9,128,128]{3,0,2,1:T(8,128)} fusion(f32[16,128,128]{2,1,0:T(8,128)S(1)} %convolution_bitcast_fusion.8, s32[16]{0:T(128)S(1)} %reshape.502), kind=kOutput, calls=%fused_computation.26 | convolution fusion | flops 100663808 | bytes 3145792 | tf_op jit(solution)/shard_map/su,scd->ucd/dot_general | solution.py:88
  97.6 2.8 %bitcast_dynamic-update-slice_fusion.7 = f32[32,9,128,128]{3,0,2,1:T(8,128)} fusion(f32[32,9,128,128]{3,0,2,1:T(8,128)} %bitcast_dynamic-update-slice_fusion.8, f32[16,128,128]{2,1,0:T(8,128)S(1)} %convolution_bitcast_fusion.7, s32[16]{0:T(128)S(1)} %reshape.502), kind=kOutput, calls=%fused_computation.25 | convolution fusion | flops 100663808 | bytes 3145792 | tf_op jit(solution)/shard_map/su,scd->ucd/dot_general | solution.py:88
  101.0 2.9 %bitcast_dynamic-update-slice_fusion.6 = f32[32,9,128,128]{3,0,2,1:T(8,128)} fusion(f32[32,9,128,128]{3,0,2,1:T(8,128)} %bitcast_dynamic-update-slice_fusion.7, f32[16,128,128]{2,1,0:T(8,128)S(1)} %convolution_bitcast_fusion.6, s32[16]{0:T(128)S(1)} %reshape.502), kind=kOutput, calls=%fused_computation.24 | convolution fusion | flops 100663808 | bytes 3145792 | tf_op jit(solution)/shard_map/su,scd->ucd/dot_general | solution.py:88
  104.4 3.0 %bitcast_dynamic-update-slice_fusion.5 = f32[32,9,128,128]{3,0,2,1:T(8,128)} fusion(f32[32,9,128,128]{3,0,2,1:T(8,128)} %bitcast_dynamic-update-slice_fusion.6, f32[16,128,128]{2,1,0:T(8,128)S(1)} %convolution_bitcast_fusion.5, s32[16]{0:T(128)S(1)} %reshape.502), kind=kOutput, calls=%fused_computation.23 | convolution fusion | flops 100663808 | bytes 3145792 | tf_op jit(solution)/shard_map/su,scd->ucd/dot_general | solution.py:88
  108.0 2.9 %bitcast_dynamic-update-slice_fusion.4 = f32[32,9,128,128]{3,0,2,1:T(8,128)} fusion(f32[32,9,128,128]{3,0,2,1:T(8,128)} %bitcast_dynamic-update-slice_fusion.5, f32[16,128,128]{2,1,0:T(8,128)S(1)} %convolution_bitcast_fusion.4, s32[16]{0:T(128)S(1)} %reshape.502), kind=kOutput, calls=%fused_computation.22 | convolution fusion | flops 100663808 | bytes 3145792 | tf_op jit(solution)/shard_map/su,scd->ucd/dot_general | solution.py:88
  111.5 3.1 %bitcast_dynamic-update-slice_fusion.3 = f32[32,9,128,128]{3,0,2,1:T(8,128)} fusion(f32[32,9,128,128]{3,0,2,1:T(8,128)} %bitcast_dynamic-update-slice_fusion.4, f32[16,128,128]{2,1,0:T(8,128)S(1)} %convolution_bitcast_fusion.3, s32[16]{0:T(128)S(1)} %reshape.502), kind=kOutput, calls=%fused_computation.21 | convolution fusion | flops 100663808 | bytes 3145792 | tf_op jit(solution)/shard_map/su,scd->ucd/dot_general | solution.py:88
  115.1 2.9 %bitcast_dynamic-update-slice_fusion.2 = f32[32,9,128,128]{3,0,2,1:T(8,128)} fusion(f32[32,9,128,128]{3,0,2,1:T(8,128)} %bitcast_dynamic-update-slice_fusion.3, f32[16,128,128]{2,1,0:T(8,128)S(1)} %convolution_bitcast_fusion.2, s32[16]{0:T(128)S(1)} %reshape.502), kind=kOutput, calls=%fused_computation.20 | convolution fusion | flops 100663808 | bytes 3145792 | tf_op jit(solution)/shard_map/su,scd->ucd/dot_general | solution.py:88
  118.5 2.9 %bitcast_dynamic-update-slice_fusion.1 = f32[32,9,128,128]{3,0,2,1:T(8,128)} fusion(f32[32,9,128,128]{3,0,2,1:T(8,128)} %bitcast_dynamic-update-slice_fusion.2, f32[16,128,128]{2,1,0:T(8,128)S(1)} %convolution_bitcast_fusion.1, s32[16]{0:T(128)S(1)} %reshape.502), kind=kOutput, calls=%fused_computation.19 | convolution fusion | flops 100663808 | bytes 3145792 | tf_op jit(solution)/shard_map/su,scd->ucd/dot_general | solution.py:88
  122.0 2.9 %bitcast_dynamic-update-slice_fusion = f32[32,9,128,128]{3,0,2,1:T(8,128)} fusion(f32[32,9,128,128]{3,0,2,1:T(8,128)} %bitcast_dynamic-update-slice_fusion.1, f32[16,128,128]{2,1,0:T(8,128)S(1)} %convolution_bitcast_fusion, s32[16]{0:T(128)S(1)} %reshape.502), kind=kOutput, calls=%fused_computation.18 | convolution fusion | flops 100663808 | bytes 3145792 | tf_op jit(solution)/shard_map/su,scd->ucd/dot_general | solution.py:88
  125.2 8.1 %gather_fusion.1 = bf16[16,9,128,128]{3,2,1,0:T(8,128)(2,1)} fusion(bf16[32,9,128,128]{3,2,1,0:T(8,128)(2,1)} %all-gather.2.cloned.1.call-done, s32[1024]{0:T(1024)S(1)} %pad_clamp_fusion), kind=kCustom, calls=%fused_computation.1 | custom fusion | bytes 9437248 | tf_op jit(solution)/shard_map/jit(_take)/gather | solution.py:143
  133.3 4.0 %copy_select_fusion = bf16[16,9,128,128]{3,2,0,1:T(8,128)(2,1)S(1)} fusion(bf16[16,9,128,128]{3,2,1,0:T(8,128)(2,1)} %gather_fusion.1, pred[16]{0:T(512)(128)(4,1)S(1)} %compare_and_fusion), kind=kLoop, calls=%fused_computation.2 | loop fusion | flops 2359296 | bytes 9437200 | tf_op jit(solution)/shard_map/jit(_take)/select_n | solution.py:143
  139.6 3.2 %fusion.4 = f32[16,18,18,128]{3,2,1,0:T(8,128)} fusion(bf16[16,16,16,128]{3,2,1,0:T(8,128)(2,1)S(1)} %bitcast.229, bf16[16,9,128,128]{3,2,0,1:T(8,128)(2,1)S(1)} %copy_select_fusion), kind=kOutput, calls=%fused_computation.33 | convolution fusion | flops 169869312 | bytes 4227072 | tf_op jit(solution)/shard_map/sxyd,scd->sxyc/dot_general | solution.py:84
  142.8 3.2 %fusion.5 = f32[16,18,18,128]{3,2,1,0:T(8,128)} fusion(bf16[16,16,16,128]{3,2,1,0:T(8,128)(2,1)S(1)} %bitcast.230, bf16[16,9,128,128]{3,2,0,1:T(8,128)(2,1)S(1)} %copy_select_fusion), kind=kOutput, calls=%fused_computation.34 | convolution fusion | flops 169869312 | bytes 4227072 | tf_op jit(solution)/shard_map/sxyd,scd->sxyc/dot_general | solution.py:84
  146.0 3.1 %fusion.6 = f32[16,18,18,128]{3,2,1,0:T(8,128)} fusion(bf16[16,16,16,128]{3,2,1,0:T(8,128)(2,1)S(1)} %bitcast.231, bf16[16,9,128,128]{3,2,0,1:T(8,128)(2,1)S(1)} %copy_select_fusion), kind=kOutput, calls=%fused_computation.35 | convolution fusion | flops 169869312 | bytes 4227072 | tf_op jit(solution)/shard_map/sxyd,scd->sxyc/dot_general | solution.py:84
  149.1 2.9 %fusion.7 = f32[16,18,18,128]{3,2,1,0:T(8,128)} fusion(bf16[16,16,16,128]{3,2,1,0:T(8,128)(2,1)S(1)} %bitcast.232, bf16[16,9,128,128]{3,2,0,1:T(8,128)(2,1)S(1)} %copy_select_fusion), kind=kOutput, calls=%fused_computation.36 | convolution fusion | flops 169869312 | bytes 4227072 | tf_op jit(solution)/shard_map/sxyd,scd->sxyc/dot_general | solution.py:84
  152.0 2.9 %fusion.8 = f32[16,18,18,128]{3,2,1,0:T(8,128)} fusion(bf16[16,16,16,128]{3,2,1,0:T(8,128)(2,1)S(1)} %bitcast.233, bf16[16,9,128,128]{3,2,0,1:T(8,128)(2,1)S(1)} %copy_select_fusion), kind=kOutput, calls=%fused_computation.37 | convolution fusion | flops 169869312 | bytes 4227072 | tf_op jit(solution)/shard_map/sxyd,scd->sxyc/dot_general | solution.py:84
  154.9 2.9 %fusion.9 = f32[16,18,18,128]{3,2,1,0:T(8,128)} fusion(bf16[16,16,16,128]{3,2,1,0:T(8,128)(2,1)S(1)} %bitcast.234, bf16[16,9,128,128]{3,2,0,1:T(8,128)(2,1)S(1)} %copy_select_fusion), kind=kOutput, calls=%fused_computation.38 | convolution fusion | flops 169869312 | bytes 4227072 | tf_op jit(solution)/shard_map/sxyd,scd->sxyc/dot_general | solution.py:84
  157.8 9.9 %add_convert_fusion = bf16[16,18,18,128]{3,2,1,0:T(8,128)(2,1)} fusion(f32[16,18,18,128]{3,2,1,0:T(8,128)} %fusion.9, f32[16,18,18,128]{3,2,1,0:T(8,128)} %fusion.8, f32[16,18,18,128]{3,2,1,0:T(8,128)} %fusion.7, f32[16,18,18,128]{3,2,1,0:T(8,128)} %fusion.6, f32[16,18,18,128]{3,2,1,0:T(8,128)} %fusion.5, f32[16,18,18,128]{3,2,1,0:T(8,128)} %fusion.4, ...), kind=kOutput, calls=%fused_computation.13 | convolution fusion | flops 175841280 | bytes 25903104 | tf_op jit(solution)/shard_map/sxyd,scd->sxyc/dot_general | solution.py:84
  167.7 3.9 %copy.37 = bf16[8,2,18,18,128]{4,1,3,2,0:T(2,128)(2,1)} copy(bf16[8,2,18,18,128]{4,3,2,1,0:T(8,128)(2,1)} %bitcast.258) | data formatting | bytes 2654208 | tf_op jit(solution)/shard_map/reshape | solution.py:156
  171.6 3.6 %all-to-all-start.4 = ((bf16[8,2,18,18,128]{4,1,3,2,0:T(2,128)(2,1)}), bf16[8,2,18,18,128]{4,1,3,2,0:T(2,128)(2,1)S(1)}, u32[]{:S(2)}, u32[]{:S(2)}) async-start(bf16[8,2,18,18,128]{4,1,3,2,0:T(2,128)(2,1)} %copy.37), calls=%async_computation.4 | async-start | bytes 2654208 | tf_op jit(solution)/shard_map/all_to_all | solution.py:157
  183.0 23.1 %all-to-all-done.4 = bf16[8,2,18,18,128]{4,1,3,2,0:T(2,128)(2,1)S(1)} async-done(((bf16[8,2,18,18,128]{4,1,3,2,0:T(2,128)(2,1)}), bf16[8,2,18,18,128]{4,1,3,2,0:T(2,128)(2,1)S(1)}, u32[]{:S(2)}, u32[]{:S(2)}) %all-to-all-start.4) | async-done | bytes 1327136 | tf_op jit(solution)/shard_map/all_to_all | solution.py:157
  206.1 3.8 %all-to-all-start.2 = ((bf16[8,2,16,16,128]{4,3,2,1,0:T(8,128)(2,1)}), bf16[8,2,16,16,128]{4,3,2,1,0:T(8,128)(2,1)S(1)}, u32[]{:S(2)}, u32[]{:S(2)}) async-start(bf16[8,2,16,16,128]{4,3,2,1,0:T(8,128)(2,1)} %bitcast.263), calls=%async_computation.2 | async-start | bytes 2097152 | tf_op jit(solution)/shard_map/all_to_all | solution.py:145
  218.2 17.5 %all-to-all-done.2 = bf16[8,2,16,16,128]{4,3,2,1,0:T(8,128)(2,1)S(1)} async-done(((bf16[8,2,16,16,128]{4,3,2,1,0:T(8,128)(2,1)}), bf16[8,2,16,16,128]{4,3,2,1,0:T(8,128)(2,1)S(1)}, u32[]{:S(2)}, u32[]{:S(2)}) %all-to-all-start.2) | async-done | bytes 1048608 | tf_op jit(solution)/shard_map/all_to_all | solution.py:145
  238.4 3.3 %collective-permute-start.7 = (bf16[36,1,128]{2,1,0:T(2,128)(2,1)S(1)}, bf16[36,1,128]{2,1,0:T(2,128)(2,1)S(1)}, u32[]{:S(2)}, u32[]{:S(2)}) collective-permute-start(bf16[36,1,128]{2,1,0:T(2,128)(2,1)S(1)} %get-tuple-element.119), channel_id=1, source_target_pairs={{1,0},{2,1},{3,2},{4,3},{5,4},{6,5},{7,6},{0,7},{9,8},{10,9},{11,1... | collective-permute-start | bytes 27656 | tf_op jit(solution)/shard_map/ppermute | solution.py:18
  247.0 16.6 %reduce-scatter.2.cloned.1.call-done = f32[8,9,128,128]{3,0,2,1:T(8,128)} async-done(((f32[32,9,128,128]{3,0,2,1:T(8,128)}), f32[8,9,128,128]{3,0,2,1:T(8,128)}) %reduce-scatter.2.cloned.1.call-update) | async-done | bytes 4718608 | tf_op jit(solution)/shard_map/reduce_scatter | solution.py:158
  263.5 5.4 %copy.52 = f32[8,9,128,128]{3,2,1,0:T(8,128)} copy(f32[8,9,128,128]{3,0,2,1:T(8,128)} %reduce-scatter.2.cloned.1.call-done) | data formatting | bytes 9437184
  (133 shorter events, 51.9 us)
Async XLA Ops:
  7.2 0.9 copy-start
  7.2 0.8 copy-start.7
  7.2 10.0 %copy-start.6 = (bf16[32,128,128]{2,1,0:T(8,128)(2,1)S(1)}, bf16[32,128,128]{2,1,0:T(8,128)(2,1)}, u32[]{:S(2)}) copy-start(bf16[32,128,128]{2,1,0:T(8,128)(2,1)} %param.22) | copy-start | bytes 3145732
  7.2 118.0 %all-gather.2.cloned.1.call-start = ((), (), s32[]{:S(2)}) async-start(), calls=%async_computation.6 | async-start | bytes 11796480 | tf_op jit(solution)/shard_map/all_gather | solution.py:135
  9.9 13.7 %all-to-all-start.1 = ((bf16[8,1,2]{2,1,0:T(2,128)(2,1)}), bf16[8,1,2]{2,1,0:T(2,128)(2,1)S(1)}, u32[]{:S(2)}, u32[]{:S(2)}) async-start(bf16[8,1,2]{2,1,0:T(2,128)(2,1)} %all_to_all.24), calls=%async_computation.1 | async-start | bytes 8192 | tf_op jit(solution)/shard_map/all_to_all | solution.py:139
  17.6 9.6 %copy-start.5 = (bf16[32,128,128]{2,1,0:T(8,128)(2,1)S(1)}, bf16[32,128,128]{2,1,0:T(8,128)(2,1)}, u32[]{:S(2)}) copy-start(bf16[32,128,128]{2,1,0:T(8,128)(2,1)} %param.21) | copy-start | bytes 3145732
  23.5 29.2 %all-to-all-start.3 = ((bf16[8,2,16,16,128]{4,1,3,2,0:T(2,128)(2,1)}), bf16[8,2,16,16,128]{4,1,3,2,0:T(2,128)(2,1)S(1)}, u32[]{:S(2)}, u32[]{:S(2)}) async-start(bf16[8,2,16,16,128]{4,1,3,2,0:T(2,128)(2,1)} %copy.35), calls=%async_computation.3 | async-start | bytes 2097152 | tf_op jit(solution)/shard_map/all_to_all | solution.py:152
  27.2 4.1 %collective-permute-start = (bf16[1,128,128]{2,1,0:T(8,128)(2,1)S(1)}, bf16[1,128,128]{2,1,0:T(8,128)(2,1)S(1)}, u32[]{:S(2)}, u32[]{:S(2)}) collective-permute-start(bf16[1,128,128]{2,1,0:T(8,128)(2,1)S(1)} %get-tuple-element.125), channel_id=1, source_target_pairs={{0,8},{8,16},{16,24},{24,0},{1,9},{9,17},{17,25},{25,1},{2,10},{10... | collective-permute-start | bytes 98312 | tf_op jit(solution)/shard_map/ppermute | solution.py:17
  27.2 4.1 %collective-permute-start.1 = (bf16[1,128,128]{2,1,0:T(8,128)(2,1)S(1)}, bf16[1,128,128]{2,1,0:T(8,128)(2,1)S(1)}, u32[]{:S(2)}, u32[]{:S(2)}) collective-permute-start(bf16[1,128,128]{2,1,0:T(8,128)(2,1)S(1)} %get-tuple-element.124), channel_id=1, source_target_pairs={{8,0},{16,8},{24,16},{0,24},{9,1},{17,9},{25,17},{1,25},{10,2},{18... | collective-permute-start | bytes 98312 | tf_op jit(solution)/shard_map/ppermute | solution.py:18
  31.4 16.9 %collective-permute-start.2 = (bf16[34,1,128]{2,1,0:T(2,128)(2,1)S(1)}, bf16[34,1,128]{2,1,0:T(2,128)(2,1)S(1)}, u32[]{:S(2)}, u32[]{:S(2)}) collective-permute-start(bf16[34,1,128]{2,1,0:T(2,128)(2,1)S(1)} %get-tuple-element.122), channel_id=1, source_target_pairs={{0,1},{1,2},{2,3},{3,4},{4,5},{5,6},{6,7},{7,0},{8,9},{9,10},{10,1... | collective-permute-start | bytes 26120 | tf_op jit(solution)/shard_map/ppermute | solution.py:17
  33.4 15.0 %collective-permute-start.3 = (bf16[34,1,128]{2,1,0:T(2,128)(2,1)S(1)}, bf16[34,1,128]{2,1,0:T(2,128)(2,1)S(1)}, u32[]{:S(2)}, u32[]{:S(2)}) collective-permute-start(bf16[34,1,128]{2,1,0:T(2,128)(2,1)S(1)} %get-tuple-element.123), channel_id=1, source_target_pairs={{1,0},{2,1},{3,2},{4,3},{5,4},{6,5},{7,6},{0,7},{9,8},{10,9},{11,1... | collective-permute-start | bytes 26120 | tf_op jit(solution)/shard_map/ppermute | solution.py:18
  52.8 39.3 %all-to-all-start = ((bf16[8,2,18,18,128]{4,1,3,2,0:T(2,128)(2,1)}), bf16[8,2,18,18,128]{4,1,3,2,0:T(2,128)(2,1)}, u32[]{:S(2)}, u32[]{:S(2)}) async-start(bf16[8,2,18,18,128]{4,1,3,2,0:T(2,128)(2,1)} %copy.28), calls=%async_computation | async-start | bytes 2654208 | tf_op jit(solution)/shard_map/all_to_all | solution.py:138
  59.4 204.1 %reduce-scatter.2.cloned.1.call-start = ((), (), s32[]{:S(2)}) async-start(), calls=%async_computation.7 | async-start | bytes 23592960 | tf_op jit(solution)/shard_map/reduce_scatter | solution.py:158
  137.3 20.5 %copy-start.2 = (bf16[16,9,128,128]{3,2,0,1:T(8,128)(2,1)}, bf16[16,9,128,128]{3,2,0,1:T(8,128)(2,1)S(1)}, u32[]{:S(2)}) copy-start(bf16[16,9,128,128]{3,2,0,1:T(8,128)(2,1)S(1)} %copy_select_fusion) | copy-start | bytes 14155780
  171.6 34.5 %all-to-all-start.4 = ((bf16[8,2,18,18,128]{4,1,3,2,0:T(2,128)(2,1)}), bf16[8,2,18,18,128]{4,1,3,2,0:T(2,128)(2,1)S(1)}, u32[]{:S(2)}, u32[]{:S(2)}) async-start(bf16[8,2,18,18,128]{4,1,3,2,0:T(2,128)(2,1)} %copy.37), calls=%async_computation.4 | async-start | bytes 2654208 | tf_op jit(solution)/shard_map/all_to_all | solution.py:157
  175.2 3.1 %copy-start.3 = (bf16[16,9,128,128]{3,2,0,1:T(8,128)(2,1)S(1)}, bf16[16,9,128,128]{3,2,0,1:T(8,128)(2,1)}, u32[]{:S(2)}) copy-start(bf16[16,9,128,128]{3,2,0,1:T(8,128)(2,1)} %copy-done.2) | copy-start | bytes 14155780
  206.1 29.6 %all-to-all-start.2 = ((bf16[8,2,16,16,128]{4,3,2,1,0:T(8,128)(2,1)}), bf16[8,2,16,16,128]{4,3,2,1,0:T(8,128)(2,1)S(1)}, u32[]{:S(2)}, u32[]{:S(2)}) async-start(bf16[8,2,16,16,128]{4,3,2,1,0:T(8,128)(2,1)} %bitcast.263), calls=%async_computation.2 | async-start | bytes 2097152 | tf_op jit(solution)/shard_map/all_to_all | solution.py:145
  216.4 20.4 %collective-permute-start.4 = (bf16[1,130,128]{2,1,0:T(8,128)(2,1)S(1)}, bf16[1,130,128]{2,1,0:T(8,128)(2,1)S(1)}, u32[]{:S(2)}, u32[]{:S(2)}) collective-permute-start(bf16[1,130,128]{2,1,0:T(8,128)(2,1)S(1)} %get-tuple-element.112), channel_id=1, source_target_pairs={{0,8},{8,16},{16,24},{24,0},{1,9},{9,17},{17,25},{25,1},{2,10},{10... | collective-permute-start | bytes 99848 | tf_op jit(solution)/shard_map/ppermute | solution.py:17
  216.4 20.4 %collective-permute-start.5 = (bf16[1,130,128]{2,1,0:T(8,128)(2,1)S(1)}, bf16[1,130,128]{2,1,0:T(8,128)(2,1)S(1)}, u32[]{:S(2)}, u32[]{:S(2)}) collective-permute-start(bf16[1,130,128]{2,1,0:T(8,128)(2,1)S(1)} %get-tuple-element.113), channel_id=1, source_target_pairs={{8,0},{16,8},{24,16},{0,24},{9,1},{17,9},{25,17},{1,25},{10,2},{18... | collective-permute-start | bytes 99848 | tf_op jit(solution)/shard_map/ppermute | solution.py:18
  236.9 7.4 %collective-permute-start.6 = (bf16[36,1,128]{2,1,0:T(2,128)(2,1)S(1)}, bf16[36,1,128]{2,1,0:T(2,128)(2,1)S(1)}, u32[]{:S(2)}, u32[]{:S(2)}) collective-permute-start(bf16[36,1,128]{2,1,0:T(2,128)(2,1)S(1)} %get-tuple-element.118), channel_id=1, source_target_pairs={{0,1},{1,2},{2,3},{3,4},{4,5},{5,6},{6,7},{7,0},{8,9},{9,10},{10,1... | collective-permute-start | bytes 27656 | tf_op jit(solution)/shard_map/ppermute | solution.py:17
  238.4 5.9 %collective-permute-start.7 = (bf16[36,1,128]{2,1,0:T(2,128)(2,1)S(1)}, bf16[36,1,128]{2,1,0:T(2,128)(2,1)S(1)}, u32[]{:S(2)}, u32[]{:S(2)}) collective-permute-start(bf16[36,1,128]{2,1,0:T(2,128)(2,1)S(1)} %get-tuple-element.119), channel_id=1, source_target_pairs={{1,0},{2,1},{3,2},{4,3},{5,4},{6,5},{7,6},{0,7},{9,8},{10,9},{11,1... | collective-permute-start | bytes 27656 | tf_op jit(solution)/shard_map/ppermute | solution.py:18
  241.7 2.4 copy-start.4
  263.5 5.5 %copy-start.1 = (s32[256]{0:T(256)S(1)}, s32[256]{0:T(256)}, u32[]{:S(2)}) copy-start(s32[256]{0:T(256)} %param.25) | copy-start | bytes 3076
Sparse Core Ops, SparseCore 0:
  9.6 67.6 all-gather.1
  125.1 138.4 reduce-scatter.1
where the time goes:
time: 281 us; the launch traced here: 276 us
  waiting for transfers between devices  108 us (38%)
  matrix products  71.4 us (25%)
  starting transfers between devices  38.5 us (14%)
  local copies, waits for them, and re-layouts  32.3 us (11%)
  between operations  15.1 us (5%)
  other arithmetic  10.7 us (4%)
    all_to_all x1, waiting for transfers between devices, local(): lax.all_to_all(sent_patches, 'lon', split_axis=0, concat_axis=0, tiled=True)  31.8 us
    dot_general x9, matrix products, expert_backward(): jnp.einsum('sxyd,scd->sxyc', shifted, kernel_in[:, tap_index], preferred_...  30.3 us
    dot_general x9, matrix products, expert_backward(): jnp.einsum('su,scd->ucd', selector, per_slot, precision=lax.Precision.HIG...  26.3 us
    all_to_all x1, waiting for transfers between devices, local(): lax.all_to_all(spread_send, 'lon', split_axis=0, concat_axis=0, tiled=True)  23.1 us
    all_to_all x1, waiting for transfers between devices, local(): lax.all_to_all(result.reshape(lon_count, CAP, BS, BS, chans), 'lon', spli...  17.5 us
    reduce_scatter x1, waiting for transfers between devices, local(): grad_bank = lax.psum_scatter(grads, 'lat', scatter_dimension=0, tiled=True)  16.6 us
    ppermute x4, waiting for transfers between devices, padded_2(): before = lax.ppermute(last, axis, up)  14.4 us
    ppermute x4, starting transfers between devices, padded_2(): after = lax.ppermute(initial, axis, down)  9.58 us
  transfers between devices with their start and end apart: 15, of which 7 were waited for; matrix products, arithmetic and copies ran while one was open for 39% of the time, Pallas kernels for 0%

commit v1 on v0

v1 whole, which is shorter than its diff:
```python
import functools

import jax
import jax.numpy as jnp
from jax import lax
from jax.experimental import pallas as pl
from jax.experimental.pallas import tpu as pltpu
from jax.sharding import PartitionSpec as P

BS = 16
CAP = 2
EDGE = BS + 2
CELLS = BS * BS
MAIN = EDGE * BS
TAIL = 48
ROWS = CELLS + MAIN + TAIL
SIDE = CELLS + MAIN
NUMBER = 2 * EDGE
GAP = 8
SPAN = 2 * BS
F32 = jnp.float32
BF16 = jnp.bfloat16


def params(mib):
    return pltpu.CompilerParams(vmem_limit_bytes=mib * 1024 * 1024)


def whole(memory=pltpu.VMEM):
    return pl.BlockSpec(memory_space=memory)


def plan_slots(experts, owner, blocks, numbers, counts, per, columns):
    lat_blocks, lon_blocks = experts.shape

    def clear_slot(s, carry):
        blocks[s] = -1
        numbers[s] = 0
        return carry

    def clear_count(s, carry):
        counts[s] = 0
        return carry

    lax.fori_loop(0, columns * CAP, clear_slot, 0)
    lax.fori_loop(0, columns, clear_count, 0)

    def place(b, carry):
        stored = owner[experts[lax.div(b, lon_blocks), lax.rem(b, lon_blocks)]]
        group = lax.div(stored, per)
        column = lax.rem(group, columns)
        rank = counts[column]
        counts[column] = rank + 1
        slot = column * CAP + rank
        blocks[slot] = b
        numbers[slot] = lax.div(group, columns) * per + lax.rem(stored, per)
        return carry

    lax.fori_loop(0, lat_blocks * lon_blocks, place, 0)


def dispatch_kernel(
    per, columns, experts, owner, fields, cot, north, south, west, east, out,
    rows, wide, tail, blocks, numbers, counts,
):
    height, width = fields.shape[:2]
    lon_blocks = width // BS
    stride = width + 2 * GAP
    step = pl.program_id(0)

    @pl.when(step == 0)
    def _():
        plan_slots(experts, owner, blocks, numbers, counts, per, columns)
        rows[0] = north[0]
        rows[height + 1] = south[0]

        def fill(r, carry):
            rows[r + 1] = fields[r]
            return carry

        lax.fori_loop(0, height, fill, 0)

        def widen(r, carry):
            start = pl.multiple_of(r * stride + GAP, 8)
            wide[pl.ds(start, width), :] = rows[r].astype(F32)
            return carry

        lax.fori_loop(0, height + 2, widen, 0)
        wide[pl.ds(GAP - 1, height + 2, stride=stride), :] = west[...].astype(F32)
        wide[pl.ds(GAP + width, height + 2, stride=stride), :] = east[...].astype(F32)

    for r in range(CAP):
        slot = step * CAP + r
        held = blocks[slot]
        block = jnp.maximum(held, 0)
        top = lax.div(block, lon_blocks) * BS
        left = pl.multiple_of(lax.rem(block, lon_blocks) * BS, BS)

        @pl.when(held >= 0)
        def _():
            part = cot[pl.ds(top, BS), pl.ds(left, BS), :]
            out[0, r, 0:CELLS, :] = part.reshape(CELLS, part.shape[2])

        @pl.when(held < 0)
        def _():
            out[0, r, 0:CELLS, :] = jnp.zeros((CELLS, out.shape[3]), BF16)

        window = rows[pl.ds(top, EDGE), pl.ds(left, BS), :]
        out[0, r, CELLS:SIDE, :] = window.reshape(MAIN, window.shape[2])
        start = top * stride + left
        tail[0:EDGE, :] = wide[pl.ds(start + GAP - 1, EDGE, stride=stride), :]
        tail[EDGE : 2 * EDGE, :] = wide[pl.ds(start + GAP + BS, EDGE, stride=stride), :]
        tail[NUMBER:TAIL, :] = jnp.full(
            (TAIL - NUMBER, tail.shape[1]), numbers[slot].astype(F32), F32
        )
        out[0, r, SIDE:ROWS, :] = tail[...].astype(BF16)


def dispatch(experts, owner, fields, cot, north, south, west, east, per, columns):
    height, width, chans = fields.shape
    return pl.pallas_call(
        functools.partial(dispatch_kernel, per, columns),
        grid=(columns,),
        out_shape=jax.ShapeDtypeStruct((columns, CAP, ROWS, chans), BF16),
        in_specs=[whole(pltpu.SMEM)] * 2 + [whole()] * 6,
        out_specs=pl.BlockSpec((1, CAP, ROWS, chans), lambda q: (q, 0, 0, 0)),
        scratch_shapes=[
            pltpu.VMEM((height + 2, width, chans), BF16),
            pltpu.VMEM(((height + 2) * (width + 2 * GAP), chans), F32),
            pltpu.VMEM((TAIL, chans), F32),
            pltpu.SMEM((columns * CAP,), jnp.int32),
            pltpu.SMEM((columns * CAP,), jnp.int32),
            pltpu.SMEM((columns,), jnp.int32),
        ],
        compiler_params=params(32),
        cost_estimate=pl.CostEstimate(flops=0, bytes_accessed=6_000_000, transcendentals=0),
        name="dispatch",
    )(experts, owner, fields, cot, north, south, west, east)


def window_rows(slot, tail):
    chans = tail.shape[1]
    tail[...] = slot[SIDE:ROWS, :].astype(F32)
    parts = []
    for a in range(3):
        start = CELLS + a * BS
        sides = jnp.concatenate(
            [tail[a : a + BS, :], tail[EDGE + a : EDGE + a + BS, :]], axis=0
        ).astype(BF16)
        parts.append(jnp.concatenate([slot[start : start + CELLS, :], sides], axis=0))
    return jnp.concatenate(parts, axis=1)


def taps_kernel(per, *refs):
    place, slot = refs[:2]
    banks = refs[2:-6]
    out, held, tail, early, late, sems = refs[-6:]
    chans = out.shape[3]
    step = pl.program_id(0)
    total = pl.num_programs(0)

    def fetch(s, buffer):
        index = place[s]
        piece = lax.div(index, per)
        row = lax.rem(index, per)
        for p, bank in enumerate(banks):

            @pl.when(piece == p)
            def _():
                pltpu.make_async_copy(bank.at[row], held.at[buffer], sems.at[buffer]).start()

    now = lax.rem(step, 2)

    @pl.when(step == 0)
    def _():
        early[...] = jnp.zeros(early.shape, F32)
        late[...] = jnp.zeros(late.shape, F32)
        fetch(step, now)

    @pl.when(step + 1 < total)
    def _():
        fetch(step + 1, 1 - now)

    pltpu.make_async_copy(banks[0].at[0], held.at[now], sems.at[now]).wait()
    data = slot.at[0, 0]
    kernel = [held[now, t] for t in range(9)]

    cot = data[0:CELLS, :]
    shifted = []
    for a in range(3):
        pieces = []
        if a > 0:
            pieces.append(jnp.zeros((a * BS, chans), BF16))
        pieces.append(cot)
        if a < 2:
            pieces.append(jnp.zeros(((2 - a) * BS, chans), BF16))
        shifted.append(jnp.concatenate(pieces, axis=0))
    spread_rows = jnp.concatenate(shifted, axis=1)
    spread_mat = jnp.concatenate(
        [jnp.concatenate([kernel[3 * a + b] for a in range(3)], axis=1) for b in range(3)], axis=0
    )
    spread = lax.dot_general(
        spread_rows, spread_mat, (((1,), (1,)), ((), ())), preferred_element_type=F32
    )
    for u in range(EDGE):
        early[SPAN * u + 8 : SPAN * u + 8 + BS, :] = spread[BS * u : BS * u + BS, 0:chans]
        late[SPAN * u + 8 : SPAN * u + 8 + BS, :] = spread[BS * u : BS * u + BS, 2 * chans :]
    tail[0:EDGE, :] = early[pl.ds(8, EDGE, stride=SPAN), :]
    tail[EDGE : 2 * EDGE, :] = late[pl.ds(8 + BS - 1, EDGE, stride=SPAN), :]
    tail[NUMBER:TAIL, :] = jnp.zeros((TAIL - NUMBER, chans), F32)
    out[0, 0, SIDE:ROWS, :] = tail[...].astype(BF16)
    zero = jnp.zeros((EDGE, chans), F32)
    early[pl.ds(8 + BS, EDGE, stride=SPAN), :] = zero
    late[pl.ds(7, EDGE, stride=SPAN), :] = zero
    for u in range(EDGE):
        line = (
            spread[BS * u : BS * u + BS, chans : 2 * chans]
            + early[SPAN * u + 9 : SPAN * u + 9 + BS, :]
            + late[SPAN * u + 7 : SPAN * u + 7 + BS, :]
        )
        out[0, 0, CELLS + BS * u : CELLS + BS * u + BS, :] = line.astype(BF16)

    rows = window_rows(data, tail)
    forward_mat = jnp.concatenate(
        [jnp.concatenate([kernel[3 * a + b] for b in range(3)], axis=1) for a in range(3)], axis=0
    )
    result = jnp.dot(rows, forward_mat, preferred_element_type=F32)
    for x in range(BS):
        early[SPAN * x + 8 : SPAN * x + 8 + BS, :] = result[BS * x : BS * x + BS, 0:chans]
        late[SPAN * x + 8 : SPAN * x + 8 + BS, :] = result[BS * x : BS * x + BS, 2 * chans :]
    early[pl.ds(7, BS, stride=SPAN), :] = result[CELLS : CELLS + BS, 0:chans]
    late[pl.ds(8 + BS, BS, stride=SPAN), :] = result[CELLS + BS :, 2 * chans :]
    for x in range(BS):
        line = (
            result[BS * x : BS * x + BS, chans : 2 * chans]
            + early[SPAN * x + 7 : SPAN * x + 7 + BS, :]
            + late[SPAN * x + 9 : SPAN * x + 9 + BS, :]
        )
        out[0, 0, BS * x : BS * x + BS, :] = line.astype(BF16)


def taps(place, slots, banks):
    columns, cap, rows, chans = slots.shape
    per = banks[0].shape[0]
    spec = pl.BlockSpec((1, 1, rows, chans), lambda s: (s // cap, s % cap, 0, 0))
    return pl.pallas_call(
        functools.partial(taps_kernel, per),
        grid=(columns * cap,),
        out_shape=jax.ShapeDtypeStruct(slots.shape, BF16),
        in_specs=[whole(pltpu.SMEM), spec] + [whole(pl.ANY)] * len(banks),
        out_specs=spec,
        scratch_shapes=[
            pltpu.VMEM((2,) + banks[0].shape[1:], BF16),
            pltpu.VMEM((TAIL, chans), F32),
            pltpu.VMEM((EDGE * SPAN, chans), F32),
            pltpu.VMEM((EDGE * SPAN, chans), F32),
            pltpu.SemaphoreType.DMA((2,)),
        ],
        compiler_params=params(32),
        cost_estimate=pl.CostEstimate(
            flops=2_800_000_000, bytes_accessed=10_000_000, transcendentals=0
        ),
        name="taps",
    )(place, slots, *banks)


def grads_kernel(first, terms, place, slots, *refs):
    added = refs[:terms]
    out, total, tail, cells = refs[terms:]
    columns, cap, _, chans = slots.shape
    wanted = first + pl.program_id(0)
    if terms:
        start = added[0][0].astype(F32)
        for term in added[1:]:
            start = start + term[0].astype(F32)
        total[...] = start
    else:
        total[...] = jnp.zeros(total.shape, F32)

    def visit(s, carry):
        @pl.when(place[s] == wanted)
        def _():
            data = slots.at[lax.div(s, cap), lax.rem(s, cap)]
            cot = data[0:CELLS, :]
            cells[8 : 8 + CELLS, :] = cot.astype(F32)
            column = lax.rem(lax.broadcasted_iota(jnp.int32, (CELLS, chans), 0), BS)
            after = jnp.where(column == BS - 1, 0.0, cells[9 : 9 + CELLS, :]).astype(BF16)
            before = jnp.where(column == 0, 0.0, cells[7 : 7 + CELLS, :]).astype(BF16)
            initial = cells[pl.ds(8, BS, stride=BS), :].astype(BF16)
            last = cells[pl.ds(8 + BS - 1, BS, stride=BS), :].astype(BF16)
            zero = jnp.zeros((BS, chans), BF16)
            right = jnp.concatenate(
                [
                    jnp.concatenate([after, initial, zero], axis=0),
                    jnp.concatenate([cot, zero, zero], axis=0),
                    jnp.concatenate([before, zero, last], axis=0),
                ],
                axis=1,
            )
            rows = window_rows(data, tail)
            term = lax.dot_general(
                rows, right, (((0,), (0,)), ((), ())), preferred_element_type=F32
            )
            for a in range(3):
                for b in range(3):
                    total[3 * a + b] += term[
                        a * chans : (a + 1) * chans, b * chans : (b + 1) * chans
                    ]

        return carry

    lax.fori_loop(0, columns * cap, visit, 0)
    out[0] = total[...].astype(out.dtype)


def grads(place, slots, piece, bank_shape, added, dtype):
    per, taps_n, chans, outs = bank_shape
    spec = pl.BlockSpec((1, taps_n, chans, outs), lambda e: (e, 0, 0, 0))
    return pl.pallas_call(
        functools.partial(grads_kernel, piece * per, len(added)),
        grid=(per,),
        out_shape=jax.ShapeDtypeStruct(bank_shape, dtype),
        in_specs=[whole(pltpu.SMEM), whole()] + [spec] * len(added),
        out_specs=spec,
        scratch_shapes=[
            pltpu.VMEM((taps_n, chans, outs), F32),
            pltpu.VMEM((TAIL, chans), F32),
            pltpu.VMEM((CELLS + 16, chans), F32),
        ],
        compiler_params=params(32),
        cost_estimate=pl.CostEstimate(
            flops=500_000_000, bytes_accessed=6_000_000, transcendentals=0
        ),
        name="grads",
    )(place, slots, *added)


def collect_kernel(
    per, columns, experts, owner, slots, outputs, canvas, north, south, west, east,
    tail, blocks, numbers, counts,
):
    height, width, chans = outputs.shape
    lon_blocks = width // BS
    stride = width + 2 * GAP
    plan_slots(experts, owner, blocks, numbers, counts, per, columns)

    def clear(r, carry):
        start = pl.multiple_of(r * stride, 8)
        canvas[pl.ds(start, stride), :] = jnp.zeros((stride, chans), F32)
        return carry

    lax.fori_loop(0, height + 2, clear, 0)

    def visit(s, carry):
        held = blocks[s]

        @pl.when(held >= 0)
        def _():
            data = slots.at[lax.div(s, CAP), lax.rem(s, CAP)]
            top = lax.div(held, lon_blocks) * BS
            left = pl.multiple_of(lax.rem(held, lon_blocks) * BS, BS)
            outputs[pl.ds(top, BS), pl.ds(left, BS), :] = data[0:CELLS, :].reshape(BS, BS, chans)
            for u in range(EDGE):
                place = pl.ds(pl.multiple_of((top + u) * stride + GAP + left, 8), BS)
                line = data[CELLS + BS * u : CELLS + BS * u + BS, :].astype(F32)
                canvas[place, :] = canvas[place, :] + line
            tail[...] = data[SIDE:ROWS, :].astype(F32)
            start = top * stride + left
            place = pl.ds(start + GAP - 1, EDGE, stride=stride)
            canvas[place, :] = canvas[place, :] + tail[0:EDGE, :]
            place = pl.ds(start + GAP + BS, EDGE, stride=stride)
            canvas[place, :] = canvas[place, :] + tail[EDGE : 2 * EDGE, :]

        return carry

    lax.fori_loop(0, columns * CAP, visit, 0)
    north[...] = canvas[0:stride, :].astype(BF16)
    south[...] = canvas[(height + 1) * stride : (height + 2) * stride, :].astype(BF16)
    west[...] = canvas[pl.ds(stride + GAP - 1, height, stride=stride), :]
    east[...] = canvas[pl.ds(stride + GAP + width, height, stride=stride), :]


def collect(experts, owner, slots, shape, per):
    height, width, chans = shape
    columns = slots.shape[0]
    stride = width + 2 * GAP
    return pl.pallas_call(
        functools.partial(collect_kernel, per, columns),
        out_shape=(
            jax.ShapeDtypeStruct(shape, BF16),
            jax.ShapeDtypeStruct(((height + 2) * stride, chans), F32),
            jax.ShapeDtypeStruct((stride, chans), BF16),
            jax.ShapeDtypeStruct((stride, chans), BF16),
            jax.ShapeDtypeStruct((height, chans), F32),
            jax.ShapeDtypeStruct((height, chans), F32),
        ),
        in_specs=[whole(pltpu.SMEM)] * 2 + [whole()],
        out_specs=(whole(),) * 6,
        scratch_shapes=[
            pltpu.VMEM((TAIL, chans), F32),
            pltpu.SMEM((columns * CAP,), jnp.int32),
            pltpu.SMEM((columns * CAP,), jnp.int32),
            pltpu.SMEM((columns,), jnp.int32),
        ],
        compiler_params=params(32),
        cost_estimate=pl.CostEstimate(flops=0, bytes_accessed=8_000_000, transcendentals=0),
        name="collect",
    )(experts, owner, slots)


def finish_kernel(canvas, north, south, west, east, out):
    height, width, chans = out.shape
    stride = width + 2 * GAP
    column = lax.broadcasted_iota(jnp.int32, (BS, chans), 0)
    for r in range(height):
        start = (r + 1) * stride + GAP
        line = canvas[start : start + width, :]
        if r == 0:
            line = line + north[GAP : GAP + width, :].astype(F32)
        if r == height - 1:
            line = line + south[GAP : GAP + width, :].astype(F32)
        first = line[:BS] + jnp.where(column == 0, west[r : r + 1, :].astype(F32), 0.0)
        last = line[width - BS :] + jnp.where(
            column == BS - 1, east[r : r + 1, :].astype(F32), 0.0
        )
        out[r] = jnp.concatenate([first, line[BS : width - BS], last], axis=0).astype(BF16)


def finish(canvas, north, south, west, east, shape):
    return pl.pallas_call(
        finish_kernel,
        out_shape=jax.ShapeDtypeStruct(shape, BF16),
        in_specs=[whole()] * 5,
        out_specs=whole(),
        compiler_params=params(32),
        cost_estimate=pl.CostEstimate(flops=0, bytes_accessed=4_000_000, transcendentals=0),
        name="finish",
    )(canvas, north, south, west, east)


def across(array, axis, shift, wrap):
    count = lax.axis_size(axis)
    pairs = [(i, i + shift) for i in range(count)]
    if wrap:
        pairs = [(i, j % count) for i, j in pairs]
    else:
        pairs = [(i, j) for i, j in pairs if 0 <= j < count]
    return lax.ppermute(array, axis, pairs)


def to_other_core(array):
    return lax.ppermute(array, "lat", [(i, i ^ 1) for i in range(lax.axis_size("lat"))])


def to_chip(array, shift):
    count = lax.axis_size("lat")
    return lax.ppermute(array, "lat", [(i, (i + 2 * shift) % count) for i in range(count)])


def swap(slots):
    return lax.all_to_all(slots, "lon", split_axis=0, concat_axis=0, tiled=True)


def local(fields, cotangent, kernel_bank, block_expert, owner):
    columns = lax.axis_size("lon")
    lat_count = lax.axis_size("lat")
    chips = lat_count // 2
    lat_index = lax.axis_index("lat")
    height, width, chans = fields.shape
    per = kernel_bank.shape[0]

    north = across(fields[height - 1 :], "lat", 1, False)
    south = across(fields[:1], "lat", -1, False)
    first = jnp.concatenate([north[:, 0], fields[:, 0], south[:, 0]], axis=0)
    last = jnp.concatenate([north[:, -1], fields[:, -1], south[:, -1]], axis=0)
    west = across(last, "lon", 1, True)
    east = across(first, "lon", -1, True)

    banks = [kernel_bank, to_other_core(kernel_bank)]
    for k in range(1, chips):
        far = to_chip(kernel_bank, -k)
        banks += [far, to_other_core(far)]

    sent = dispatch(
        block_expert, owner, fields, cotangent, north, south, west, east, per, columns
    )
    slots = swap(sent)
    numbers = slots[:, :, SIDE + NUMBER, 0].reshape(-1).astype(jnp.int32)
    owner_lat = numbers // per
    chip_step = (owner_lat // 2 - lat_index // 2 + chips) % chips
    core_step = (owner_lat % 2 - lat_index % 2 + 2) % 2
    place = (2 * chip_step + core_step) * per + numbers % per

    returned = swap(taps(place, slots, banks))

    shape = kernel_bank.shape
    arrived = []
    for k in range(1, chips):
        part = to_other_core(grads(place, slots, 2 * k + 1, shape, [], BF16))
        arrived.append(to_chip(grads(place, slots, 2 * k, shape, [part], BF16), k))
    arrived.append(to_other_core(grads(place, slots, 1, shape, [], BF16)))
    grad_bank = grads(place, slots, 0, shape, arrived, F32)

    outputs, canvas, top, bottom, left, right = collect(
        block_expert, owner, returned, fields.shape, per
    )
    above = across(bottom, "lat", 1, False)
    below = across(top, "lat", -1, False)

    def with_corners(line, column):
        line = line.at[0].add(above[column].astype(F32))
        return line.at[height - 1].add(below[column].astype(F32)).astype(BF16)

    from_west = across(with_corners(right, GAP + width), "lon", 1, True)
    from_east = across(with_corners(left, GAP - 1), "lon", -1, True)
    grad_fields = finish(canvas, above, below, from_west, from_east, fields.shape)
    return (outputs, grad_fields, grad_bank)


def solution(mesh):
    return jax.shard_map(
        local,
        mesh=mesh,
        in_specs=(
            P("lat", "lon", None),
            P("lat", "lon", None),
            P(("lat", "lon"), None, None, None),
            P("lat", "lon"),
            P(),
        ),
        out_specs=(
            P("lat", "lon", None),
            P("lat", "lon", None),
            P(("lat", "lon"), None, None, None),
        ),
        check_vma=False,
    )
```

time: 281 us -> 197 us (0.70); the launches traced: 276 us -> 196 us
  matrix products: 71.4 us -> 0 us
  Pallas kernels: 0 us -> 50.7 us
  local copies, waits for them, and re-layouts: 32.3 us -> 9.99 us
  between operations: 15.1 us -> 0.85 us
  other arithmetic: 10.7 us -> 0.45 us
  waiting for transfers between devices: 108 us -> 101 us
  starting transfers between devices: 38.5 us -> 33.5 us
    dot_general x41 -> x0, matrix products: 71.4 us -> none  [the longest x9 30.3 us: expert_backward(): jnp.einsum('sxyd,scd->sxyc', shifted, kernel_in[:, tap_index], preferred_...]
    pallas_call x0 -> x8, Pallas kernels: none -> 50.7 us  [the longest x4 29 us: grads(): pl.pallas_call(functools.partial(grads_kernel, piece * per, len(added)),...]
    ppermute x8 -> x14, waiting for transfers between devices: 14.4 us -> 35.7 us  [the longest x2 31.1 us: to_chip(): lax.ppermute(array, 'lat', [(i, (i + 2 * shift) % count) for i in range(c...]
    reduce_scatter x1 -> x0, waiting for transfers between devices: 16.6 us -> none  [local(): grad_bank = lax.psum_scatter(grads, 'lat', scatter_dimension=0, tiled=True)]
    all_to_all x5 -> x2, starting transfers between devices: 24.9 us -> 11.3 us  [swap(): return lax.all_to_all(slots, 'lon', split_axis=0, concat_axis=0, tiled=True)]
    all_to_all x5 -> x2, waiting for transfers between devices: 76.5 us -> 65.1 us  [swap(): return lax.all_to_all(slots, 'lon', split_axis=0, concat_axis=0, tiled=True)]
    ppermute x8 -> x14, starting transfers between devices: 13.1 us -> 22.2 us  [the longest x8 15.9 us: across(): return lax.ppermute(array, axis, pairs)]
    gather x3 -> x0, local copies, waits for them, and re-layouts: 8.83 us -> none  [the longest x1 8.08 us: local(): kernel_in = jnp.take(column_kernels, slot_ids, axis=0)]
  transfers between devices with their start and end apart: 15 -> 16, of which waited for: 7 -> 5; matrix products, arithmetic and copies ran while one was open for 39% -> 1% of each run, Pallas kernels for 0% -> 25%
where the time goes in v1:
time: 197 us; the launch traced here: 196 us
  waiting for transfers between devices  101 us (51%)
  Pallas kernels  50.7 us (26%)
  starting transfers between devices  33.5 us (17%)
  local copies, waits for them, and re-layouts  9.99 us (5%)
    all_to_all x2, waiting for transfers between devices, swap(): return lax.all_to_all(slots, 'lon', split_axis=0, concat_axis=0, tiled=True)  65.1 us
    ppermute x2, waiting for transfers between devices, to_chip(): lax.ppermute(array, 'lat', [(i, (i + 2 * shift) % count) for i in range(c...  31.1 us
    pallas_call x4, Pallas kernels, grads(): pl.pallas_call(functools.partial(grads_kernel, piece * per, len(added)),...  29 us
    ppermute x8, starting transfers between devices, across(): return lax.ppermute(array, axis, pairs)  15.9 us
    pallas_call x1, Pallas kernels, taps(): pl.pallas_call(functools.partial(taps_kernel, per), grid=(columns * cap,)...  13.9 us
    all_to_all x2, starting transfers between devices, swap(): return lax.all_to_all(slots, 'lon', split_axis=0, concat_axis=0, tiled=True)  11.3 us
    unnamed x24, local copies, waits for them, and re-layouts  8.09 us
    ppermute x2, starting transfers between devices, to_chip(): lax.ppermute(array, 'lat', [(i, (i + 2 * shift) % count) for i in range(c...  6.29 us
  transfers between devices with their start and end apart: 16, of which 5 were waited for; matrix products, arithmetic and copies ran while one was open for 1% of the time, Pallas kernels for 25%

profile of v1, /device:TPU:0, one launch (start us, length us, event | category | flops | bytes accessed | tf_op | source)
XLA Modules:
  0.0 196.2 jit_solution(6192845058630458140)
XLA Ops:
  0.6 0.8 fusion.13
  1.4 2.3 %collective-permute-start = (bf16[1,128,128]{2,1,0:T(8,128)(2,1)S(1)}, bf16[1,128,128]{2,1,0:T(8,128)(2,1)S(1)}, u32[]{:S(2)}, u32[]{:S(2)}) collective-permute-start(bf16[1,128,128]{2,1,0:T(8,128)(2,1)S(1)} %get-tuple-element.66), channel_id=1, source_target_pairs={{0,8},{8,16},{16,24},{1,9},{9,17},{17,25},{2,10},{10,18},{18,26},{... | collective-permute-start | bytes 98312 | tf_op jit(solution)/shard_map/ppermute | solution.py:448
  3.8 1.3 collective-permute-start.1
  5.1 4.9 %collective-permute-start.5 = (bf16[8,9,128,128]{3,2,1,0:T(8,128)(2,1)}, bf16[8,9,128,128]{3,2,1,0:T(8,128)(2,1)}, u32[]{:S(2)}, u32[]{:S(2)}) collective-permute-start(bf16[8,9,128,128]{3,2,1,0:T(8,128)(2,1)} %refs_2_.1), channel_id=1, source_target_pairs={{0,16},{8,24},{16,0},{24,8},{1,17},{9,25},{17,1},{25,9},{2,18},{10... | collective-permute-start | bytes 7077896 | tf_op jit(solution)/shard_map/ppermute | solution.py:457
  10.0 0.9 fusion.12
  11.0 1.6 collective-permute-start.2
  12.6 3.3 %collective-permute-start.3 = (bf16[34,128]{1,0:T(8,128)(2,1)S(1)}, bf16[34,128]{1,0:T(8,128)(2,1)S(1)}, u32[]{:S(2)}, u32[]{:S(2)}) collective-permute-start(bf16[34,128]{1,0:T(8,128)(2,1)S(1)} %pad_maximum_fusion.1), channel_id=1, source_target_pairs={{0,7},{1,0},{2,1},{3,2},{4,3},{5,4},{6,5},{7,6},{8,15},{9,8},{10,9... | collective-permute-start | bytes 26120 | tf_op jit(solution)/shard_map/ppermute | solution.py:448
  15.8 1.6 collective-permute-done.2.west
  17.4 1.2 copy-done.5
  18.6 1.2 copy-done.6
  21.2 2.4 %dispatch.1 = bf16[8,2,592,128]{3,2,1,0:T(8,128)(2,1)S(1)} custom-call(s32[2,8]{1,0:T(2,128)S(1)} %copy-done.7, s32[256]{0:T(256)S(1)} %copy-done.9, bf16[32,128,128]{2,1,0:T(8,128)(2,1)S(1)} %copy-done.5, bf16[32,128,128]{2,1,0:T(8,128)(2,1)S(1)} %copy-done.6, bf16[1,128,128]{2,1,0:T(8,128)(2,1)S(1)} %collective-permute-done.north, ...), custom_call_target="tpu_custom_call" | custom-call | bytes 6000000 | tf_op jit(solution)/shard_map/dispatch/pallas_call | solution.py:121
  23.6 1.4 copy-done
  25.0 6.1 %all-to-all-start = ((bf16[8,2,592,128]{3,2,1,0:T(8,128)(2,1)}), bf16[8,2,592,128]{3,2,1,0:T(8,128)(2,1)S(1)}, u32[]{:S(2)}, u32[]{:S(2)}) async-start(bf16[8,2,592,128]{3,2,1,0:T(8,128)(2,1)} %copy-done), calls=%async_computation | async-start | bytes 4849664 | tf_op jit(solution)/shard_map/all_to_all | solution.py:461
  31.1 31.1 %collective-permute-done.5.refs_4_ = bf16[8,9,128,128]{3,2,1,0:T(8,128)(2,1)} collective-permute-done((bf16[8,9,128,128]{3,2,1,0:T(8,128)(2,1)}, bf16[8,9,128,128]{3,2,1,0:T(8,128)(2,1)}, u32[]{:S(2)}, u32[]{:S(2)}) %collective-permute-start.5) | collective-permute-done | bytes 2359328 | tf_op jit(solution)/shard_map/ppermute | solution.py:457
  62.2 24.4 %all-to-all-done.refs_1_.slots = bf16[8,2,592,128]{3,2,1,0:T(8,128)(2,1)S(1)} async-done(((bf16[8,2,592,128]{3,2,1,0:T(8,128)(2,1)}), bf16[8,2,592,128]{3,2,1,0:T(8,128)(2,1)S(1)}, u32[]{:S(2)}, u32[]{:S(2)}) %all-to-all-start) | async-done | bytes 2424864 | tf_op jit(solution)/shard_map/all_to_all | solution.py:461
  87.1 4.9 %grads.4 = bf16[8,9,128,128]{3,2,1,0:T(8,128)(2,1)} custom-call(s32[16]{0:T(128)S(1)} %fusion.2.refs_0_.place, bf16[8,2,592,128]{3,2,1,0:T(8,128)(2,1)S(1)} %all-to-all-done.refs_1_.slots), custom_call_target="tpu_custom_call" | custom-call | flops 500000000 | bytes 6000000 | tf_op jit(solution)/shard_map/grads/pallas_call | solution.py:319
  92.0 13.9 %taps.1 = bf16[8,2,592,128]{3,2,1,0:T(8,128)(2,1)S(1)} custom-call(s32[16]{0:T(128)S(1)} %fusion.2.refs_0_.place, bf16[8,2,592,128]{3,2,1,0:T(8,128)(2,1)S(1)} %all-to-all-done.refs_1_.slots, bf16[8,9,128,128]{3,2,1,0:T(8,128)(2,1)S(1)} %copy-done.4, bf16[8,9,128,128]{3,2,1,0:T(8,128)(2,1)} %collective-permute-done.4.refs_3_, ...), custom_call_target="tpu_custom_call" | custom-call | flops 2800000000 | bytes 10000000 | tf_op jit(solution)/shard_map/taps/pallas_call | solution.py:246
  105.9 1.4 copy-done.1
  107.3 5.2 %all-to-all-start.1 = ((bf16[8,2,592,128]{3,2,1,0:T(8,128)(2,1)}), bf16[8,2,592,128]{3,2,1,0:T(8,128)(2,1)}, u32[]{:S(2)}, u32[]{:S(2)}) async-start(bf16[8,2,592,128]{3,2,1,0:T(8,128)(2,1)} %copy-done.1), calls=%async_computation.1 | async-start | bytes 4849664 | tf_op jit(solution)/shard_map/all_to_all | solution.py:461
  112.6 6.4 %grads.6 = bf16[8,9,128,128]{3,2,1,0:T(8,128)(2,1)} custom-call(s32[16]{0:T(128)S(1)} %fusion.2.refs_0_.place, bf16[8,2,592,128]{3,2,1,0:T(8,128)(2,1)S(1)} %all-to-all-done.refs_1_.slots), custom_call_target="tpu_custom_call" | custom-call | flops 500000000 | bytes 6000000 | tf_op jit(solution)/shard_map/grads/pallas_call | solution.py:319
  119.0 7.1 %grads.5 = bf16[8,9,128,128]{3,2,1,0:T(8,128)(2,1)} custom-call(s32[16]{0:T(128)S(1)} %fusion.2.refs_0_.place, bf16[8,2,592,128]{3,2,1,0:T(8,128)(2,1)S(1)} %all-to-all-done.refs_1_.slots, bf16[8,9,128,128]{3,2,1,0:T(8,128)(2,1)} %collective-permute-done.11.refs_0_), custom_call_target="tpu_custom_call" | custom-call | flops 500000000 | bytes 6000000 | tf_op jit(solution)/shard_map/grads/pallas_call | solution.py:319
  126.1 1.4 collective-permute-start.12
  127.5 40.8 %all-to-all-done.1.slots = bf16[8,2,592,128]{3,2,1,0:T(8,128)(2,1)} async-done(((bf16[8,2,592,128]{3,2,1,0:T(8,128)(2,1)}), bf16[8,2,592,128]{3,2,1,0:T(8,128)(2,1)}, u32[]{:S(2)}, u32[]{:S(2)}) %all-to-all-start.1) | async-done | bytes 2424864 | tf_op jit(solution)/shard_map/all_to_all | solution.py:461
  168.3 4.3 %collect.1 = (bf16[32,128,128]{2,1,0:T(8,128)(2,1)}, f32[4896,128]{1,0:T(8,128)S(1)}, bf16[144,128]{1,0:T(8,128)(2,1)S(1)}, bf16[144,128]{1,0:T(8,128)(2,1)S(1)}...) custom-call(s32[2,8]{1,0:T(2,128)S(1)} %copy-done.8, s32[256]{0:T(256)S(1)} %copy-done.10, ...), custom_call_target="tpu_custom_call" | custom-call | bytes 8000000 | tf_op jit(solution)/shard_map/collect/pallas_call | solution.py:387
  172.5 1.4 copy-done.2
  173.9 1.3 collective-permute-start.7
  175.2 1.3 collective-permute-start.8
  176.6 3.0 %collective-permute-done.8.south = bf16[144,128]{1,0:T(8,128)(2,1)S(1)} collective-permute-done((bf16[144,128]{1,0:T(8,128)(2,1)S(1)}, bf16[144,128]{1,0:T(8,128)(2,1)S(1)}, u32[]{:S(2)}, u32[]{:S(2)}) %collective-permute-start.8) | collective-permute-done | bytes 36896 | tf_op jit(solution)/shard_map/ppermute | solution.py:448
  179.7 1.5 collective-permute-start.9
  181.2 3.3 %collective-permute-start.10 = (bf16[32,128]{1,0:T(8,128)(2,1)S(1)}, bf16[32,128]{1,0:T(8,128)(2,1)S(1)}, u32[]{:S(2)}, u32[]{:S(2)}) collective-permute-start(bf16[32,128]{1,0:T(8,128)(2,1)S(1)} %convert_element_type.35), channel_id=1, source_target_pairs={{0,7},{1,0},{2,1},{3,2},{4,3},{5,4},{6,5},{7,6},{8,15},{9,8},{10,9... | collective-permute-start | bytes 24584 | tf_op jit(solution)/shard_map/ppermute | solution.py:448
  184.5 10.6 %grads.7 = f32[8,9,128,128]{3,2,1,0:T(8,128)} custom-call(s32[16]{0:T(128)S(1)} %fusion.2.refs_0_.place, bf16[8,2,592,128]{3,2,1,0:T(8,128)(2,1)S(1)} %all-to-all-done.refs_1_.slots, bf16[8,9,128,128]{3,2,1,0:T(8,128)(2,1)} %collective-permute-done.12.refs_0_, bf16[8,9,128,128]{3,2,1,0:T(8,128)(2,1)} %collective-permute-done.13.refs_1_), custom_call_target="tpu_custom_call" | custom-call | flops 500000000 | bytes 6000000 | tf_op jit(solution)/shard_map/grads/pallas_call | solution.py:319
  195.1 1.1 finish.1
  (49 shorter events, 2.1 us)
Async XLA Ops:
  1.4 9.5 %collective-permute-start = (bf16[1,128,128]{2,1,0:T(8,128)(2,1)S(1)}, bf16[1,128,128]{2,1,0:T(8,128)(2,1)S(1)}, u32[]{:S(2)}, u32[]{:S(2)}) collective-permute-start(bf16[1,128,128]{2,1,0:T(8,128)(2,1)S(1)} %get-tuple-element.66), channel_id=1, source_target_pairs={{0,8},{8,16},{16,24},{1,9},{9,17},{17,25},{2,10},{10,18},{18,26},{... | collective-permute-start | bytes 98312 | tf_op jit(solution)/shard_map/ppermute | solution.py:448
  3.8 7.1 %collective-permute-start.1 = (bf16[1,128,128]{2,1,0:T(8,128)(2,1)S(1)}, bf16[1,128,128]{2,1,0:T(8,128)(2,1)S(1)}, u32[]{:S(2)}, u32[]{:S(2)}) collective-permute-start(bf16[1,128,128]{2,1,0:T(8,128)(2,1)S(1)} %get-tuple-element.65), channel_id=1, source_target_pairs={{8,0},{16,8},{24,16},{9,1},{17,9},{25,17},{10,2},{18,10},{26,18},{... | collective-permute-start | bytes 98312 | tf_op jit(solution)/shard_map/ppermute | solution.py:448
  5.1 57.1 %collective-permute-start.5 = (bf16[8,9,128,128]{3,2,1,0:T(8,128)(2,1)}, bf16[8,9,128,128]{3,2,1,0:T(8,128)(2,1)}, u32[]{:S(2)}, u32[]{:S(2)}) collective-permute-start(bf16[8,9,128,128]{3,2,1,0:T(8,128)(2,1)} %refs_2_.1), channel_id=1, source_target_pairs={{0,16},{8,24},{16,0},{24,8},{1,17},{9,25},{17,1},{25,9},{2,18},{10... | collective-permute-start | bytes 7077896 | tf_op jit(solution)/shard_map/ppermute | solution.py:457
  11.0 6.4 %collective-permute-start.2 = (bf16[34,128]{1,0:T(8,128)(2,1)S(1)}, bf16[34,128]{1,0:T(8,128)(2,1)S(1)}, u32[]{:S(2)}, u32[]{:S(2)}) collective-permute-start(bf16[34,128]{1,0:T(8,128)(2,1)S(1)} %pad_maximum_fusion), channel_id=1, source_target_pairs={{0,1},{1,2},{2,3},{3,4},{4,5},{5,6},{6,7},{7,0},{8,9},{9,10},{10,1... | collective-permute-start | bytes 26120 | tf_op jit(solution)/shard_map/ppermute | solution.py:448
  12.6 4.8 %collective-permute-start.3 = (bf16[34,128]{1,0:T(8,128)(2,1)S(1)}, bf16[34,128]{1,0:T(8,128)(2,1)S(1)}, u32[]{:S(2)}, u32[]{:S(2)}) collective-permute-start(bf16[34,128]{1,0:T(8,128)(2,1)S(1)} %pad_maximum_fusion.1), channel_id=1, source_target_pairs={{0,7},{1,0},{2,1},{3,2},{4,3},{5,4},{6,5},{7,6},{8,15},{9,8},{10,9... | collective-permute-start | bytes 26120 | tf_op jit(solution)/shard_map/ppermute | solution.py:448
  17.4 1.2 copy-start.5
  18.6 1.2 copy-start.6
  19.9 0.7 copy-start.7
  20.5 0.7 copy-start.9
  23.6 1.4 copy-start
  25.0 61.5 %all-to-all-start = ((bf16[8,2,592,128]{3,2,1,0:T(8,128)(2,1)}), bf16[8,2,592,128]{3,2,1,0:T(8,128)(2,1)S(1)}, u32[]{:S(2)}, u32[]{:S(2)}) async-start(bf16[8,2,592,128]{3,2,1,0:T(8,128)(2,1)} %copy-done), calls=%async_computation | async-start | bytes 4849664 | tf_op jit(solution)/shard_map/all_to_all | solution.py:461
  31.1 60.9 %collective-permute-start.4 = (bf16[8,9,128,128]{3,2,1,0:T(8,128)(2,1)}, bf16[8,9,128,128]{3,2,1,0:T(8,128)(2,1)}, u32[]{:S(2)}, u32[]{:S(2)}) collective-permute-start(bf16[8,9,128,128]{3,2,1,0:T(8,128)(2,1)} %refs_2_.1), channel_id=1, source_target_pairs={{0,8},{8,0},{16,24},{24,16},{1,9},{9,1},{17,25},{25,17},{2,10},{10... | collective-permute-start | bytes 7077896 | tf_op jit(solution)/shard_map/ppermute | solution.py:452
  62.2 29.8 %collective-permute-start.6 = (bf16[8,9,128,128]{3,2,1,0:T(8,128)(2,1)}, bf16[8,9,128,128]{3,2,1,0:T(8,128)(2,1)}, u32[]{:S(2)}, u32[]{:S(2)}) collective-permute-start(bf16[8,9,128,128]{3,2,1,0:T(8,128)(2,1)} %collective-permute-done.5.refs_4_), channel_id=1, source_target_pairs={{0,8},{8,0},{16,24},{24,16},{1,9},{9,1},{17,25},{25,17},{2,10},{10... | collective-permute-start | bytes 7077896 | tf_op jit(solution)/shard_map/ppermute | solution.py:452
  87.0 4.9 %copy-start.4 = (bf16[8,9,128,128]{3,2,1,0:T(8,128)(2,1)S(1)}, bf16[8,9,128,128]{3,2,1,0:T(8,128)(2,1)}, u32[]{:S(2)}) copy-start(bf16[8,9,128,128]{3,2,1,0:T(8,128)(2,1)} %refs_2_.1) | copy-start | bytes 7077892
  92.0 27.0 %collective-permute-start.11 = (bf16[8,9,128,128]{3,2,1,0:T(8,128)(2,1)}, bf16[8,9,128,128]{3,2,1,0:T(8,128)(2,1)}, u32[]{:S(2)}, u32[]{:S(2)}) collective-permute-start(bf16[8,9,128,128]{3,2,1,0:T(8,128)(2,1)} %grads.4), channel_id=1, source_target_pairs={{0,8},{8,0},{16,24},{24,16},{1,9},{9,1},{17,25},{25,17},{2,10},{10... | collective-permute-start | bytes 7077896 | tf_op jit(solution)/shard_map/ppermute | solution.py:452
  105.9 1.4 copy-start.1
  107.3 60.9 %all-to-all-start.1 = ((bf16[8,2,592,128]{3,2,1,0:T(8,128)(2,1)}), bf16[8,2,592,128]{3,2,1,0:T(8,128)(2,1)}, u32[]{:S(2)}, u32[]{:S(2)}) async-start(bf16[8,2,592,128]{3,2,1,0:T(8,128)(2,1)} %copy-done.1), calls=%async_computation.1 | async-start | bytes 4849664 | tf_op jit(solution)/shard_map/all_to_all | solution.py:461
  119.0 49.3 %copy-start.8 = (s32[2,8]{1,0:T(2,128)S(1)}, s32[2,8]{1,0:T(2,128)}, u32[]{:S(2)}) copy-start(s32[2,8]{1,0:T(2,128)} %experts.3) | copy-start | bytes 196
  119.0 49.3 %copy-start.10 = (s32[256]{0:T(256)S(1)}, s32[256]{0:T(256)}, u32[]{:S(2)}) copy-start(s32[256]{0:T(256)} %owner.3) | copy-start | bytes 3076
  119.0 65.6 %collective-permute-start.13 = (bf16[8,9,128,128]{3,2,1,0:T(8,128)(2,1)}, bf16[8,9,128,128]{3,2,1,0:T(8,128)(2,1)}, u32[]{:S(2)}, u32[]{:S(2)}) collective-permute-start(bf16[8,9,128,128]{3,2,1,0:T(8,128)(2,1)} %grads.6), channel_id=1, source_target_pairs={{0,8},{8,0},{16,24},{24,16},{1,9},{9,1},{17,25},{25,17},{2,10},{10... | collective-permute-start | bytes 7077896 | tf_op jit(solution)/shard_map/ppermute | solution.py:452
  126.1 58.4 %collective-permute-start.12 = (bf16[8,9,128,128]{3,2,1,0:T(8,128)(2,1)}, bf16[8,9,128,128]{3,2,1,0:T(8,128)(2,1)}, u32[]{:S(2)}, u32[]{:S(2)}) collective-permute-start(bf16[8,9,128,128]{3,2,1,0:T(8,128)(2,1)} %grads.5), channel_id=1, source_target_pairs={{0,16},{8,24},{16,0},{24,8},{1,17},{9,25},{17,1},{25,9},{2,18},{10... | collective-permute-start | bytes 7077896 | tf_op jit(solution)/shard_map/ppermute | solution.py:457
  172.5 1.4 copy-start.2
  173.9 2.6 %collective-permute-start.7 = (bf16[144,128]{1,0:T(8,128)(2,1)S(1)}, bf16[144,128]{1,0:T(8,128)(2,1)S(1)}, u32[]{:S(2)}, u32[]{:S(2)}) collective-permute-start(bf16[144,128]{1,0:T(8,128)(2,1)S(1)} %get-tuple-element.59), channel_id=1, source_target_pairs={{0,8},{8,16},{16,24},{1,9},{9,17},{17,25},{2,10},{10,18},{18,26},{... | collective-permute-start | bytes 110600 | tf_op jit(solution)/shard_map/ppermute | solution.py:448
  175.2 4.4 %collective-permute-start.8 = (bf16[144,128]{1,0:T(8,128)(2,1)S(1)}, bf16[144,128]{1,0:T(8,128)(2,1)S(1)}, u32[]{:S(2)}, u32[]{:S(2)}) collective-permute-start(bf16[144,128]{1,0:T(8,128)(2,1)S(1)} %get-tuple-element.60), channel_id=1, source_target_pairs={{8,0},{16,8},{24,16},{9,1},{17,9},{25,17},{10,2},{18,10},{26,18},{... | collective-permute-start | bytes 110600 | tf_op jit(solution)/shard_map/ppermute | solution.py:448
  179.7 15.4 %collective-permute-start.9 = (bf16[32,128]{1,0:T(8,128)(2,1)S(1)}, bf16[32,128]{1,0:T(8,128)(2,1)S(1)}, u32[]{:S(2)}, u32[]{:S(2)}) collective-permute-start(bf16[32,128]{1,0:T(8,128)(2,1)S(1)} %convert_element_type.32), channel_id=1, source_target_pairs={{0,1},{1,2},{2,3},{3,4},{4,5},{5,6},{6,7},{7,0},{8,9},{9,10},{10,1... | collective-permute-start | bytes 24584 | tf_op jit(solution)/shard_map/ppermute | solution.py:448
  181.2 13.9 %copy-start.3 = (f32[4896,128]{1,0:T(8,128)S(1)}, f32[4896,128]{1,0:T(8,128)}, u32[]{:S(2)}) copy-start(f32[4896,128]{1,0:T(8,128)} %copy-done.2) | copy-start | bytes 7520260
  181.2 13.9 %collective-permute-start.10 = (bf16[32,128]{1,0:T(8,128)(2,1)S(1)}, bf16[32,128]{1,0:T(8,128)(2,1)S(1)}, u32[]{:S(2)}, u32[]{:S(2)}) collective-permute-start(bf16[32,128]{1,0:T(8,128)(2,1)S(1)} %convert_element_type.35), channel_id=1, source_target_pairs={{0,7},{1,0},{2,1},{3,2},{4,3},{5,4},{6,5},{7,6},{8,15},{9,8},{10,9... | collective-permute-start | bytes 24584 | tf_op jit(solution)/shard_map/ppermute | solution.py:448

commit v2 on v1

v2 whole, which is shorter than its diff:
```python
import functools

import jax
import jax.numpy as jnp
from jax import lax
from jax.experimental import pallas as pl
from jax.experimental.pallas import tpu as pltpu
from jax.sharding import PartitionSpec as P

BS = 16
CAP = 2
EDGE = BS + 2
CELLS = BS * BS
MAIN = EDGE * BS
TAIL = 48
OWN = 2 * BS
RING = 5
LINES = OWN + RING
NUMBER = 4 * BS + 4
WINDOW = EDGE + TAIL // BS
BACK = BS + WINDOW
GAP = 8
SPAN = 2 * BS
F32 = jnp.float32
BF16 = jnp.bfloat16


def params(mib):
    return pltpu.CompilerParams(vmem_limit_bytes=mib * 1024 * 1024)


TOKEN = jax.ShapeDtypeStruct((8, 128), jnp.float32)


def whole(memory=pltpu.VMEM):
    return pl.BlockSpec(memory_space=memory)


def copy(source, target, sem):
    return pltpu.make_async_copy(source, target, sem)


def corner(block, lon_blocks):
    top = lax.div(block, lon_blocks) * BS
    return top, pl.multiple_of(lax.rem(block, lon_blocks) * BS, BS)


def tables(columns):
    return [
        pltpu.SMEM((columns * CAP,), jnp.int32),
        pltpu.SMEM((columns * CAP,), jnp.int32),
        pltpu.SMEM((columns,), jnp.int32),
    ]


def plan_slots(experts, owner, blocks, numbers, counts, per, columns):
    lat_blocks, lon_blocks = experts.shape

    def clear_slot(s, carry):
        blocks[s] = -1
        numbers[s] = 0
        return carry

    def clear_count(s, carry):
        counts[s] = 0
        return carry

    lax.fori_loop(0, columns * CAP, clear_slot, 0)
    lax.fori_loop(0, columns, clear_count, 0)

    def place(b, carry):
        stored = owner[experts[lax.div(b, lon_blocks), lax.rem(b, lon_blocks)]]
        group = lax.div(stored, per)
        column = lax.rem(group, columns)
        rank = counts[column]
        counts[column] = rank + 1
        slot = column * CAP + rank
        blocks[slot] = b
        numbers[slot] = lax.div(group, columns) * per + lax.rem(stored, per)
        return carry

    lax.fori_loop(0, lat_blocks * lon_blocks, place, 0)


def own_kernel(per, columns, experts, owner, fields, cot, *refs):
    out, grid, cells, blank, blocks, numbers, counts, load_sems, sems = refs
    height, width, chans = fields.shape
    sources = (cells, grid)
    loads = [copy(cot, cells, load_sems.at[0]), copy(fields, grid, load_sems.at[1])]
    for load in loads:
        load.start()
    plan_slots(experts, owner, blocks, numbers, counts, per, columns)
    blank[...] = jnp.zeros(blank.shape, BF16)
    for part, source in enumerate(sources):
        loads[part].wait()
        for column in range(columns):
            for r in range(CAP):
                s = column * CAP + r
                held = blocks[s]
                top, left = corner(jnp.maximum(held, 0), experts.shape[1])
                target = out.at[column, r, pl.ds(part * BS, BS)]

                @pl.when(held >= 0)
                def _():
                    copy(
                        source.at[pl.ds(top, BS), pl.ds(left, BS), :], target, sems.at[part, s]
                    ).start()

                @pl.when(held < 0)
                def _():
                    copy(blank, target, sems.at[part, s]).start()

    for part in range(2):
        for s in range(columns * CAP):
            copy(blank, out.at[0, 0, pl.ds(0, BS)], sems.at[part, s]).wait()


def dispatch_own(experts, owner, fields, cot, per, columns):
    chans = cot.shape[2]
    out = pl.pallas_call(
        functools.partial(own_kernel, per, columns),
        out_shape=[
            jax.ShapeDtypeStruct((columns, CAP, OWN, BS, chans), BF16),
        ],
        in_specs=[whole(pltpu.SMEM)] * 2 + [whole(pltpu.HBM)] * 2,
        out_specs=[whole(pltpu.HBM)],
        scratch_shapes=[
            pltpu.VMEM(fields.shape, BF16),
            pltpu.VMEM(cot.shape, BF16),
            pltpu.VMEM((BS, BS, chans), BF16),
        ]
        + tables(columns)
        + [pltpu.SemaphoreType.DMA((2,)), pltpu.SemaphoreType.DMA((2, columns * CAP))],
        compiler_params=params(60),
        cost_estimate=pl.CostEstimate(flops=0, bytes_accessed=6_000_000, transcendentals=0),
        name="dispatch_own",
    )(experts, owner, fields, cot)
    return out[0]


def rims_kernel(north, south, first, last, first_out, last_out):
    width = north.shape[1]
    for inner, out, left, column in (
        (first, first_out, 0, 0),
        (last, last_out, width - BS, BS - 1),
    ):
        above = north[0, left : left + BS, :].astype(F32)
        below = south[0, left : left + BS, :].astype(F32)
        out[...] = jnp.concatenate(
            [above[column : column + 1], inner[...], below[column : column + 1]], axis=0
        ).astype(BF16)


def rims_of(north, south, first, last):
    height, chans = first.shape
    return pl.pallas_call(
        rims_kernel,
        out_shape=[jax.ShapeDtypeStruct((height + 2, chans), BF16)] * 2,
        in_specs=[whole()] * 4,
        out_specs=[whole()] * 2,
        compiler_params=params(4),
        name="rims",
    )(north, south, first, last)


def corners_kernel(above, below, left, right, _, left_out, right_out):
    height = left.shape[0]
    row = lax.broadcasted_iota(jnp.int32, left.shape, 0)
    stride = above.shape[0]
    for line, out, start, column in (
        (left, left_out, 0, GAP - 1),
        (right, right_out, stride - BS, BS - GAP),
    ):
        top = above[start : start + BS, :].astype(F32)[column : column + 1]
        bottom = below[start : start + BS, :].astype(F32)[column : column + 1]
        out[...] = (
            line[...]
            + jnp.where(row == 0, top, 0.0)
            + jnp.where(row == height - 1, bottom, 0.0)
        ).astype(BF16)


def corners_of(above, below, left, right, after):
    return pl.pallas_call(
        corners_kernel,
        out_shape=[jax.ShapeDtypeStruct(left.shape, BF16)] * 2,
        in_specs=[whole()] * 4 + [whole(pltpu.HBM)],
        out_specs=[whole()] * 2,
        compiler_params=params(4),
        name="corners",
    )(above, below, left, right, after)


def ring_kernel(
    per, columns, me, experts, owner, fields, north, south, west, east, *refs
):
    outs = refs[:columns]
    rows, wide, rings, blocks, numbers, counts, load_sem, sems = refs[columns:]
    height, width, chans = fields.shape
    stride = width + 2 * GAP
    load = copy(fields, rows.at[pl.ds(1, height)], load_sem)
    load.start()
    plan_slots(experts, owner, blocks, numbers, counts, per, columns)
    rows[0] = north[0]
    rows[height + 1] = south[0]
    load.wait()

    def widen(r, carry):
        start = pl.multiple_of(r * stride + GAP, 8)
        wide[pl.ds(start, width), :] = rows[r].astype(F32)
        return carry

    lax.fori_loop(0, height + 2, widen, 0)
    wide[pl.ds(GAP - 1, height + 2, stride=stride), :] = west[...].astype(F32)
    wide[pl.ds(GAP + width, height + 2, stride=stride), :] = east[...].astype(F32)
    for k in range(columns):
        for r in range(CAP):
            s = k * CAP + r
            slot = (me[0] ^ k) * CAP + r
            top, left = corner(jnp.maximum(blocks[slot], 0), experts.shape[1])
            start = pl.multiple_of(top * stride + left, 8)
            upper = wide[pl.ds(start, BS + 2 * GAP), :]
            start = pl.multiple_of(start + (EDGE - 1) * stride, 8)
            lower = wide[pl.ds(start, BS + 2 * GAP), :]
            start = (top + 1) * stride + left
            ring = jnp.concatenate(
                [
                    upper[GAP - 1 : GAP + BS + 1],
                    lower[GAP - 1 : GAP + BS + 1],
                    wide[pl.ds(start + GAP - 1, BS, stride=stride), :],
                    wide[pl.ds(start + GAP + BS, BS, stride=stride), :],
                    jnp.full((RING * BS - NUMBER, chans), numbers[slot].astype(F32), F32),
                ],
                axis=0,
            )
            rings[s] = ring.astype(BF16).reshape(RING, BS, chans)
            copy(rings.at[s], outs[k].at[r], sems.at[s]).start()
    for k in range(columns):
        for r in range(CAP):
            s = k * CAP + r
            copy(rings.at[s], outs[k].at[r], sems.at[s]).wait()


def dispatch_rings(me, experts, owner, fields, north, south, west, east, per, columns):
    height, width, chans = fields.shape
    slots = columns * CAP
    return pl.pallas_call(
        functools.partial(ring_kernel, per, columns),
        out_shape=[jax.ShapeDtypeStruct((CAP, RING, BS, chans), BF16)] * columns,
        in_specs=[whole(pltpu.SMEM)] * 3 + [whole(pltpu.HBM)] + [whole()] * 4,
        out_specs=[whole(pltpu.HBM)] * columns,
        scratch_shapes=[
            pltpu.VMEM((height + 2, width, chans), BF16),
            pltpu.VMEM(((height + 2) * (width + 2 * GAP), chans), F32),
            pltpu.VMEM((slots, RING, BS, chans), BF16),
        ]
        + tables(columns)
        + [pltpu.SemaphoreType.DMA, pltpu.SemaphoreType.DMA((slots,))],
        compiler_params=params(60),
        cost_estimate=pl.CostEstimate(flops=0, bytes_accessed=3_000_000, transcendentals=0),
        name="dispatch_rings",
    )(me, experts, owner, fields, north, south, west, east)


def load_slot(own, ring, column, r, target, sem):
    copy(own.at[column, r], target.at[pl.ds(0, OWN)], sem).start()
    copy(ring.at[r], target.at[pl.ds(OWN, RING)], sem).start()


def shifted_windows(data, wide):
    chans = wide.shape[1]
    ring = data[OWN:LINES].reshape(RING * BS, chans).astype(F32)
    bottom = SPAN * (EDGE - 1)
    wide[7 : 7 + EDGE, :] = ring[0:EDGE]
    wide[bottom + 7 : bottom + 7 + EDGE, :] = ring[EDGE : 2 * EDGE]
    wide[pl.ds(SPAN + 7, BS, stride=SPAN), :] = ring[2 * EDGE : 2 * EDGE + BS]
    wide[pl.ds(SPAN + 8 + BS, BS, stride=SPAN), :] = ring[2 * EDGE + BS : NUMBER]
    for x in range(BS):
        start = SPAN * (x + 1) + 8
        wide[start : start + BS, :] = data[BS + x].astype(F32)
    first = [wide[SPAN * u + 7 : SPAN * u + 7 + BS, :] for u in range(EDGE)]
    third = [wide[SPAN * u + 9 : SPAN * u + 9 + BS, :] for u in range(EDGE)]
    return (
        jnp.concatenate(first, axis=0).astype(BF16),
        jnp.concatenate(
            [
                wide[8 : 8 + BS, :].astype(BF16),
                data[BS:OWN].reshape(CELLS, chans),
                wide[bottom + 8 : bottom + 8 + BS, :].astype(BF16),
            ],
            axis=0,
        ),
        jnp.concatenate(third, axis=0).astype(BF16),
    )


def nine_taps(windows):
    return jnp.concatenate(
        [w[BS * a : BS * a + CELLS] for a in range(3) for w in windows], axis=1
    )


def load_banks(place, banks, held, sems, slots, size):
    for s in range(slots):
        piece = lax.div(place[s], size)
        row = lax.rem(place[s], size)
        p = 0
        for bank in banks:
            for start in range(0, bank.shape[0], size):

                @pl.when(piece == p)
                def _():
                    copy(bank.at[start + row], held.at[s], sems.at[s]).start()

                p += 1


def taps_kernel(size, columns, pieces, extras, me, place, own, *refs):
    rings, refs = refs[:columns], refs[columns:]
    banks, refs = refs[:pieces], refs[pieces + extras :]
    (out, _, held, stage, result, wide, cots, lines, before, after, bank_sems, load_sems,
     out_sems) = refs
    chans = cots.shape[1]
    slots = CAP * columns
    for k in range(columns):
        for r in range(CAP):
            s = k * CAP + r
            load_slot(own, rings[k], me[0] ^ k, r, stage.at[s], load_sems.at[s])
    load_banks(place, banks, held, bank_sems, slots, size)
    cots[...] = jnp.zeros(cots.shape, F32)
    lines[...] = jnp.zeros(lines.shape, BF16)
    before[...] = jnp.zeros(before.shape, F32)
    after[...] = jnp.zeros(after.shape, F32)

    def visit(s, carry):
        copy(stage.at[s], stage.at[s], load_sems.at[s]).wait()
        copy(held.at[s], held.at[s], bank_sems.at[s]).wait()
        data = stage.at[s]
        bank = held.at[s]
        for x in range(BS):
            cots[SPAN * x + 8 : SPAN * x + 8 + BS, :] = data[x].astype(F32)
            lines[1, BS * (x + 2) : BS * (x + 3), :] = data[x]
        for x in range(BS):
            lines[0, BS * (x + 2) : BS * (x + 3), :] = cots[
                SPAN * x + 9 : SPAN * x + 9 + BS, :
            ].astype(BF16)
            lines[2, BS * (x + 2) : BS * (x + 3), :] = cots[
                SPAN * x + 7 : SPAN * x + 7 + BS, :
            ].astype(BF16)
        before[2 : 2 + BS, :] = cots[pl.ds(8, BS, stride=SPAN), :]
        after[EDGE + 2 : EDGE + 2 + BS, :] = cots[pl.ds(8 + BS - 1, BS, stride=SPAN), :]
        sides = []
        for a in range(3):
            for b in range(3):
                if b == 0:
                    tail = before[2 - a : 2 - a + TAIL, :].astype(BF16)
                elif b == 2:
                    tail = after[2 - a : 2 - a + TAIL, :].astype(BF16)
                else:
                    tail = jnp.zeros((TAIL, chans), BF16)
                main = lines[b, (2 - a) * BS : (2 - a) * BS + MAIN, :]
                sides.append(jnp.concatenate([main, tail], axis=0))
        spread = lax.dot_general(
            jnp.concatenate(sides, axis=1),
            jnp.concatenate([bank[t] for t in range(9)], axis=1),
            (((1,), (1,)), ((), ())),
            preferred_element_type=F32,
        )
        result[s, BS:] = spread.astype(BF16).reshape(WINDOW, BS, chans)
        output = jnp.dot(
            nine_taps(shifted_windows(data, wide)),
            bank[...].reshape(9 * chans, chans),
            preferred_element_type=F32,
        )
        result[s, 0:BS] = output.astype(BF16).reshape(BS, BS, chans)
        target = out.at[me[0] ^ lax.div(s, CAP), lax.rem(s, CAP)]
        copy(result.at[s], target, out_sems.at[s]).start()
        return carry

    lax.fori_loop(0, slots, visit, 0)
    for s in range(slots):
        copy(result.at[s], result.at[s], out_sems.at[s]).wait()


def taps(me, place, own, rings, banks, after):
    columns, chans = len(rings), own.shape[-1]
    slots = CAP * columns
    size = min(bank.shape[0] for bank in banks)
    inputs = [me, place, own] + list(rings) + list(banks) + list(after)
    return pl.pallas_call(
        functools.partial(taps_kernel, size, columns, len(banks), len(after)),
        out_shape=[
            jax.ShapeDtypeStruct((columns, CAP, BACK, BS, chans), BF16),
            TOKEN,
        ],
        in_specs=[whole(pltpu.SMEM)] * 2
        + [whole(pltpu.HBM)] * (len(inputs) - 2),
        out_specs=[whole(pltpu.HBM)] * 2,
        scratch_shapes=[
            pltpu.VMEM((slots,) + banks[0].shape[1:], BF16),
            pltpu.VMEM((slots, LINES, BS, chans), BF16),
            pltpu.VMEM((slots, BACK, BS, chans), BF16),
            pltpu.VMEM((EDGE * SPAN, chans), F32),
            pltpu.VMEM((EDGE * SPAN, chans), F32),
            pltpu.VMEM((3, (BS + 4) * BS, chans), BF16),
            pltpu.VMEM((TAIL + 8, chans), F32),
            pltpu.VMEM((TAIL + 8, chans), F32),
        ]
        + [pltpu.SemaphoreType.DMA((slots,))] * 3,
        compiler_params=params(60),
        cost_estimate=pl.CostEstimate(
            flops=175_000_000 * slots, bytes_accessed=600_000 * slots, transcendentals=0
        ),
        name="taps",
    )(*inputs)


def grads_kernel(piece, per, columns, terms, extras, me, place, own, *refs):
    rings, refs = refs[:columns], refs[columns:]
    added, refs = refs[:terms], refs[terms + extras :]
    (out, _, stage, extra, total, wide, result, seen, load_sems, extra_sems,
     out_sems) = refs
    slots = CAP * columns
    chans = wide.shape[1]
    for k in range(columns):
        for r in range(CAP):
            s = k * CAP + r

            @pl.when(lax.div(place[s], per) == piece)
            def _():
                load_slot(own, rings[k], me[0] ^ k, r, stage.at[s], load_sems.at[s])

    for j in range(per):
        seen[j] = 0
        for i, term in enumerate(added):
            copy(term.at[j], extra.at[i, j], extra_sems.at[i * per + j]).start()

    def visit(s, carry):
        index = place[s]

        @pl.when(lax.div(index, per) == piece)
        def _():
            j = lax.rem(index, per)
            copy(stage.at[s], stage.at[s], load_sems.at[s]).wait()
            data = stage.at[s]
            term = lax.dot_general(
                data[0:BS].reshape(CELLS, chans),
                nine_taps(shifted_windows(data, wide)),
                (((0,), (0,)), ((), ())),
                preferred_element_type=F32,
            )

            @pl.when(seen[j] == 0)
            def _():
                total[j] = term

            @pl.when(seen[j] > 0)
            def _():
                total[j] += term

            seen[j] = 1

        return carry

    lax.fori_loop(0, slots, visit, 0)

    def expert(j, carry):
        for i in range(terms):
            copy(extra.at[i, j], extra.at[i, j], extra_sems.at[i * per + j]).wait()

        @pl.when(seen[j] > 0)
        def _():
            value = total[j]
            for i in range(terms):
                value = value + extra[i, j].astype(F32)
            result[j] = value.astype(result.dtype)

        @pl.when(seen[j] == 0)
        def _():
            value = jnp.zeros(result.shape[1:], F32)
            for i in range(terms):
                value = value + extra[i, j].astype(F32)
            result[j] = value.astype(result.dtype)

        copy(result.at[j], out.at[j], out_sems.at[j]).start()
        return carry

    lax.fori_loop(0, per, expert, 0)
    for j in range(per):
        copy(result.at[j], out.at[j], out_sems.at[j]).wait()


def grads(me, place, own, rings, piece, bank_shape, added, after, dtype):
    per, taps_n, chans, outs = bank_shape
    columns = len(rings)
    slots = CAP * columns
    terms = max(len(added), 1)
    shape = (per, outs, taps_n * chans)
    inputs = [me, place, own] + list(rings) + list(added) + list(after)
    return pl.pallas_call(
        functools.partial(grads_kernel, piece, per, columns, len(added), len(after)),
        out_shape=[jax.ShapeDtypeStruct(shape, dtype), TOKEN],
        in_specs=[whole(pltpu.SMEM)] * 2
        + [whole(pltpu.HBM)] * (len(inputs) - 2),
        out_specs=[whole(pltpu.HBM)] * 2,
        scratch_shapes=[
            pltpu.VMEM((slots, LINES, BS, chans), BF16),
            pltpu.VMEM((terms, per if added else 1) + shape[1:], BF16),
            pltpu.VMEM(shape, F32),
            pltpu.VMEM((EDGE * SPAN, chans), F32),
            pltpu.VMEM(shape, dtype),
            pltpu.SMEM((per,), jnp.int32),
            pltpu.SemaphoreType.DMA((slots,)),
            pltpu.SemaphoreType.DMA((terms * per,)),
            pltpu.SemaphoreType.DMA((per,)),
        ],
        compiler_params=params(60),
        cost_estimate=pl.CostEstimate(
            flops=300_000_000, bytes_accessed=6_000_000, transcendentals=0
        ),
        name="grads",
    )(*inputs)


def bank_kernel(count, *refs):
    terms, refs = refs[:count], refs[count:]
    out = refs[0]
    stages, refs = refs[2 : count + 2], refs[count + 2 :]
    result, load_sems, out_sems = refs
    per, taps_n, chans, outs = out.shape
    for j in range(per):
        for i, (term, stage) in enumerate(zip(terms, stages)):
            copy(term.at[j], stage.at[j], load_sems.at[i * per + j]).start()

    def expert(j, carry):
        for i, stage in enumerate(stages):
            copy(stage.at[j], stage.at[j], load_sems.at[i * per + j]).wait()
        for t in range(taps_n):
            columns = slice(t * chans, (t + 1) * chans)
            value = stages[0][j, :, columns].astype(F32)
            for stage in stages[1:]:
                value = value + stage[j, :, columns].astype(F32)
            result[j, t] = value.T
        copy(result.at[j], out.at[j], out_sems.at[j]).start()
        return carry

    lax.fori_loop(0, per, expert, 0)
    for j in range(per):
        copy(result.at[j], out.at[j], out_sems.at[j]).wait()


def bank_of(terms, bank_shape):
    per = bank_shape[0]
    return pl.pallas_call(
        functools.partial(bank_kernel, len(terms)),
        out_shape=[jax.ShapeDtypeStruct(bank_shape, F32), TOKEN],
        in_specs=[whole(pltpu.HBM)] * len(terms),
        out_specs=[whole(pltpu.HBM)] * 2,
        scratch_shapes=[pltpu.VMEM(term.shape, term.dtype) for term in terms]
        + [
            pltpu.VMEM(bank_shape, F32),
            pltpu.SemaphoreType.DMA((len(terms) * per,)),
            pltpu.SemaphoreType.DMA((per,)),
        ],
        compiler_params=params(24),
        cost_estimate=pl.CostEstimate(flops=0, bytes_accessed=12_000_000, transcendentals=0),
        name="bank",
    )(*terms)


def canvas_kernel(per, columns, shape, extras, experts, owner, source, *refs):
    refs = refs[extras:]
    canvas, north, south, west, east, blocks, numbers, counts = refs
    height, width, chans = shape
    stride = width + 2 * GAP
    plan_slots(experts, owner, blocks, numbers, counts, per, columns)

    def clear(r, carry):
        start = pl.multiple_of(r * stride, 8)
        canvas[pl.ds(start, stride), :] = jnp.zeros((stride, chans), F32)
        return carry

    lax.fori_loop(0, height + 2, clear, 0)

    def visit(s, carry):
        data = source.at[lax.div(s, CAP), lax.rem(s, CAP)]
        held = blocks[s]

        @pl.when(held >= 0)
        def _():
            top, left = corner(held, experts.shape[1])
            for u in range(EDGE):
                place = pl.ds(pl.multiple_of((top + u) * stride + GAP + left, 8), BS)
                canvas[place, :] = canvas[place, :] + data[BS + u].astype(F32)
            tail = data[BS + EDGE : BACK].reshape(TAIL, chans).astype(F32)
            start = top * stride + left
            place = pl.ds(start + GAP - 1, EDGE, stride=stride)
            canvas[place, :] = canvas[place, :] + tail[0:EDGE]
            place = pl.ds(start + GAP + BS, EDGE, stride=stride)
            canvas[place, :] = canvas[place, :] + tail[EDGE : 2 * EDGE]

        return carry

    lax.fori_loop(0, columns * CAP, visit, 0)
    north[...] = canvas[0:stride, :].astype(BF16)
    south[...] = canvas[(height + 1) * stride : (height + 2) * stride, :].astype(BF16)
    west[...] = canvas[pl.ds(stride + GAP - 1, height, stride=stride), :]
    east[...] = canvas[pl.ds(stride + GAP + width, height, stride=stride), :]


def canvas_of(experts, owner, source, after, shape, per):
    height, width, chans = shape
    columns = source.shape[0]
    stride = width + 2 * GAP
    return pl.pallas_call(
        functools.partial(canvas_kernel, per, columns, shape, len(after)),
        out_shape=(
            jax.ShapeDtypeStruct(((height + 2) * stride, chans), F32),
            jax.ShapeDtypeStruct((stride, chans), BF16),
            jax.ShapeDtypeStruct((stride, chans), BF16),
            jax.ShapeDtypeStruct((height, chans), F32),
            jax.ShapeDtypeStruct((height, chans), F32),
        ),
        in_specs=[whole(pltpu.SMEM)] * 2
        + [whole()]
        + [whole(pltpu.HBM)] * len(after),
        out_specs=(whole(),) * 5,
        scratch_shapes=tables(columns),
        compiler_params=params(16),
        cost_estimate=pl.CostEstimate(flops=0, bytes_accessed=6_000_000, transcendentals=0),
        name="canvas",
    )(experts, owner, source, *after)


def outputs_kernel(per, columns, experts, owner, source, out, _, blocks, numbers, counts, sems):
    plan_slots(experts, owner, blocks, numbers, counts, per, columns)
    for wait in (False, True):
        for s in range(columns * CAP):
            held = blocks[s]

            @pl.when(held >= 0)
            def _():
                top, left = corner(held, experts.shape[1])
                target = out.at[pl.ds(top, BS), pl.ds(left, BS), :]
                move = copy(source.at[s // CAP, s % CAP, pl.ds(0, BS)], target, sems.at[s])
                if wait:
                    move.wait()
                else:
                    move.start()


def outputs_of(experts, owner, source, shape, per):
    columns = source.shape[0]
    return pl.pallas_call(
        functools.partial(outputs_kernel, per, columns),
        out_shape=[jax.ShapeDtypeStruct(shape, BF16), TOKEN],
        in_specs=[whole(pltpu.SMEM)] * 2 + [whole()],
        out_specs=[whole(pltpu.HBM)] * 2,
        scratch_shapes=tables(columns) + [pltpu.SemaphoreType.DMA((columns * CAP,))],
        compiler_params=params(16),
        cost_estimate=pl.CostEstimate(flops=0, bytes_accessed=3_000_000, transcendentals=0),
        name="outputs",
    )(experts, owner, source)


def finish_kernel(canvas, north, south, west, east, _, out):
    height, width, chans = out.shape
    stride = width + 2 * GAP
    column = lax.broadcasted_iota(jnp.int32, (BS, chans), 0)
    for r in range(height):
        start = (r + 1) * stride + GAP
        line = canvas[start : start + width, :]
        if r == 0:
            line = line + north[GAP : GAP + width, :].astype(F32)
        if r == height - 1:
            line = line + south[GAP : GAP + width, :].astype(F32)
        first = line[:BS] + jnp.where(column == 0, west[r : r + 1, :].astype(F32), 0.0)
        last = line[width - BS :] + jnp.where(
            column == BS - 1, east[r : r + 1, :].astype(F32), 0.0
        )
        out[r] = jnp.concatenate([first, line[BS : width - BS], last], axis=0).astype(BF16)


def finish(canvas, north, south, west, east, after, shape):
    return pl.pallas_call(
        finish_kernel,
        out_shape=jax.ShapeDtypeStruct(shape, BF16),
        in_specs=[whole()] * 5 + [whole(pltpu.HBM)],
        out_specs=whole(),
        compiler_params=params(16),
        cost_estimate=pl.CostEstimate(flops=0, bytes_accessed=4_000_000, transcendentals=0),
        name="finish",
    )(canvas, north, south, west, east, after)


def across(array, axis, shift, wrap):
    count = lax.axis_size(axis)
    pairs = [(i, i + shift) for i in range(count)]
    if wrap:
        pairs = [(i, j % count) for i, j in pairs]
    else:
        pairs = [(i, j) for i, j in pairs if 0 <= j < count]
    return lax.ppermute(array, axis, pairs)


def to_other_core(array):
    return lax.ppermute(array, "lat", [(i, i ^ 1) for i in range(lax.axis_size("lat"))])


def to_chip(array, shift):
    count = lax.axis_size("lat")
    return lax.ppermute(array, "lat", [(i, (i + 2 * shift) % count) for i in range(count)])


def swap(array, k):
    if k == 0:
        return array
    return lax.ppermute(array, "lon", [(i, i ^ k) for i in range(lax.axis_size("lon"))])


def exchange(array):
    return lax.all_to_all(array, "lon", split_axis=0, concat_axis=0, tiled=True)


def tied(arrays, others):
    return lax.optimization_barrier((arrays, others))[0]


def places_of(rings, chips, per):
    lat_index = lax.axis_index("lat")
    line, row = NUMBER // BS, NUMBER % BS
    numbers = jnp.concatenate([ring[:, line, row, 0] for ring in rings]).astype(jnp.int32)
    owner_lat = numbers // per
    chip_step = (owner_lat // 2 - lat_index // 2 + chips) % chips
    core_step = (owner_lat % 2 - lat_index % 2 + 2) % 2
    return (2 * chip_step + core_step) * per + numbers % per


def local(fields, cotangent, kernel_bank, block_expert, owner):
    columns = lax.axis_size("lon")
    chips = lax.axis_size("lat") // 2
    per = kernel_bank.shape[0]
    shape = kernel_bank.shape
    me = lax.axis_index("lon").astype(jnp.int32).reshape(1)

    north = across(fields[-1:], "lat", 1, False)
    south = across(fields[:1], "lat", -1, False)
    first, last = rims_of(
        north, south, fields[:, 0].astype(F32), fields[:, -1].astype(F32)
    )
    west = across(last, "lon", 1, True)
    east = across(first, "lon", -1, True)
    own = dispatch_own(block_expert, owner, fields, cotangent, per, columns)
    own = exchange(tied(own, (west, east)))

    rings = dispatch_rings(
        me, block_expert, owner, fields, north, south, west, east, per, columns
    )
    rings = [swap(array, k) for k, array in enumerate(rings)]
    stored = tied(kernel_bank, (west, east))
    banks = [kernel_bank, to_other_core(stored)]
    for k in range(1, chips):
        distant = tied(to_chip(stored, -k), rings[1 : columns // 2])
        banks += [distant, to_other_core(distant)]

    place = places_of(rings, chips, per)
    slots = (me, place, own, rings)

    results, taps_token = taps(*slots, banks, [])
    results = exchange(results)

    arrived, tokens = [], [taps_token]
    for k in range(1, chips):
        part, token = grads(*slots, 2 * k + 1, shape, [], tokens, BF16)
        part, token = grads(*slots, 2 * k, shape, [to_other_core(part)], [token], BF16)
        arrived.append(to_chip(part, k))
        tokens = [token]
    core_part, core_token = grads(*slots, 1, shape, [], tokens, BF16)
    own_part, own_token = grads(*slots, 0, shape, [], tokens, F32)
    arrived.append(to_other_core(core_part))

    canvas, top, bottom, left, right = canvas_of(
        block_expert, owner, results, [core_token, own_token], fields.shape, per
    )
    above = across(bottom, "lat", 1, False)
    below = across(top, "lat", -1, False)
    outputs, token = outputs_of(block_expert, owner, results, fields.shape, per)
    left, right = corners_of(above, below, left, right, token)
    from_west = across(right, "lon", 1, True)
    from_east = across(left, "lon", -1, True)
    grad_bank, token = bank_of([own_part] + arrived, shape)
    grad_fields = finish(canvas, above, below, from_west, from_east, token, fields.shape)
    return (outputs, grad_fields, grad_bank)


def solution(mesh):
    return jax.shard_map(
        local,
        mesh=mesh,
        in_specs=(
            P("lat", "lon", None),
            P("lat", "lon", None),
            P(("lat", "lon"), None, None, None),
            P("lat", "lon"),
            P(),
        ),
        out_specs=(
            P("lat", "lon", None),
            P("lat", "lon", None),
            P(("lat", "lon"), None, None, None),
        ),
        check_vma=False,
    )
```

time: 197 us -> 186 us (0.944)
  waiting for transfers between devices: 101 us -> 85.3 us
  starting transfers between devices: 33.5 us -> 43.7 us
  local copies, waits for them, and re-layouts: 9.99 us -> 5.33 us
  Pallas kernels: 50.7 us -> 48 us
    ppermute x0 -> x7, waiting for transfers between devices: none -> 33.7 us  [swap(): lax.ppermute(array, 'lon', [(i, i ^ k) for i in range(lax.axis_size('lon'...]
    all_to_all x2, waiting for transfers between devices: 65.1 us -> 34.8 us  [exchange(): return lax.all_to_all(array, 'lon', split_axis=0, concat_axis=0, tiled=True)]
    ppermute x2, waiting for transfers between devices: 31.1 us -> 7.84 us  [to_chip(): lax.ppermute(array, 'lat', [(i, (i + 2 * shift) % count) for i in range(c...]
    ppermute x0 -> x7, starting transfers between devices: none -> 9.96 us  [swap(): lax.ppermute(array, 'lon', [(i, i ^ k) for i in range(lax.axis_size('lon'...]
    unnamed x24 -> x34, local copies, waits for them, and re-layouts: 8.09 us -> 2.03 us
    ppermute x4, starting transfers between devices: 0.01 us -> 3.56 us  [to_other_core(): lax.ppermute(array, 'lat', [(i, i ^ 1) for i in range(lax.axis_size('lat'...]
    ppermute x8, waiting for transfers between devices: 4.59 us -> 8.09 us  [across(): return lax.ppermute(array, axis, pairs)]
    pallas_call x7 -> x12, Pallas kernels: 49.6 us -> 46.9 us  [the longest x4 19.2 us: grads(): pl.pallas_call(functools.partial(grads_kernel, piece, per, columns, len(a...]
  transfers between devices with their start and end apart: 16 -> 23, of which waited for: 5 -> 12; matrix products, arithmetic and copies ran while one was open for 1% -> 2% of each run, Pallas kernels for 25% -> 17%
where the time goes in v2:
time: 186 us; the launch traced here: 184 us
  waiting for transfers between devices  85.3 us (46%)
  Pallas kernels  48 us (26%)
  starting transfers between devices  43.7 us (23%)
  local copies, waits for them, and re-layouts  5.33 us (3%)
    all_to_all x2, waiting for transfers between devices, exchange(): return lax.all_to_all(array, 'lon', split_axis=0, concat_axis=0, tiled=True)  34.8 us
    ppermute x7, waiting for transfers between devices, swap(): lax.ppermute(array, 'lon', [(i, i ^ k) for i in range(lax.axis_size('lon'...  33.7 us
    pallas_call x4, Pallas kernels, grads(): pl.pallas_call(functools.partial(grads_kernel, piece, per, columns, len(a...  19.2 us
    ppermute x8, starting transfers between devices, across(): return lax.ppermute(array, axis, pairs)  15.8 us
    pallas_call x1, Pallas kernels, taps(): pl.pallas_call(functools.partial(taps_kernel, size, columns, len(banks),...  12.4 us
    ppermute x7, starting transfers between devices, swap(): lax.ppermute(array, 'lon', [(i, i ^ k) for i in range(lax.axis_size('lon'...  9.96 us
    all_to_all x2, starting transfers between devices, exchange(): return lax.all_to_all(array, 'lon', split_axis=0, concat_axis=0, tiled=True)  9.56 us
    ppermute x8, waiting for transfers between devices, across(): return lax.ppermute(array, axis, pairs)  8.09 us
  transfers between devices with their start and end apart: 23, of which 12 were waited for; matrix products, arithmetic and copies ran while one was open for 2% of the time, Pallas kernels for 17%

profile of v2, /device:TPU:0, one launch (start us, length us, event | category | flops | bytes accessed | tf_op | source)
XLA Modules:
  0.0 183.8 jit_solution(16676456094239777878)
XLA Ops:
  1.4 2.3 %collective-permute-start = (bf16[1,128,128]{2,1,0:T(8,128)(2,1)S(1)}, bf16[1,128,128]{2,1,0:T(8,128)(2,1)S(1)}, u32[]{:S(2)}, u32[]{:S(2)}) collective-permute-start(bf16[1,128,128]{2,1,0:T(8,128)(2,1)S(1)} %get-tuple-element.74), channel_id=1, source_target_pairs={{0,8},{8,16},{16,24},{1,9},{9,17},{17,25},{2,10},{10,18},{18,26},{... | collective-permute-start | bytes 98312 | tf_op jit(solution)/shard_map/ppermute | solution.py:703
  6.0 3.0 %collective-permute-done.1.south = bf16[1,128,128]{2,1,0:T(8,128)(2,1)S(1)} collective-permute-done((bf16[1,128,128]{2,1,0:T(8,128)(2,1)S(1)}, bf16[1,128,128]{2,1,0:T(8,128)(2,1)S(1)}, u32[]{:S(2)}, u32[]{:S(2)}) %collective-permute-start.1) | collective-permute-done | bytes 32800 | tf_op jit(solution)/shard_map/ppermute | solution.py:703
  9.0 1.6 collective-permute-start.2
  10.6 3.2 %collective-permute-start.3 = (bf16[34,128]{1,0:T(8,128)(2,1)S(1)}, bf16[34,128]{1,0:T(8,128)(2,1)S(1)}, u32[]{:S(2)}, u32[]{:S(2)}) collective-permute-start(bf16[34,128]{1,0:T(8,128)(2,1)S(1)} %get-tuple-element.38), channel_id=1, source_target_pairs={{0,7},{1,0},{2,1},{3,2},{4,3},{5,4},{6,5},{7,6},{8,15},{9,8},{10,9... | collective-permute-start | bytes 26120 | tf_op jit(solution)/shard_map/ppermute | solution.py:703
  13.8 1.6 collective-permute-done.2.west
  15.4 2.6 %collective-permute-start.12 = (bf16[8,9,128,128]{3,2,1,0:T(8,128)(2,1)}, bf16[8,9,128,128]{3,2,1,0:T(8,128)(2,1)}, u32[]{:S(2)}, u32[]{:S(2)}) collective-permute-start(bf16[8,9,128,128]{3,2,1,0:T(8,128)(2,1)} %refs_8_.1), channel_id=1, source_target_pairs={{0,16},{8,24},{16,0},{24,8},{1,17},{9,25},{17,1},{25,9},{2,18},{10... | collective-permute-start | bytes 7077896 | tf_op jit(solution)/shard_map/ppermute | solution.py:712
  18.0 3.5 %dispatch_own.1 = bf16[8,2,32,16,128]{4,3,2,1,0:T(8,128)(2,1)} custom-call(s32[2,8]{1,0:T(2,128)} %experts.7, s32[256]{0:T(256)} %owner.7, bf16[32,128,128]{2,1,0:T(8,128)(2,1)} %fields.3, bf16[32,128,128]{2,1,0:T(8,128)(2,1)} %cot.1), custom_call_target="tpu_custom_call" | custom-call | bytes 6000000 | tf_op jit(solution)/shard_map/dispatch_own/pallas_call | solution.py:120
  21.6 5.9 %all-to-all-start = ((bf16[8,2,32,16,128]{4,3,2,1,0:T(8,128)(2,1)}), bf16[8,2,32,16,128]{4,3,2,1,0:T(8,128)(2,1)S(1)}, u32[]{:S(2)}, u32[]{:S(2)}) async-start(bf16[8,2,32,16,128]{4,3,2,1,0:T(8,128)(2,1)} %dispatch_own.1), calls=%async_computation | async-start | bytes 4194304 | tf_op jit(solution)/shard_map/all_to_all | solution.py:722
  27.5 3.2 %dispatch_rings.1 = (bf16[2,5,16,128]{3,2,1,0:T(8,128)(2,1)}, bf16[2,5,16,128]{3,2,1,0:T(8,128)(2,1)}, bf16[2,5,16,128]{3,2,1,0:T(8,128)(2,1)}, bf16[2,5,16,128]...) custom-call(s32[1]{0:T(128)} %bitcast.me, ...), custom_call_target="tpu_custom_call" | custom-call | bytes 3000000 | tf_op jit(solution)/shard_map/dispatch_rings/pallas_call | solution.py:247
  30.8 2.1 %collective-permute-start.4 = (bf16[2,5,16,128]{3,2,1,0:T(8,128)(2,1)}, bf16[2,5,16,128]{3,2,1,0:T(8,128)(2,1)S(1)}, u32[]{:S(2)}, u32[]{:S(2)}) collective-permute-start(bf16[2,5,16,128]{3,2,1,0:T(8,128)(2,1)} %get-tuple-element.40), channel_id=1, source_target_pairs={{0,1},{1,0},{2,3},{3,2},{4,5},{5,4},{6,7},{7,6},{8,9},{9,8},{10,11... | collective-permute-start | bytes 122888 | tf_op jit(solution)/shard_map/ppermute | solution.py:718
  34.4 11.3 %collective-permute-done.4.refs_1_ = bf16[2,5,16,128]{3,2,1,0:T(8,128)(2,1)S(1)} collective-permute-done((bf16[2,5,16,128]{3,2,1,0:T(8,128)(2,1)}, bf16[2,5,16,128]{3,2,1,0:T(8,128)(2,1)S(1)}, u32[]{:S(2)}, u32[]{:S(2)}) %collective-permute-start.4) | collective-permute-done | bytes 40992 | tf_op jit(solution)/shard_map/ppermute | solution.py:718
  45.7 16.3 %collective-permute-done.5.refs_2_ = bf16[2,5,16,128]{3,2,1,0:T(8,128)(2,1)S(1)} collective-permute-done((bf16[2,5,16,128]{3,2,1,0:T(8,128)(2,1)}, bf16[2,5,16,128]{3,2,1,0:T(8,128)(2,1)S(1)}, u32[]{:S(2)}, u32[]{:S(2)}) %collective-permute-start.5) | collective-permute-done | bytes 40992 | tf_op jit(solution)/shard_map/ppermute | solution.py:718
  62.4 7.8 %collective-permute-done.12.refs_10_ = bf16[8,9,128,128]{3,2,1,0:T(8,128)(2,1)} collective-permute-done((bf16[8,9,128,128]{3,2,1,0:T(8,128)(2,1)}, bf16[8,9,128,128]{3,2,1,0:T(8,128)(2,1)}, u32[]{:S(2)}, u32[]{:S(2)}) %collective-permute-start.12) | collective-permute-done | bytes 2359328 | tf_op jit(solution)/shard_map/ppermute | solution.py:712
  70.4 4.6 %collective-permute-start.10 = (bf16[2,5,16,128]{3,2,1,0:T(8,128)(2,1)}, bf16[2,5,16,128]{3,2,1,0:T(8,128)(2,1)S(1)}, u32[]{:S(2)}, u32[]{:S(2)}) collective-permute-start(bf16[2,5,16,128]{3,2,1,0:T(8,128)(2,1)} %get-tuple-element.46), channel_id=1, source_target_pairs={{0,7},{1,6},{2,5},{3,4},{4,3},{5,2},{6,1},{7,0},{8,15},{9,14},{10,... | collective-permute-start | bytes 122888 | tf_op jit(solution)/shard_map/ppermute | solution.py:718
  77.5 1.7 collective-permute-start.7
  79.4 1.9 %collective-permute-done.9.refs_6_ = bf16[2,5,16,128]{3,2,1,0:T(8,128)(2,1)S(1)} collective-permute-done((bf16[2,5,16,128]{3,2,1,0:T(8,128)(2,1)}, bf16[2,5,16,128]{3,2,1,0:T(8,128)(2,1)S(1)}, u32[]{:S(2)}, u32[]{:S(2)}) %collective-permute-start.9) | collective-permute-done | bytes 40992 | tf_op jit(solution)/shard_map/ppermute | solution.py:718
  81.4 2.3 %collective-permute-done.7.refs_4_ = bf16[2,5,16,128]{3,2,1,0:T(8,128)(2,1)S(1)} collective-permute-done((bf16[2,5,16,128]{3,2,1,0:T(8,128)(2,1)}, bf16[2,5,16,128]{3,2,1,0:T(8,128)(2,1)S(1)}, u32[]{:S(2)}, u32[]{:S(2)}) %collective-permute-start.7) | collective-permute-done | bytes 40992 | tf_op jit(solution)/shard_map/ppermute | solution.py:718
  85.9 12.4 %taps.1 = (bf16[8,2,37,16,128]{4,3,2,1,0:T(8,128)(2,1)}, f32[8,128]{1,0:T(8,128)}) custom-call(s32[1]{0:T(128)} %bitcast.me, s32[16]{0:T(128)} %fusion.3.place, bf16[8,2,32,16,128]{4,3,2,1,0:T(8,128)(2,1)} %copy-done.7, bf16[2,5,16,128]{3,2,1,0:T(8,128)(2,1)} %get-tuple-element.39.refs_0_, bf16[2,5,16,128]{3,2,1,0:T(8,128)(2,1)} %copy-done.8, ...), custom_call_target="tpu_custom_call" | custom-call | flops 2800000000 | bytes 9600000 | tf_op jit(solution)/shard_map/taps/pallas_call | solution.py:390
  98.3 2.7 %grads.4 = (bf16[8,128,1152]{2,1,0:T(8,128)(2,1)}, f32[8,128]{1,0:T(8,128)}) custom-call(s32[1]{0:T(128)} %bitcast.me, s32[16]{0:T(128)} %fusion.3.place, bf16[8,2,32,16,128]{4,3,2,1,0:T(8,128)(2,1)} %copy-done.7, bf16[2,5,16,128]{3,2,1,0:T(8,128)(2,1)} %get-tuple-element.39.refs_0_, bf16[2,5,16,128]{3,2,1,0:T(8,128)(2,1)} %copy-done.8, ...), custom_call_target="tpu_custom_call" | custom-call | flops 300000000 | bytes 6000000 | tf_op jit(solution)/shard_map/grads/pallas_call | solution.py:500
  101.1 2.1 %collective-permute-start.14 = (bf16[8,128,1152]{2,1,0:T(8,128)(2,1)}, bf16[8,128,1152]{2,1,0:T(8,128)(2,1)}, u32[]{:S(2)}, u32[]{:S(2)}) collective-permute-start(bf16[8,128,1152]{2,1,0:T(8,128)(2,1)} %get-tuple-element.53), channel_id=1, source_target_pairs={{0,8},{8,0},{16,24},{24,16},{1,9},{9,1},{17,25},{25,17},{2,10},{10... | collective-permute-start | bytes 7077896 | tf_op jit(solution)/shard_map/ppermute | solution.py:707
  103.1 3.6 %all-to-all-start.1 = ((bf16[8,2,37,16,128]{4,3,2,1,0:T(8,128)(2,1)}), bf16[8,2,37,16,128]{4,3,2,1,0:T(8,128)(2,1)S(1)}, u32[]{:S(2)}, u32[]{:S(2)}) async-start(bf16[8,2,37,16,128]{4,3,2,1,0:T(8,128)(2,1)} %get-tuple-element.50), calls=%async_computation.1 | async-start | bytes 4849664 | tf_op jit(solution)/shard_map/all_to_all | solution.py:722
  107.6 4.2 %grads.5 = (bf16[8,128,1152]{2,1,0:T(8,128)(2,1)}, f32[8,128]{1,0:T(8,128)}) custom-call(s32[1]{0:T(128)} %bitcast.me, s32[16]{0:T(128)} %fusion.3.place, bf16[8,2,32,16,128]{4,3,2,1,0:T(8,128)(2,1)} %copy-done.7, bf16[2,5,16,128]{3,2,1,0:T(8,128)(2,1)} %get-tuple-element.39.refs_0_, bf16[2,5,16,128]{3,2,1,0:T(8,128)(2,1)} %copy-done.8, ...), custom_call_target="tpu_custom_call" | custom-call | flops 300000000 | bytes 6000000 | tf_op jit(solution)/shard_map/grads/pallas_call | solution.py:500
  111.9 5.2 %grads.6 = (bf16[8,128,1152]{2,1,0:T(8,128)(2,1)}, f32[8,128]{1,0:T(8,128)}) custom-call(s32[1]{0:T(128)} %bitcast.me, s32[16]{0:T(128)} %fusion.3.place, bf16[8,2,32,16,128]{4,3,2,1,0:T(8,128)(2,1)} %copy-done.7, bf16[2,5,16,128]{3,2,1,0:T(8,128)(2,1)} %get-tuple-element.39.refs_0_, bf16[2,5,16,128]{3,2,1,0:T(8,128)(2,1)} %copy-done.8, ...), custom_call_target="tpu_custom_call" | custom-call | flops 300000000 | bytes 6000000 | tf_op jit(solution)/shard_map/grads/pallas_call | solution.py:500
  118.5 2.2 %collective-permute-start.19 = (bf16[8,128,1152]{2,1,0:T(8,128)(2,1)}, bf16[8,128,1152]{2,1,0:T(8,128)(2,1)}, u32[]{:S(2)}, u32[]{:S(2)}) collective-permute-start(bf16[8,128,1152]{2,1,0:T(8,128)(2,1)} %get-tuple-element.67), channel_id=1, source_target_pairs={{0,16},{8,24},{16,0},{24,8},{1,17},{9,25},{17,1},{25,9},{2,18},{10... | collective-permute-start | bytes 7077896 | tf_op jit(solution)/shard_map/ppermute | solution.py:712
  120.7 7.1 %grads.7 = (f32[8,128,1152]{2,1,0:T(8,128)}, f32[8,128]{1,0:T(8,128)}) custom-call(s32[1]{0:T(128)} %bitcast.me, s32[16]{0:T(128)} %fusion.3.place, bf16[8,2,32,16,128]{4,3,2,1,0:T(8,128)(2,1)} %copy-done.7, bf16[2,5,16,128]{3,2,1,0:T(8,128)(2,1)} %get-tuple-element.39.refs_0_, bf16[2,5,16,128]{3,2,1,0:T(8,128)(2,1)} %copy-done.8, ...), custom_call_target="tpu_custom_call" | custom-call | flops 300000000 | bytes 6000000 | tf_op jit(solution)/shard_map/grads/pallas_call | solution.py:500
  127.8 34.8 %all-to-all-done.1.source = bf16[8,2,37,16,128]{4,3,2,1,0:T(8,128)(2,1)S(1)} async-done(((bf16[8,2,37,16,128]{4,3,2,1,0:T(8,128)(2,1)}), bf16[8,2,37,16,128]{4,3,2,1,0:T(8,128)(2,1)S(1)}, u32[]{:S(2)}, u32[]{:S(2)}) %all-to-all-start.1) | async-done | bytes 2424864 | tf_op jit(solution)/shard_map/all_to_all | solution.py:722
  163.3 2.0 %canvas.1 = (f32[4896,128]{1,0:T(8,128)S(1)}, bf16[144,128]{1,0:T(8,128)(2,1)S(1)}, bf16[144,128]{1,0:T(8,128)(2,1)S(1)}, f32[32,128]{1,0:T(8,128)S(1)}, f32[32,128]{1,0:T(8,128)S(1)}) custom-call(s32[2,8]{1,0:T(2,128)S(1)} %copy-done.3, s32[256]{0:T(256)S(1)} %copy-done.4, bf16[8,2,37,16,128]{4,3,2,1,0:T(8,128)(2,1)S(1)} %all-to-all-done.1.source, ...), custom_call_target="tpu_custom_call" | custom-call | bytes 6000000 | tf_op jit(solution)/shard_map/canvas/pallas_call | solution.py:615
  167.9 2.2 %outputs.1 = (bf16[32,128,128]{2,1,0:T(8,128)(2,1)}, f32[8,128]{1,0:T(8,128)S(1)}) custom-call(s32[2,8]{1,0:T(2,128)S(1)} %copy-done.3, s32[256]{0:T(256)S(1)} %copy-done.4, bf16[8,2,37,16,128]{4,3,2,1,0:T(8,128)(2,1)S(1)} %all-to-all-done.1.source), custom_call_target="tpu_custom_call" | custom-call | bytes 3000000 | tf_op jit(solution)/shard_map/outputs/pallas_call | solution.py:654
  170.2 3.5 %collective-permute-done.16.below.south = bf16[144,128]{1,0:T(8,128)(2,1)S(1)} collective-permute-done((bf16[144,128]{1,0:T(8,128)(2,1)S(1)}, bf16[144,128]{1,0:T(8,128)(2,1)S(1)}, u32[]{:S(2)}, u32[]{:S(2)}) %collective-permute-start.16) | collective-permute-done | bytes 36896 | tf_op jit(solution)/shard_map/ppermute | solution.py:703
  173.7 1.5 collective-permute-start.17
  175.2 3.3 %collective-permute-start.18 = (bf16[32,128]{1,0:T(8,128)(2,1)S(1)}, bf16[32,128]{1,0:T(8,128)(2,1)S(1)}, u32[]{:S(2)}, u32[]{:S(2)}) collective-permute-start(bf16[32,128]{1,0:T(8,128)(2,1)S(1)} %get-tuple-element.65), channel_id=1, source_target_pairs={{0,7},{1,0},{2,1},{3,2},{4,3},{5,4},{6,5},{7,6},{8,15},{9,8},{10,9... | collective-permute-start | bytes 24584 | tf_op jit(solution)/shard_map/ppermute | solution.py:703
  178.4 4.2 %bank.1 = (f32[8,9,128,128]{3,2,1,0:T(8,128)}, f32[8,128]{1,0:T(8,128)S(1)}) custom-call(f32[8,128,1152]{2,1,0:T(8,128)S(1)} %copy-done, bf16[8,128,1152]{2,1,0:T(8,128)(2,1)} %collective-permute-done.19.refs_1_, bf16[8,128,1152]{2,1,0:T(8,128)(2,1)} %collective-permute-done.20.refs_2_), custom_call_target="tpu_custom_call" | custom-call | bytes 12000000 | tf_op jit(solution)/shard_map/bank/pallas_call | solution.py:554
  (74 shorter events, 16.7 us)
Async XLA Ops:
  1.4 4.6 %collective-permute-start = (bf16[1,128,128]{2,1,0:T(8,128)(2,1)S(1)}, bf16[1,128,128]{2,1,0:T(8,128)(2,1)S(1)}, u32[]{:S(2)}, u32[]{:S(2)}) collective-permute-start(bf16[1,128,128]{2,1,0:T(8,128)(2,1)S(1)} %get-tuple-element.74), channel_id=1, source_target_pairs={{0,8},{8,16},{16,24},{1,9},{9,17},{17,25},{2,10},{10,18},{18,26},{... | collective-permute-start | bytes 98312 | tf_op jit(solution)/shard_map/ppermute | solution.py:703
  3.8 5.2 %collective-permute-start.1 = (bf16[1,128,128]{2,1,0:T(8,128)(2,1)S(1)}, bf16[1,128,128]{2,1,0:T(8,128)(2,1)S(1)}, u32[]{:S(2)}, u32[]{:S(2)}) collective-permute-start(bf16[1,128,128]{2,1,0:T(8,128)(2,1)S(1)} %get-tuple-element.73), channel_id=1, source_target_pairs={{8,0},{16,8},{24,16},{9,1},{17,9},{25,17},{10,2},{18,10},{26,18},{... | collective-permute-start | bytes 98312 | tf_op jit(solution)/shard_map/ppermute | solution.py:703
  6.0 15.5 %copy-start.1 = (bf16[1,128,128]{2,1,0:T(8,128)(2,1)}, bf16[1,128,128]{2,1,0:T(8,128)(2,1)S(1)}, u32[]{:S(2)}) copy-start(bf16[1,128,128]{2,1,0:T(8,128)(2,1)S(1)} %collective-permute-done.north) | copy-start | bytes 98308
  9.0 12.6 %copy-start.2 = (bf16[1,128,128]{2,1,0:T(8,128)(2,1)}, bf16[1,128,128]{2,1,0:T(8,128)(2,1)S(1)}, u32[]{:S(2)}) copy-start(bf16[1,128,128]{2,1,0:T(8,128)(2,1)S(1)} %collective-permute-done.1.south) | copy-start | bytes 98308
  9.0 6.4 %collective-permute-start.2 = (bf16[34,128]{1,0:T(8,128)(2,1)S(1)}, bf16[34,128]{1,0:T(8,128)(2,1)S(1)}, u32[]{:S(2)}, u32[]{:S(2)}) collective-permute-start(bf16[34,128]{1,0:T(8,128)(2,1)S(1)} %get-tuple-element.37), channel_id=1, source_target_pairs={{0,1},{1,2},{2,3},{3,4},{4,5},{5,6},{6,7},{7,0},{8,9},{9,10},{10,1... | collective-permute-start | bytes 26120 | tf_op jit(solution)/shard_map/ppermute | solution.py:703
  10.6 4.9 %collective-permute-start.3 = (bf16[34,128]{1,0:T(8,128)(2,1)S(1)}, bf16[34,128]{1,0:T(8,128)(2,1)S(1)}, u32[]{:S(2)}, u32[]{:S(2)}) collective-permute-start(bf16[34,128]{1,0:T(8,128)(2,1)S(1)} %get-tuple-element.38), channel_id=1, source_target_pairs={{0,7},{1,0},{2,1},{3,2},{4,3},{5,4},{6,5},{7,6},{8,15},{9,8},{10,9... | collective-permute-start | bytes 26120 | tf_op jit(solution)/shard_map/ppermute | solution.py:703
  15.4 54.9 %collective-permute-start.12 = (bf16[8,9,128,128]{3,2,1,0:T(8,128)(2,1)}, bf16[8,9,128,128]{3,2,1,0:T(8,128)(2,1)}, u32[]{:S(2)}, u32[]{:S(2)}) collective-permute-start(bf16[8,9,128,128]{3,2,1,0:T(8,128)(2,1)} %refs_8_.1), channel_id=1, source_target_pairs={{0,16},{8,24},{16,0},{24,8},{1,17},{9,25},{17,1},{25,9},{2,18},{10... | collective-permute-start | bytes 7077896 | tf_op jit(solution)/shard_map/ppermute | solution.py:712
  21.6 63.0 %all-to-all-start = ((bf16[8,2,32,16,128]{4,3,2,1,0:T(8,128)(2,1)}), bf16[8,2,32,16,128]{4,3,2,1,0:T(8,128)(2,1)S(1)}, u32[]{:S(2)}, u32[]{:S(2)}) async-start(bf16[8,2,32,16,128]{4,3,2,1,0:T(8,128)(2,1)} %dispatch_own.1), calls=%async_computation | async-start | bytes 4194304 | tf_op jit(solution)/shard_map/all_to_all | solution.py:722
  30.8 15.0 %collective-permute-start.4 = (bf16[2,5,16,128]{3,2,1,0:T(8,128)(2,1)}, bf16[2,5,16,128]{3,2,1,0:T(8,128)(2,1)S(1)}, u32[]{:S(2)}, u32[]{:S(2)}) collective-permute-start(bf16[2,5,16,128]{3,2,1,0:T(8,128)(2,1)} %get-tuple-element.40), channel_id=1, source_target_pairs={{0,1},{1,0},{2,3},{3,2},{4,5},{5,4},{6,7},{7,6},{8,9},{9,8},{10,11... | collective-permute-start | bytes 122888 | tf_op jit(solution)/shard_map/ppermute | solution.py:718
  32.8 29.2 %collective-permute-start.5 = (bf16[2,5,16,128]{3,2,1,0:T(8,128)(2,1)}, bf16[2,5,16,128]{3,2,1,0:T(8,128)(2,1)S(1)}, u32[]{:S(2)}, u32[]{:S(2)}) collective-permute-start(bf16[2,5,16,128]{3,2,1,0:T(8,128)(2,1)} %get-tuple-element.41), channel_id=1, source_target_pairs={{0,2},{1,3},{2,0},{3,1},{4,6},{5,7},{6,4},{7,5},{8,10},{9,11},{10,... | collective-permute-start | bytes 122888 | tf_op jit(solution)/shard_map/ppermute | solution.py:718
  34.3 28.1 %collective-permute-start.6 = (bf16[2,5,16,128]{3,2,1,0:T(8,128)(2,1)}, bf16[2,5,16,128]{3,2,1,0:T(8,128)(2,1)S(1)}, u32[]{:S(2)}, u32[]{:S(2)}) collective-permute-start(bf16[2,5,16,128]{3,2,1,0:T(8,128)(2,1)} %get-tuple-element.42), channel_id=1, source_target_pairs={{0,3},{1,2},{2,1},{3,0},{4,7},{5,6},{6,5},{7,4},{8,11},{9,10},{10,... | collective-permute-start | bytes 122888 | tf_op jit(solution)/shard_map/ppermute | solution.py:718
  34.4 50.1 %collective-permute-start.11 = (bf16[8,9,128,128]{3,2,1,0:T(8,128)(2,1)}, bf16[8,9,128,128]{3,2,1,0:T(8,128)(2,1)}, u32[]{:S(2)}, u32[]{:S(2)}) collective-permute-start(bf16[8,9,128,128]{3,2,1,0:T(8,128)(2,1)} %refs_8_.1), channel_id=1, source_target_pairs={{0,8},{8,0},{16,24},{24,16},{1,9},{9,1},{17,25},{25,17},{2,10},{10... | collective-permute-start | bytes 7077896 | tf_op jit(solution)/shard_map/ppermute | solution.py:707
  45.7 38.8 %copy-start.8 = (bf16[2,5,16,128]{3,2,1,0:T(8,128)(2,1)}, bf16[2,5,16,128]{3,2,1,0:T(8,128)(2,1)S(1)}, u32[]{:S(2)}) copy-start(bf16[2,5,16,128]{3,2,1,0:T(8,128)(2,1)S(1)} %collective-permute-done.4.refs_1_) | copy-start | bytes 122884
  62.0 22.5 %copy-start.9 = (bf16[2,5,16,128]{3,2,1,0:T(8,128)(2,1)}, bf16[2,5,16,128]{3,2,1,0:T(8,128)(2,1)S(1)}, u32[]{:S(2)}) copy-start(bf16[2,5,16,128]{3,2,1,0:T(8,128)(2,1)S(1)} %collective-permute-done.5.refs_2_) | copy-start | bytes 122884
  62.4 22.1 %copy-start.10 = (bf16[2,5,16,128]{3,2,1,0:T(8,128)(2,1)}, bf16[2,5,16,128]{3,2,1,0:T(8,128)(2,1)S(1)}, u32[]{:S(2)}) copy-start(bf16[2,5,16,128]{3,2,1,0:T(8,128)(2,1)S(1)} %collective-permute-done.6.refs_3_) | copy-start | bytes 122884
  70.3 14.2 %collective-permute-start.13 = (bf16[8,9,128,128]{3,2,1,0:T(8,128)(2,1)}, bf16[8,9,128,128]{3,2,1,0:T(8,128)(2,1)}, u32[]{:S(2)}, u32[]{:S(2)}) collective-permute-start(bf16[8,9,128,128]{3,2,1,0:T(8,128)(2,1)} %collective-permute-done.12.refs_10_), channel_id=1, source_target_pairs={{0,8},{8,0},{16,24},{24,16},{1,9},{9,1},{17,25},{25,17},{2,10},{10... | collective-permute-start | bytes 7077896 | tf_op jit(solution)/shard_map/ppermute | solution.py:707
  70.4 7.1 %collective-permute-start.10 = (bf16[2,5,16,128]{3,2,1,0:T(8,128)(2,1)}, bf16[2,5,16,128]{3,2,1,0:T(8,128)(2,1)S(1)}, u32[]{:S(2)}, u32[]{:S(2)}) collective-permute-start(bf16[2,5,16,128]{3,2,1,0:T(8,128)(2,1)} %get-tuple-element.46), channel_id=1, source_target_pairs={{0,7},{1,6},{2,5},{3,4},{4,3},{5,2},{6,1},{7,0},{8,15},{9,14},{10,... | collective-permute-start | bytes 122888 | tf_op jit(solution)/shard_map/ppermute | solution.py:718
  75.0 6.2 %collective-permute-start.9 = (bf16[2,5,16,128]{3,2,1,0:T(8,128)(2,1)}, bf16[2,5,16,128]{3,2,1,0:T(8,128)(2,1)S(1)}, u32[]{:S(2)}, u32[]{:S(2)}) collective-permute-start(bf16[2,5,16,128]{3,2,1,0:T(8,128)(2,1)} %get-tuple-element.45), channel_id=1, source_target_pairs={{0,6},{1,7},{2,4},{3,5},{4,2},{5,3},{6,0},{7,1},{8,14},{9,15},{10,... | collective-permute-start | bytes 122888 | tf_op jit(solution)/shard_map/ppermute | solution.py:718
  75.0 6.3 %collective-permute-start.8 = (bf16[2,5,16,128]{3,2,1,0:T(8,128)(2,1)}, bf16[2,5,16,128]{3,2,1,0:T(8,128)(2,1)S(1)}, u32[]{:S(2)}, u32[]{:S(2)}) collective-permute-start(bf16[2,5,16,128]{3,2,1,0:T(8,128)(2,1)} %get-tuple-element.44), channel_id=1, source_target_pairs={{0,5},{1,4},{2,7},{3,6},{4,1},{5,0},{6,3},{7,2},{8,13},{9,12},{10,... | collective-permute-start | bytes 122888 | tf_op jit(solution)/shard_map/ppermute | solution.py:718
  77.5 6.2 %collective-permute-start.7 = (bf16[2,5,16,128]{3,2,1,0:T(8,128)(2,1)}, bf16[2,5,16,128]{3,2,1,0:T(8,128)(2,1)S(1)}, u32[]{:S(2)}, u32[]{:S(2)}) collective-permute-start(bf16[2,5,16,128]{3,2,1,0:T(8,128)(2,1)} %get-tuple-element.43), channel_id=1, source_target_pairs={{0,4},{1,5},{2,6},{3,7},{4,0},{5,1},{6,2},{7,3},{8,12},{9,13},{10,... | collective-permute-start | bytes 122888 | tf_op jit(solution)/shard_map/ppermute | solution.py:718
  101.1 6.6 %collective-permute-start.14 = (bf16[8,128,1152]{2,1,0:T(8,128)(2,1)}, bf16[8,128,1152]{2,1,0:T(8,128)(2,1)}, u32[]{:S(2)}, u32[]{:S(2)}) collective-permute-start(bf16[8,128,1152]{2,1,0:T(8,128)(2,1)} %get-tuple-element.53), channel_id=1, source_target_pairs={{0,8},{8,0},{16,24},{24,16},{1,9},{9,1},{17,25},{25,17},{2,10},{10... | collective-permute-start | bytes 7077896 | tf_op jit(solution)/shard_map/ppermute | solution.py:707
  103.1 59.5 %all-to-all-start.1 = ((bf16[8,2,37,16,128]{4,3,2,1,0:T(8,128)(2,1)}), bf16[8,2,37,16,128]{4,3,2,1,0:T(8,128)(2,1)S(1)}, u32[]{:S(2)}, u32[]{:S(2)}) async-start(bf16[8,2,37,16,128]{4,3,2,1,0:T(8,128)(2,1)} %get-tuple-element.50), calls=%async_computation.1 | async-start | bytes 4849664 | tf_op jit(solution)/shard_map/all_to_all | solution.py:722
  111.8 50.8 %copy-start.3 = (s32[2,8]{1,0:T(2,128)S(1)}, s32[2,8]{1,0:T(2,128)}, u32[]{:S(2)}) copy-start(s32[2,8]{1,0:T(2,128)} %experts.7) | copy-start | bytes 196
  111.8 50.8 %copy-start.4 = (s32[256]{0:T(256)S(1)}, s32[256]{0:T(256)}, u32[]{:S(2)}) copy-start(s32[256]{0:T(256)} %owner.7) | copy-start | bytes 3076
  117.1 45.6 %copy-start.5 = (f32[8,128]{1,0:T(8,128)S(1)}, f32[8,128]{1,0:T(8,128)}, u32[]{:S(2)}) copy-start(f32[8,128]{1,0:T(8,128)} %get-tuple-element.56.refs_0_) | copy-start | bytes 12292
  117.1 61.4 %collective-permute-start.20 = (bf16[8,128,1152]{2,1,0:T(8,128)(2,1)}, bf16[8,128,1152]{2,1,0:T(8,128)(2,1)}, u32[]{:S(2)}, u32[]{:S(2)}) collective-permute-start(bf16[8,128,1152]{2,1,0:T(8,128)(2,1)} %get-tuple-element.68), channel_id=1, source_target_pairs={{0,8},{8,0},{16,24},{24,16},{1,9},{9,1},{17,25},{25,17},{2,10},{10... | collective-permute-start | bytes 7077896 | tf_op jit(solution)/shard_map/ppermute | solution.py:707
  118.5 60.0 %collective-permute-start.19 = (bf16[8,128,1152]{2,1,0:T(8,128)(2,1)}, bf16[8,128,1152]{2,1,0:T(8,128)(2,1)}, u32[]{:S(2)}, u32[]{:S(2)}) collective-permute-start(bf16[8,128,1152]{2,1,0:T(8,128)(2,1)} %get-tuple-element.67), channel_id=1, source_target_pairs={{0,16},{8,24},{16,0},{24,8},{1,17},{9,25},{17,1},{25,9},{2,18},{10... | collective-permute-start | bytes 7077896 | tf_op jit(solution)/shard_map/ppermute | solution.py:712
  163.3 15.1 %copy-start = (f32[8,128,1152]{2,1,0:T(8,128)S(1)}, f32[8,128,1152]{2,1,0:T(8,128)}, u32[]{:S(2)}) copy-start(f32[8,128,1152]{2,1,0:T(8,128)} %get-tuple-element.66.refs_0_) | copy-start | bytes 14155780
  165.3 4.8 %collective-permute-start.15 = (bf16[144,128]{1,0:T(8,128)(2,1)S(1)}, bf16[144,128]{1,0:T(8,128)(2,1)S(1)}, u32[]{:S(2)}, u32[]{:S(2)}) collective-permute-start(bf16[144,128]{1,0:T(8,128)(2,1)S(1)} %get-tuple-element.59), channel_id=1, source_target_pairs={{0,8},{8,16},{16,24},{1,9},{9,17},{17,25},{2,10},{10,18},{18,26},{... | collective-permute-start | bytes 110600 | tf_op jit(solution)/shard_map/ppermute | solution.py:703
  166.6 7.0 %collective-permute-start.16 = (bf16[144,128]{1,0:T(8,128)(2,1)S(1)}, bf16[144,128]{1,0:T(8,128)(2,1)S(1)}, u32[]{:S(2)}, u32[]{:S(2)}) collective-permute-start(bf16[144,128]{1,0:T(8,128)(2,1)S(1)} %get-tuple-element.60), channel_id=1, source_target_pairs={{8,0},{16,8},{24,16},{9,1},{17,9},{25,17},{10,2},{18,10},{26,18},{... | collective-permute-start | bytes 110600 | tf_op jit(solution)/shard_map/ppermute | solution.py:703
  173.7 9.0 %collective-permute-start.17 = (bf16[32,128]{1,0:T(8,128)(2,1)S(1)}, bf16[32,128]{1,0:T(8,128)(2,1)S(1)}, u32[]{:S(2)}, u32[]{:S(2)}) collective-permute-start(bf16[32,128]{1,0:T(8,128)(2,1)S(1)} %get-tuple-element.64), channel_id=1, source_target_pairs={{0,1},{1,2},{2,3},{3,4},{4,5},{5,6},{6,7},{7,0},{8,9},{9,10},{10,1... | collective-permute-start | bytes 24584 | tf_op jit(solution)/shard_map/ppermute | solution.py:703
  175.2 7.5 %collective-permute-start.18 = (bf16[32,128]{1,0:T(8,128)(2,1)S(1)}, bf16[32,128]{1,0:T(8,128)(2,1)S(1)}, u32[]{:S(2)}, u32[]{:S(2)}) collective-permute-start(bf16[32,128]{1,0:T(8,128)(2,1)S(1)} %get-tuple-element.65), channel_id=1, source_target_pairs={{0,7},{1,0},{2,1},{3,2},{4,3},{5,4},{6,5},{7,6},{8,15},{9,8},{10,9... | collective-permute-start | bytes 24584 | tf_op jit(solution)/shard_map/ppermute | solution.py:703
  (8 other events, 28.8 us)

commit v3 on v2

--- a/solution.py
+++ b/solution.py
@@ -21,6 +21,7 @@
 BACK = BS + WINDOW
 GAP = 8
 SPAN = 2 * BS
+GRANT = 59
 F32 = jnp.float32
 BF16 = jnp.bfloat16
 
@@ -83,7 +84,7 @@
 
 
 def own_kernel(per, columns, experts, owner, fields, cot, *refs):
-    out, grid, cells, blank, blocks, numbers, counts, load_sems, sems = refs
+    out, _, grid, cells, blank, blocks, numbers, counts, load_sems, sems = refs
     height, width, chans = fields.shape
     sources = (cells, grid)
     loads = [copy(cot, cells, load_sems.at[0]), copy(fields, grid, load_sems.at[1])]
@@ -120,10 +121,11 @@
     out = pl.pallas_call(
         functools.partial(own_kernel, per, columns),
         out_shape=[
-            jax.ShapeDtypeStruct((columns, CAP, OWN, BS, chans), BF16),
+            jax.ShapeDtypeStruct((columns, CAP, LINES, BS, chans), BF16),
+            TOKEN,
         ],
         in_specs=[whole(pltpu.SMEM)] * 2 + [whole(pltpu.HBM)] * 2,
-        out_specs=[whole(pltpu.HBM)],
+        out_specs=[whole(pltpu.HBM)] * 2,
         scratch_shapes=[
             pltpu.VMEM(fields.shape, BF16),
             pltpu.VMEM(cot.shape, BF16),
@@ -131,11 +133,11 @@
         ]
         + tables(columns)
         + [pltpu.SemaphoreType.DMA((2,)), pltpu.SemaphoreType.DMA((2, columns * CAP))],
-        compiler_params=params(60),
+        compiler_params=params(GRANT),
         cost_estimate=pl.CostEstimate(flops=0, bytes_accessed=6_000_000, transcendentals=0),
         name="dispatch_own",
     )(experts, owner, fields, cot)
-    return out[0]
+    return out
 
 
 def rims_kernel(north, south, first, last, first_out, last_out):
@@ -192,10 +194,9 @@
 
 
 def ring_kernel(
-    per, columns, me, experts, owner, fields, north, south, west, east, *refs
+    per, columns, experts, owner, fields, north, south, west, east, _, out, rows, wide, rings,
+    blocks, numbers, counts, load_sem, sems,
 ):
-    outs = refs[:columns]
-    rows, wide, rings, blocks, numbers, counts, load_sem, sems = refs[columns:]
     height, width, chans = fields.shape
     stride = width + 2 * GAP
     load = copy(fields, rows.at[pl.ds(1, height)], load_sem)
@@ -213,42 +214,44 @@
     lax.fori_loop(0, height + 2, widen, 0)
     wide[pl.ds(GAP - 1, height + 2, stride=stride), :] = west[...].astype(F32)
     wide[pl.ds(GAP + width, height + 2, stride=stride), :] = east[...].astype(F32)
-    for k in range(columns):
-        for r in range(CAP):
-            s = k * CAP + r
-            slot = (me[0] ^ k) * CAP + r
-            top, left = corner(jnp.maximum(blocks[slot], 0), experts.shape[1])
-            start = pl.multiple_of(top * stride + left, 8)
-            upper = wide[pl.ds(start, BS + 2 * GAP), :]
-            start = pl.multiple_of(start + (EDGE - 1) * stride, 8)
-            lower = wide[pl.ds(start, BS + 2 * GAP), :]
-            start = (top + 1) * stride + left
-            ring = jnp.concatenate(
-                [
-                    upper[GAP - 1 : GAP + BS + 1],
-                    lower[GAP - 1 : GAP + BS + 1],
-                    wide[pl.ds(start + GAP - 1, BS, stride=stride), :],
-                    wide[pl.ds(start + GAP + BS, BS, stride=stride), :],
-                    jnp.full((RING * BS - NUMBER, chans), numbers[slot].astype(F32), F32),
-                ],
-                axis=0,
-            )
-            rings[s] = ring.astype(BF16).reshape(RING, BS, chans)
-            copy(rings.at[s], outs[k].at[r], sems.at[s]).start()
-    for k in range(columns):
-        for r in range(CAP):
-            s = k * CAP + r
-            copy(rings.at[s], outs[k].at[r], sems.at[s]).wait()
-
-
-def dispatch_rings(me, experts, owner, fields, north, south, west, east, per, columns):
+    for s in range(columns * CAP):
+        top, left = corner(jnp.maximum(blocks[s], 0), experts.shape[1])
+        start = pl.multiple_of(top * stride + left, 8)
+        upper = wide[pl.ds(start, BS + 2 * GAP), :]
+        start = pl.multiple_of(start + (EDGE - 1) * stride, 8)
+        lower = wide[pl.ds(start, BS + 2 * GAP), :]
+        start = (top + 1) * stride + left
+        ring = jnp.concatenate(
+            [
+                upper[GAP - 1 : GAP + BS + 1],
+                lower[GAP - 1 : GAP + BS + 1],
+                wide[pl.ds(start + GAP - 1, BS, stride=stride), :],
+                wide[pl.ds(start + GAP + BS, BS, stride=stride), :],
+                jnp.full((RING * BS - NUMBER, chans), numbers[s].astype(F32), F32),
+            ],
+            axis=0,
+        )
+        rings[s] = ring.astype(BF16).reshape(RING, BS, chans)
+        target = out.at[s // CAP, s % CAP, pl.ds(OWN, RING)]
+        copy(rings.at[s], target, sems.at[s]).start()
+    for s in range(columns * CAP):
+        target = out.at[s // CAP, s % CAP, pl.ds(OWN, RING)]
+        copy(rings.at[s], target, sems.at[s]).wait()
+
+
+def dispatch_rings(experts, owner, fields, north, south, west, east, filled, per):
     height, width, chans = fields.shape
+    columns = filled.shape[0]
     slots = columns * CAP
     return pl.pallas_call(
         functools.partial(ring_kernel, per, columns),
-        out_shape=[jax.ShapeDtypeStruct((CAP, RING, BS, chans), BF16)] * columns,
-        in_specs=[whole(pltpu.SMEM)] * 3 + [whole(pltpu.HBM)] + [whole()] * 4,
-        out_specs=[whole(pltpu.HBM)] * columns,
+        out_shape=jax.ShapeDtypeStruct(filled.shape, BF16),
+        in_specs=[whole(pltpu.SMEM)] * 2
+        + [whole(pltpu.HBM)]
+        + [whole()] * 4
+        + [whole(pltpu.HBM)],
+        out_specs=whole(pltpu.HBM),
+        input_output_aliases={7: 0},
         scratch_shapes=[
             pltpu.VMEM((height + 2, width, chans), BF16),
             pltpu.VMEM(((height + 2) * (width + 2 * GAP), chans), F32),
@@ -256,15 +259,10 @@
         ]
         + tables(columns)
         + [pltpu.SemaphoreType.DMA, pltpu.SemaphoreType.DMA((slots,))],
-        compiler_params=params(60),
+        compiler_params=params(GRANT),
         cost_estimate=pl.CostEstimate(flops=0, bytes_accessed=3_000_000, transcendentals=0),
         name="dispatch_rings",
-    )(me, experts, owner, fields, north, south, west, east)
-
-
-def load_slot(own, ring, column, r, target, sem):
-    copy(own.at[column, r], target.at[pl.ds(0, OWN)], sem).start()
-    copy(ring.at[r], target.at[pl.ds(OWN, RING)], sem).start()
+    )(experts, owner, fields, north, south, west, east, filled)
 
 
 def shifted_windows(data, wide):
@@ -300,33 +298,32 @@
     )
 
 
-def load_banks(place, banks, held, sems, slots, size):
+def load_bank(index, banks, target, sem, size):
+    piece = lax.div(index, size)
+    row = lax.rem(index, size)
+    p = 0
+    for bank in banks:
+        for start in range(0, bank.shape[0], size):
+
+            @pl.when(piece == p)
+            def _():
+                copy(bank.at[start + row], target, sem).start()
+
+            p += 1
+
+
+def taps_kernel(size, per, wanted, pieces, place, slots_in, *refs):
+    banks, refs = refs[:pieces], refs[pieces:]
+    out, sums, refs = refs[0], refs[1 : len(wanted) + 1], refs[len(wanted) + 1 :]
+    (held, stage, result, wide, cots, lines, before, after, total, rounded, seen, bank_sems,
+     load_sems, out_sems, sum_sems) = refs
+    chans = cots.shape[1]
+    slots = CAP * slots_in.shape[0]
     for s in range(slots):
-        piece = lax.div(place[s], size)
-        row = lax.rem(place[s], size)
-        p = 0
-        for bank in banks:
-            for start in range(0, bank.shape[0], size):
-
-                @pl.when(piece == p)
-                def _():
-                    copy(bank.at[start + row], held.at[s], sems.at[s]).start()
-
-                p += 1
-
-
-def taps_kernel(size, columns, pieces, extras, me, place, own, *refs):
-    rings, refs = refs[:columns], refs[columns:]
-    banks, refs = refs[:pieces], refs[pieces + extras :]
-    (out, _, held, stage, result, wide, cots, lines, before, after, bank_sems, load_sems,
-     out_sems) = refs
-    chans = cots.shape[1]
-    slots = CAP * columns
-    for k in range(columns):
-        for r in range(CAP):
-            s = k * CAP + r
-            load_slot(own, rings[k], me[0] ^ k, r, stage.at[s], load_sems.at[s])
-    load_banks(place, banks, held, bank_sems, slots, size)
+        copy(slots_in.at[s // CAP, s % CAP], stage.at[s], load_sems.at[s]).start()
+        load_bank(place[s // CAP, s % CAP], banks, held.at[s], bank_sems.at[s], size)
+    for e in range(len(wanted) * per):
+        seen[e] = 0
     cots[...] = jnp.zeros(cots.shape, F32)
     lines[...] = jnp.zeros(lines.shape, BF16)
     before[...] = jnp.zeros(before.shape, F32)
@@ -367,35 +364,79 @@
             preferred_element_type=F32,
         )
         result[s, BS:] = spread.astype(BF16).reshape(WINDOW, BS, chans)
+        windows = nine_taps(shifted_windows(data, wide))
         output = jnp.dot(
-            nine_taps(shifted_windows(data, wide)),
+            windows,
             bank[...].reshape(9 * chans, chans),
             preferred_element_type=F32,
         )
         result[s, 0:BS] = output.astype(BF16).reshape(BS, BS, chans)
-        target = out.at[me[0] ^ lax.div(s, CAP), lax.rem(s, CAP)]
+        target = out.at[lax.div(s, CAP), lax.rem(s, CAP)]
         copy(result.at[s], target, out_sems.at[s]).start()
+        index = place[lax.div(s, CAP), lax.rem(s, CAP)]
+        piece = lax.div(index, per)
+        for i, p in enumerate(wanted):
+
+            @pl.when(piece == p)
+            def _():
+                e = i * per + lax.rem(index, per)
+                term = lax.dot_general(
+                    data[0:BS].reshape(CELLS, chans),
+                    windows,
+                    (((0,), (0,)), ((), ())),
+                    preferred_element_type=F32,
+                )
+
+                @pl.when(seen[e] == 0)
+                def _():
+                    total[e] = term
+
+                @pl.when(seen[e] > 0)
+                def _():
+                    total[e] += term
+
+                seen[e] = 1
+
         return carry
 
     lax.fori_loop(0, slots, visit, 0)
+    for i in range(len(wanted)):
+
+        def expert(j, carry, i=i):
+            e = i * per + j
+
+            @pl.when(seen[e] > 0)
+            def _():
+                rounded[e] = total[e].astype(BF16)
+
+            @pl.when(seen[e] == 0)
+            def _():
+                rounded[e] = jnp.zeros(rounded.shape[1:], BF16)
+
+            copy(rounded.at[e], sums[i].at[j], sum_sems.at[e]).start()
+            return carry
+
+        lax.fori_loop(0, per, expert, 0)
     for s in range(slots):
         copy(result.at[s], result.at[s], out_sems.at[s]).wait()
-
-
-def taps(me, place, own, rings, banks, after):
-    columns, chans = len(rings), own.shape[-1]
+    for i in range(len(wanted)):
+        for j in range(per):
+            copy(rounded.at[0], sums[i].at[j], sum_sems.at[i * per + j]).wait()
+
+
+def taps(place, slots_in, banks, wanted):
+    columns, chans = slots_in.shape[0], slots_in.shape[-1]
     slots = CAP * columns
+    per, taps_n = banks[0].shape[:2]
     size = min(bank.shape[0] for bank in banks)
-    inputs = [me, place, own] + list(rings) + list(banks) + list(after)
-    return pl.pallas_call(
-        functools.partial(taps_kernel, size, columns, len(banks), len(after)),
-        out_shape=[
-            jax.ShapeDtypeStruct((columns, CAP, BACK, BS, chans), BF16),
-            TOKEN,
-        ],
-        in_specs=[whole(pltpu.SMEM)] * 2
-        + [whole(pltpu.HBM)] * (len(inputs) - 2),
-        out_specs=[whole(pltpu.HBM)] * 2,
+    shape = (per, chans, taps_n * chans)
+    found = (len(wanted) * per,) + shape[1:]
+    out = pl.pallas_call(
+        functools.partial(taps_kernel, size, per, wanted, len(banks)),
+        out_shape=[jax.ShapeDtypeStruct((columns, CAP, BACK, BS, chans), BF16)]
+        + [jax.ShapeDtypeStruct(shape, BF16)] * len(wanted),
+        in_specs=[whole(pltpu.SMEM)] + [whole(pltpu.HBM)] * (len(banks) + 1),
+        out_specs=[whole(pltpu.HBM)] * (len(wanted) + 1),
         scratch_shapes=[
             pltpu.VMEM((slots,) + banks[0].shape[1:], BF16),
             pltpu.VMEM((slots, LINES, BS, chans), BF16),
@@ -405,30 +446,32 @@
             pltpu.VMEM((3, (BS + 4) * BS, chans), BF16),
             pltpu.VMEM((TAIL + 8, chans), F32),
             pltpu.VMEM((TAIL + 8, chans), F32),
+            pltpu.VMEM(found, F32),
+            pltpu.VMEM(found, BF16),
+            pltpu.SMEM((found[0],), jnp.int32),
         ]
-        + [pltpu.SemaphoreType.DMA((slots,))] * 3,
-        compiler_params=params(60),
+        + [pltpu.SemaphoreType.DMA((slots,))] * 3
+        + [pltpu.SemaphoreType.DMA((found[0],))],
+        compiler_params=params(GRANT),
         cost_estimate=pl.CostEstimate(
-            flops=175_000_000 * slots, bytes_accessed=600_000 * slots, transcendentals=0
+            flops=200_000_000 * slots, bytes_accessed=800_000 * slots, transcendentals=0
         ),
         name="taps",
-    )(*inputs)
-
-
-def grads_kernel(piece, per, columns, terms, extras, me, place, own, *refs):
-    rings, refs = refs[:columns], refs[columns:]
+    )(place, slots_in, *banks)
+    return out[0], out[1:]
+
+
+def grads_kernel(piece, per, terms, extras, place, slots_in, *refs):
     added, refs = refs[:terms], refs[terms + extras :]
     (out, _, stage, extra, total, wide, result, seen, load_sems, extra_sems,
      out_sems) = refs
-    slots = CAP * columns
+    slots = CAP * slots_in.shape[0]
     chans = wide.shape[1]
-    for k in range(columns):
-        for r in range(CAP):
-            s = k * CAP + r
-
-            @pl.when(lax.div(place[s], per) == piece)
-            def _():
-                load_slot(own, rings[k], me[0] ^ k, r, stage.at[s], load_sems.at[s])
+    for s in range(slots):
+
+        @pl.when(lax.div(place[s // CAP, s % CAP], per) == piece)
+        def _():
+            copy(slots_in.at[s // CAP, s % CAP], stage.at[s], load_sems.at[s]).start()
 
     for j in range(per):
         seen[j] = 0
@@ -436,7 +479,7 @@
             copy(term.at[j], extra.at[i, j], extra_sems.at[i * per + j]).start()
 
     def visit(s, carry):
-        index = place[s]
+        index = place[lax.div(s, CAP), lax.rem(s, CAP)]
 
         @pl.when(lax.div(index, per) == piece)
         def _():
@@ -490,18 +533,16 @@
         copy(result.at[j], out.at[j], out_sems.at[j]).wait()
 
 
-def grads(me, place, own, rings, piece, bank_shape, added, after, dtype):
+def grads(place, slots_in, piece, bank_shape, added, after, dtype):
     per, taps_n, chans, outs = bank_shape
-    columns = len(rings)
-    slots = CAP * columns
+    slots = CAP * slots_in.shape[0]
     terms = max(len(added), 1)
     shape = (per, outs, taps_n * chans)
-    inputs = [me, place, own] + list(rings) + list(added) + list(after)
+    inputs = [place, slots_in] + list(added) + list(after)
     return pl.pallas_call(
-        functools.partial(grads_kernel, piece, per, columns, len(added), len(after)),
+        functools.partial(grads_kernel, piece, per, len(added), len(after)),
         out_shape=[jax.ShapeDtypeStruct(shape, dtype), TOKEN],
-        in_specs=[whole(pltpu.SMEM)] * 2
-        + [whole(pltpu.HBM)] * (len(inputs) - 2),
+        in_specs=[whole(pltpu.SMEM)] + [whole(pltpu.HBM)] * (len(inputs) - 1),
         out_specs=[whole(pltpu.HBM)] * 2,
         scratch_shapes=[
             pltpu.VMEM((slots, LINES, BS, chans), BF16),
@@ -514,7 +555,7 @@
             pltpu.SemaphoreType.DMA((terms * per,)),
             pltpu.SemaphoreType.DMA((per,)),
         ],
-        compiler_params=params(60),
+        compiler_params=params(GRANT),
         cost_estimate=pl.CostEstimate(
             flops=300_000_000, bytes_accessed=6_000_000, transcendentals=0
         ),
@@ -712,12 +753,6 @@
     return lax.ppermute(array, "lat", [(i, (i + 2 * shift) % count) for i in range(count)])
 
 
-def swap(array, k):
-    if k == 0:
-        return array
-    return lax.ppermute(array, "lon", [(i, i ^ k) for i in range(lax.axis_size("lon"))])
-
-
 def exchange(array):
     return lax.all_to_all(array, "lon", split_axis=0, concat_axis=0, tiled=True)
 
@@ -726,10 +761,10 @@
     return lax.optimization_barrier((arrays, others))[0]
 
 
-def places_of(rings, chips, per):
+def places_of(slots, chips, per):
     lat_index = lax.axis_index("lat")
-    line, row = NUMBER // BS, NUMBER % BS
-    numbers = jnp.concatenate([ring[:, line, row, 0] for ring in rings]).astype(jnp.int32)
+    line, row = OWN + NUMBER // BS, NUMBER % BS
+    numbers = slots[:, :, line, row, 0].astype(jnp.int32)
     owner_lat = numbers // per
     chip_step = (owner_lat // 2 - lat_index // 2 + chips) % chips
     core_step = (owner_lat % 2 - lat_index % 2 + 2) % 2
@@ -741,43 +776,40 @@
     chips = lax.axis_size("lat") // 2
     per = kernel_bank.shape[0]
     shape = kernel_bank.shape
-    me = lax.axis_index("lon").astype(jnp.int32).reshape(1)
 
     north = across(fields[-1:], "lat", 1, False)
     south = across(fields[:1], "lat", -1, False)
+    filled, _ = dispatch_own(block_expert, owner, fields, cotangent, per, columns)
     first, last = rims_of(
         north, south, fields[:, 0].astype(F32), fields[:, -1].astype(F32)
     )
     west = across(last, "lon", 1, True)
     east = across(first, "lon", -1, True)
-    own = dispatch_own(block_expert, owner, fields, cotangent, per, columns)
-    own = exchange(tied(own, (west, east)))
-
-    rings = dispatch_rings(
-        me, block_expert, owner, fields, north, south, west, east, per, columns
+    filled = dispatch_rings(
+        block_expert, owner, fields, north, south, west, east, filled, per
     )
-    rings = [swap(array, k) for k, array in enumerate(rings)]
-    stored = tied(kernel_bank, (west, east))
-    banks = [kernel_bank, to_other_core(stored)]
+    arrived = exchange(filled)
+    place = places_of(arrived, chips, per)
+    slots = (place, arrived)
+
+    banks = [kernel_bank, to_other_core(tied(kernel_bank, (west, east)))]
     for k in range(1, chips):
-        distant = tied(to_chip(stored, -k), rings[1 : columns // 2])
+        distant = to_chip(tied(kernel_bank, (first, last)), -k)
         banks += [distant, to_other_core(distant)]
 
-    place = places_of(rings, chips, per)
-    slots = (me, place, own, rings)
-
-    results, taps_token = taps(*slots, banks, [])
+    results, beside = taps(
+        place, arrived, banks, tuple(2 * k + 1 for k in range(1, chips))
+    )
     results = exchange(results)
-
-    arrived, tokens = [], [taps_token]
+    beside = [to_other_core(part) for part in beside]
+    chip_parts, tokens = [], []
     for k in range(1, chips):
-        part, token = grads(*slots, 2 * k + 1, shape, [], tokens, BF16)
-        part, token = grads(*slots, 2 * k, shape, [to_other_core(part)], [token], BF16)
-        arrived.append(to_chip(part, k))
+        part, token = grads(*slots, 2 * k, shape, [beside[k - 1]], tokens, BF16)
+        chip_parts.append(to_chip(part, k))
         tokens = [token]
     core_part, core_token = grads(*slots, 1, shape, [], tokens, BF16)
     own_part, own_token = grads(*slots, 0, shape, [], tokens, F32)
-    arrived.append(to_other_core(core_part))
+    terms = [own_part, to_other_core(core_part)] + chip_parts
 
     canvas, top, bottom, left, right = canvas_of(
         block_expert, owner, results, [core_token, own_token], fields.shape, per
@@ -788,7 +820,7 @@
     left, right = corners_of(above, below, left, right, token)
     from_west = across(right, "lon", 1, True)
     from_east = across(left, "lon", -1, True)
-    grad_bank, token = bank_of([own_part] + arrived, shape)
+    grad_bank, token = bank_of(terms, shape)
     grad_fields = finish(canvas, above, below, from_west, from_east, token, fields.shape)
     return (outputs, grad_fields, grad_bank)
 

time: 186 us -> 182 us (0.978)
  starting transfers between devices: 43.7 us -> 32.5 us
  waiting for transfers between devices: 85.3 us -> 94.5 us
    ppermute x7 -> x0, waiting for transfers between devices: 33.7 us -> none  [swap(): lax.ppermute(array, 'lon', [(i, i ^ k) for i in range(lax.axis_size('lon'...]
    ppermute x2, waiting for transfers between devices: 7.84 us -> 35.1 us  [to_chip(): lax.ppermute(array, 'lat', [(i, (i + 2 * shift) % count) for i in range(c...]
    all_to_all x2, waiting for transfers between devices: 34.8 us -> 54.1 us  [exchange(): return lax.all_to_all(array, 'lon', split_axis=0, concat_axis=0, tiled=True)]
    ppermute x7 -> x0, starting transfers between devices: 9.96 us -> none  [swap(): lax.ppermute(array, 'lon', [(i, i ^ k) for i in range(lax.axis_size('lon'...]
    ppermute x8, waiting for transfers between devices: 8.09 us -> 5.29 us  [across(): return lax.ppermute(array, axis, pairs)]
    ppermute x4, starting transfers between devices: 3.56 us -> 1.19 us  [to_other_core(): lax.ppermute(array, 'lat', [(i, i ^ 1) for i in range(lax.axis_size('lat'...]
    pallas_call x6 -> x5, Pallas kernels: 34.9 us -> 34 us  [the longest x3 16.2 us: grads(): pl.pallas_call(functools.partial(grads_kernel, piece, per, len(added), le...]
  transfers between devices with their start and end apart: 23 -> 16, of which waited for: 12 -> 5; matrix products, arithmetic and copies ran while one was open for 2% -> 1% of each run, Pallas kernels for 17% -> 18%
where the time goes in v3:
time: 182 us; the launch traced here: 179 us
  waiting for transfers between devices  94.5 us (52%)
  Pallas kernels  47.1 us (26%)
  starting transfers between devices  32.5 us (18%)
  local copies, waits for them, and re-layouts  3.52 us (2%)
    all_to_all x2, waiting for transfers between devices, exchange(): return lax.all_to_all(array, 'lon', split_axis=0, concat_axis=0, tiled=True)  54.1 us
    ppermute x2, waiting for transfers between devices, to_chip(): lax.ppermute(array, 'lat', [(i, (i + 2 * shift) % count) for i in range(c...  35.1 us
    pallas_call x3, Pallas kernels, grads(): pl.pallas_call(functools.partial(grads_kernel, piece, per, len(added), le...  16.2 us
    ppermute x8, starting transfers between devices, across(): return lax.ppermute(array, axis, pairs)  15.7 us
    pallas_call x1, Pallas kernels, taps(): pl.pallas_call(functools.partial(taps_kernel, size, per, wanted, len(bank...  14.5 us
    all_to_all x2, starting transfers between devices, exchange(): return lax.all_to_all(array, 'lon', split_axis=0, concat_axis=0, tiled=True)  9.28 us
    ppermute x2, starting transfers between devices, to_chip(): lax.ppermute(array, 'lat', [(i, (i + 2 * shift) % count) for i in range(c...  6.35 us
    ppermute x8, waiting for transfers between devices, across(): return lax.ppermute(array, axis, pairs)  5.29 us
  transfers between devices with their start and end apart: 16, of which 5 were waited for; matrix products, arithmetic and copies ran while one was open for 1% of the time, Pallas kernels for 18%

profile of v3, /device:TPU:0, one launch (start us, length us, event | category | flops | bytes accessed | tf_op | source)
XLA Modules:
  0.0 179.4 jit_solution(9294505248461133610)
XLA Ops:
  0.6 0.8 fusion.15
  1.4 2.3 %collective-permute-start = (bf16[1,128,128]{2,1,0:T(8,128)(2,1)S(1)}, bf16[1,128,128]{2,1,0:T(8,128)(2,1)S(1)}, u32[]{:S(2)}, u32[]{:S(2)}) collective-permute-start(bf16[1,128,128]{2,1,0:T(8,128)(2,1)S(1)} %get-tuple-element.54), channel_id=1, source_target_pairs={{0,8},{8,16},{16,24},{1,9},{9,17},{17,25},{2,10},{10,18},{18,26},{... | collective-permute-start | bytes 98312 | tf_op jit(solution)/shard_map/ppermute | solution.py:744
  3.8 1.3 collective-permute-start.1
  5.1 0.9 fusion.14
  6.0 3.0 %collective-permute-done.1.south = bf16[1,128,128]{2,1,0:T(8,128)(2,1)S(1)} collective-permute-done((bf16[1,128,128]{2,1,0:T(8,128)(2,1)S(1)}, bf16[1,128,128]{2,1,0:T(8,128)(2,1)S(1)}, u32[]{:S(2)}, u32[]{:S(2)}) %collective-permute-start.1) | collective-permute-done | bytes 32800 | tf_op jit(solution)/shard_map/ppermute | solution.py:744
  9.0 2.6 %collective-permute-start.5 = (bf16[8,9,128,128]{3,2,1,0:T(8,128)(2,1)}, bf16[8,9,128,128]{3,2,1,0:T(8,128)(2,1)}, u32[]{:S(2)}, u32[]{:S(2)}) collective-permute-start(bf16[8,9,128,128]{3,2,1,0:T(8,128)(2,1)} %refs_0_.1), channel_id=1, source_target_pairs={{0,16},{8,24},{16,0},{24,8},{1,17},{9,25},{17,1},{25,9},{2,18},{10... | collective-permute-start | bytes 7077896 | tf_op jit(solution)/shard_map/ppermute | solution.py:753
  11.6 1.5 collective-permute-start.2
  13.1 3.2 %collective-permute-start.3 = (bf16[34,128]{1,0:T(8,128)(2,1)S(1)}, bf16[34,128]{1,0:T(8,128)(2,1)S(1)}, u32[]{:S(2)}, u32[]{:S(2)}) collective-permute-start(bf16[34,128]{1,0:T(8,128)(2,1)S(1)} %get-tuple-element.28), channel_id=1, source_target_pairs={{0,7},{1,0},{2,1},{3,2},{4,3},{5,4},{6,5},{7,6},{8,15},{9,8},{10,9... | collective-permute-start | bytes 26120 | tf_op jit(solution)/shard_map/ppermute | solution.py:744
  16.3 3.5 %dispatch_own.1 = (bf16[8,2,37,16,128]{4,3,2,1,0:T(8,128)(2,1)}, f32[8,128]{1,0:T(8,128)}) custom-call(s32[2,8]{1,0:T(2,128)} %experts.7, s32[256]{0:T(256)} %owner.7, bf16[32,128,128]{2,1,0:T(8,128)(2,1)} %fields.3, bf16[32,128,128]{2,1,0:T(8,128)(2,1)} %cot.1), custom_call_target="tpu_custom_call" | custom-call | bytes 6000000 | tf_op jit(solution)/shard_map/dispatch_own/pallas_call | solution.py:121
  20.4 3.3 %dispatch_rings.1 = bf16[8,2,37,16,128]{4,3,2,1,0:T(8,128)(2,1)} custom-call(s32[2,8]{1,0:T(2,128)} %experts.7, s32[256]{0:T(256)} %owner.7, bf16[32,128,128]{2,1,0:T(8,128)(2,1)} %fields.3, bf16[1,128,128]{2,1,0:T(8,128)(2,1)} %copy-done.1, bf16[1,128,128]{2,1,0:T(8,128)(2,1)} %copy-done.2, ...), custom_call_target="tpu_custom_call", output_to_operand_aliasing={{}: (7, {})} | custom-call | bytes 3000000 | tf_op jit(solution)/shard_map/dispatch_rings/pallas_call | solution.py:246
  23.7 4.1 %all-to-all-start = ((bf16[8,2,37,16,128]{4,3,2,1,0:T(8,128)(2,1)}), bf16[8,2,37,16,128]{4,3,2,1,0:T(8,128)(2,1)S(1)}, u32[]{:S(2)}, u32[]{:S(2)}) async-start(bf16[8,2,37,16,128]{4,3,2,1,0:T(8,128)(2,1)} %dispatch_rings.1), calls=%async_computation | async-start | bytes 4849664 | tf_op jit(solution)/shard_map/all_to_all | solution.py:757
  27.8 35.1 %collective-permute-done.5.refs_2_ = bf16[8,9,128,128]{3,2,1,0:T(8,128)(2,1)} collective-permute-done((bf16[8,9,128,128]{3,2,1,0:T(8,128)(2,1)}, bf16[8,9,128,128]{3,2,1,0:T(8,128)(2,1)}, u32[]{:S(2)}, u32[]{:S(2)}) %collective-permute-start.5) | collective-permute-done | bytes 2359328 | tf_op jit(solution)/shard_map/ppermute | solution.py:753
  63.0 1.0 collective-permute-start.6
  64.0 18.8 %all-to-all-done.slots_in = bf16[8,2,37,16,128]{4,3,2,1,0:T(8,128)(2,1)S(1)} async-done(((bf16[8,2,37,16,128]{4,3,2,1,0:T(8,128)(2,1)}), bf16[8,2,37,16,128]{4,3,2,1,0:T(8,128)(2,1)S(1)}, u32[]{:S(2)}, u32[]{:S(2)}) %all-to-all-start) | async-done | bytes 2424864 | tf_op jit(solution)/shard_map/all_to_all | solution.py:757
  83.0 0.9 fusion.8.place
  84.2 14.5 %taps.1 = (bf16[8,2,37,16,128]{4,3,2,1,0:T(8,128)(2,1)}, bf16[8,128,1152]{2,1,0:T(8,128)(2,1)}) custom-call(s32[8,2]{1,0:T(8,128)} %fusion.8.place, bf16[8,2,37,16,128]{4,3,2,1,0:T(8,128)(2,1)} %copy-done.7, bf16[8,9,128,128]{3,2,1,0:T(8,128)(2,1)} %refs_0_.1, bf16[8,9,128,128]{3,2,1,0:T(8,128)(2,1)} %collective-permute-done.4.refs_1_, ...), custom_call_target="tpu_custom_call" | custom-call | flops 3200000000 | bytes 12800000 | tf_op jit(solution)/shard_map/taps/pallas_call | solution.py:434
  98.8 5.2 %all-to-all-start.1 = ((bf16[8,2,37,16,128]{4,3,2,1,0:T(8,128)(2,1)}), bf16[8,2,37,16,128]{4,3,2,1,0:T(8,128)(2,1)S(1)}, u32[]{:S(2)}, u32[]{:S(2)}) async-start(bf16[8,2,37,16,128]{4,3,2,1,0:T(8,128)(2,1)} %get-tuple-element.32), calls=%async_computation.1 | async-start | bytes 4849664 | tf_op jit(solution)/shard_map/all_to_all | solution.py:757
  104.0 4.6 %grads.3 = (bf16[8,128,1152]{2,1,0:T(8,128)(2,1)}, f32[8,128]{1,0:T(8,128)}) custom-call(s32[8,2]{1,0:T(8,128)} %fusion.8.place, bf16[8,2,37,16,128]{4,3,2,1,0:T(8,128)(2,1)} %copy-done.7, bf16[8,128,1152]{2,1,0:T(8,128)(2,1)} %collective-permute-done.7.refs_0_), custom_call_target="tpu_custom_call" | custom-call | flops 300000000 | bytes 6000000 | tf_op jit(solution)/shard_map/grads/pallas_call | solution.py:542
  108.6 5.0 %grads.4 = (bf16[8,128,1152]{2,1,0:T(8,128)(2,1)}, f32[8,128]{1,0:T(8,128)}) custom-call(s32[8,2]{1,0:T(8,128)} %fusion.8.place, bf16[8,2,37,16,128]{4,3,2,1,0:T(8,128)(2,1)} %copy-done.7, f32[8,128]{1,0:T(8,128)} %get-tuple-element.35.refs_0_), custom_call_target="tpu_custom_call" | custom-call | flops 300000000 | bytes 6000000 | tf_op jit(solution)/shard_map/grads/pallas_call | solution.py:542
  113.7 3.8 %collective-permute-start.13 = (bf16[8,128,1152]{2,1,0:T(8,128)(2,1)}, bf16[8,128,1152]{2,1,0:T(8,128)(2,1)}, u32[]{:S(2)}, u32[]{:S(2)}) collective-permute-start(bf16[8,128,1152]{2,1,0:T(8,128)(2,1)} %get-tuple-element.48), channel_id=1, source_target_pairs={{0,16},{8,24},{16,0},{24,8},{1,17},{9,25},{17,1},{25,9},{2,18},{10... | collective-permute-start | bytes 7077896 | tf_op jit(solution)/shard_map/ppermute | solution.py:753
  117.5 6.6 %grads.5 = (f32[8,128,1152]{2,1,0:T(8,128)}, f32[8,128]{1,0:T(8,128)}) custom-call(s32[8,2]{1,0:T(8,128)} %fusion.8.place, bf16[8,2,37,16,128]{4,3,2,1,0:T(8,128)(2,1)} %copy-done.7, f32[8,128]{1,0:T(8,128)} %get-tuple-element.35.refs_0_), custom_call_target="tpu_custom_call" | custom-call | flops 300000000 | bytes 6000000 | tf_op jit(solution)/shard_map/grads/pallas_call | solution.py:542
  124.1 35.3 %all-to-all-done.1.source = bf16[8,2,37,16,128]{4,3,2,1,0:T(8,128)(2,1)S(1)} async-done(((bf16[8,2,37,16,128]{4,3,2,1,0:T(8,128)(2,1)}), bf16[8,2,37,16,128]{4,3,2,1,0:T(8,128)(2,1)S(1)}, u32[]{:S(2)}, u32[]{:S(2)}) %all-to-all-start.1) | async-done | bytes 2424864 | tf_op jit(solution)/shard_map/all_to_all | solution.py:757
  159.4 0.7 copy-done.6
  160.1 2.0 %canvas.1 = (f32[4896,128]{1,0:T(8,128)S(1)}, bf16[144,128]{1,0:T(8,128)(2,1)S(1)}, bf16[144,128]{1,0:T(8,128)(2,1)S(1)}, f32[32,128]{1,0:T(8,128)S(1)}, f32[32,128]{1,0:T(8,128)S(1)}) custom-call(s32[2,8]{1,0:T(2,128)S(1)} %copy-done.3, s32[256]{0:T(256)S(1)} %copy-done.4, bf16[8,2,37,16,128]{4,3,2,1,0:T(8,128)(2,1)S(1)} %all-to-all-done.1.source, ...), custom_call_target="tpu_custom_call" | custom-call | bytes 6000000 | tf_op jit(solution)/shard_map/canvas/pallas_call | solution.py:656
  162.1 1.3 collective-permute-start.8
  163.4 1.3 collective-permute-start.9
  164.7 2.2 %outputs.1 = (bf16[32,128,128]{2,1,0:T(8,128)(2,1)}, f32[8,128]{1,0:T(8,128)S(1)}) custom-call(s32[2,8]{1,0:T(2,128)S(1)} %copy-done.3, s32[256]{0:T(256)S(1)} %copy-done.4, bf16[8,2,37,16,128]{4,3,2,1,0:T(8,128)(2,1)S(1)} %all-to-all-done.1.source), custom_call_target="tpu_custom_call" | custom-call | bytes 3000000 | tf_op jit(solution)/shard_map/outputs/pallas_call | solution.py:695
  167.0 2.3 %collective-permute-done.9.below.south = bf16[144,128]{1,0:T(8,128)(2,1)S(1)} collective-permute-done((bf16[144,128]{1,0:T(8,128)(2,1)S(1)}, bf16[144,128]{1,0:T(8,128)(2,1)S(1)}, u32[]{:S(2)}, u32[]{:S(2)}) %collective-permute-start.9) | collective-permute-done | bytes 36896 | tf_op jit(solution)/shard_map/ppermute | solution.py:744
  169.3 1.5 collective-permute-start.10
  170.8 3.3 %collective-permute-start.11 = (bf16[32,128]{1,0:T(8,128)(2,1)S(1)}, bf16[32,128]{1,0:T(8,128)(2,1)S(1)}, u32[]{:S(2)}, u32[]{:S(2)}) collective-permute-start(bf16[32,128]{1,0:T(8,128)(2,1)S(1)} %get-tuple-element.45), channel_id=1, source_target_pairs={{0,7},{1,0},{2,1},{3,2},{4,3},{5,4},{6,5},{7,6},{8,15},{9,8},{10,9... | collective-permute-start | bytes 24584 | tf_op jit(solution)/shard_map/ppermute | solution.py:744
  174.1 4.2 %bank.1 = (f32[8,9,128,128]{3,2,1,0:T(8,128)}, f32[8,128]{1,0:T(8,128)S(1)}) custom-call(f32[8,128,1152]{2,1,0:T(8,128)S(1)} %copy-done, bf16[8,128,1152]{2,1,0:T(8,128)(2,1)} %collective-permute-done.12.refs_1_, bf16[8,128,1152]{2,1,0:T(8,128)(2,1)} %collective-permute-done.13.refs_2_), custom_call_target="tpu_custom_call" | custom-call | bytes 12000000 | tf_op jit(solution)/shard_map/bank/pallas_call | solution.py:595
  178.3 1.1 finish.1
  (39 shorter events, 1.4 us)
Async XLA Ops:
  1.4 4.6 %collective-permute-start = (bf16[1,128,128]{2,1,0:T(8,128)(2,1)S(1)}, bf16[1,128,128]{2,1,0:T(8,128)(2,1)S(1)}, u32[]{:S(2)}, u32[]{:S(2)}) collective-permute-start(bf16[1,128,128]{2,1,0:T(8,128)(2,1)S(1)} %get-tuple-element.54), channel_id=1, source_target_pairs={{0,8},{8,16},{16,24},{1,9},{9,17},{17,25},{2,10},{10,18},{18,26},{... | collective-permute-start | bytes 98312 | tf_op jit(solution)/shard_map/ppermute | solution.py:744
  3.8 5.2 %collective-permute-start.1 = (bf16[1,128,128]{2,1,0:T(8,128)(2,1)S(1)}, bf16[1,128,128]{2,1,0:T(8,128)(2,1)S(1)}, u32[]{:S(2)}, u32[]{:S(2)}) collective-permute-start(bf16[1,128,128]{2,1,0:T(8,128)(2,1)S(1)} %get-tuple-element.53), channel_id=1, source_target_pairs={{8,0},{16,8},{24,16},{9,1},{17,9},{25,17},{10,2},{18,10},{26,18},{... | collective-permute-start | bytes 98312 | tf_op jit(solution)/shard_map/ppermute | solution.py:744
  6.0 13.9 %copy-start.1 = (bf16[1,128,128]{2,1,0:T(8,128)(2,1)}, bf16[1,128,128]{2,1,0:T(8,128)(2,1)S(1)}, u32[]{:S(2)}) copy-start(bf16[1,128,128]{2,1,0:T(8,128)(2,1)S(1)} %collective-permute-done.north) | copy-start | bytes 98308
  9.0 10.9 %copy-start.2 = (bf16[1,128,128]{2,1,0:T(8,128)(2,1)}, bf16[1,128,128]{2,1,0:T(8,128)(2,1)S(1)}, u32[]{:S(2)}) copy-start(bf16[1,128,128]{2,1,0:T(8,128)(2,1)S(1)} %collective-permute-done.1.south) | copy-start | bytes 98308
  9.0 54.0 %collective-permute-start.5 = (bf16[8,9,128,128]{3,2,1,0:T(8,128)(2,1)}, bf16[8,9,128,128]{3,2,1,0:T(8,128)(2,1)}, u32[]{:S(2)}, u32[]{:S(2)}) collective-permute-start(bf16[8,9,128,128]{3,2,1,0:T(8,128)(2,1)} %refs_0_.1), channel_id=1, source_target_pairs={{0,16},{8,24},{16,0},{24,8},{1,17},{9,25},{17,1},{25,9},{2,18},{10... | collective-permute-start | bytes 7077896 | tf_op jit(solution)/shard_map/ppermute | solution.py:753
  11.6 8.2 %collective-permute-start.2 = (bf16[34,128]{1,0:T(8,128)(2,1)S(1)}, bf16[34,128]{1,0:T(8,128)(2,1)S(1)}, u32[]{:S(2)}, u32[]{:S(2)}) collective-permute-start(bf16[34,128]{1,0:T(8,128)(2,1)S(1)} %get-tuple-element.27), channel_id=1, source_target_pairs={{0,1},{1,2},{2,3},{3,4},{4,5},{5,6},{6,7},{7,0},{8,9},{9,10},{10,1... | collective-permute-start | bytes 26120 | tf_op jit(solution)/shard_map/ppermute | solution.py:744
  13.1 6.7 %collective-permute-start.3 = (bf16[34,128]{1,0:T(8,128)(2,1)S(1)}, bf16[34,128]{1,0:T(8,128)(2,1)S(1)}, u32[]{:S(2)}, u32[]{:S(2)}) collective-permute-start(bf16[34,128]{1,0:T(8,128)(2,1)S(1)} %get-tuple-element.28), channel_id=1, source_target_pairs={{0,7},{1,0},{2,1},{3,2},{4,3},{5,4},{6,5},{7,6},{8,15},{9,8},{10,9... | collective-permute-start | bytes 26120 | tf_op jit(solution)/shard_map/ppermute | solution.py:744
  19.8 0.6 copy-start.8
  19.8 0.6 copy-start.9
  23.7 59.1 %all-to-all-start = ((bf16[8,2,37,16,128]{4,3,2,1,0:T(8,128)(2,1)}), bf16[8,2,37,16,128]{4,3,2,1,0:T(8,128)(2,1)S(1)}, u32[]{:S(2)}, u32[]{:S(2)}) async-start(bf16[8,2,37,16,128]{4,3,2,1,0:T(8,128)(2,1)} %dispatch_rings.1), calls=%async_computation | async-start | bytes 4849664 | tf_op jit(solution)/shard_map/all_to_all | solution.py:757
  27.8 56.0 %collective-permute-start.4 = (bf16[8,9,128,128]{3,2,1,0:T(8,128)(2,1)}, bf16[8,9,128,128]{3,2,1,0:T(8,128)(2,1)}, u32[]{:S(2)}, u32[]{:S(2)}) collective-permute-start(bf16[8,9,128,128]{3,2,1,0:T(8,128)(2,1)} %refs_0_.1), channel_id=1, source_target_pairs={{0,8},{8,0},{16,24},{24,16},{1,9},{9,1},{17,25},{25,17},{2,10},{10... | collective-permute-start | bytes 7077896 | tf_op jit(solution)/shard_map/ppermute | solution.py:748
  63.0 20.9 %collective-permute-start.6 = (bf16[8,9,128,128]{3,2,1,0:T(8,128)(2,1)}, bf16[8,9,128,128]{3,2,1,0:T(8,128)(2,1)}, u32[]{:S(2)}, u32[]{:S(2)}) collective-permute-start(bf16[8,9,128,128]{3,2,1,0:T(8,128)(2,1)} %collective-permute-done.5.refs_2_), channel_id=1, source_target_pairs={{0,8},{8,0},{16,24},{24,16},{1,9},{9,1},{17,25},{25,17},{2,10},{10... | collective-permute-start | bytes 7077896 | tf_op jit(solution)/shard_map/ppermute | solution.py:748
  82.8 1.4 copy-start.7
  98.7 5.3 %collective-permute-start.7 = (bf16[8,128,1152]{2,1,0:T(8,128)(2,1)}, bf16[8,128,1152]{2,1,0:T(8,128)(2,1)}, u32[]{:S(2)}, u32[]{:S(2)}) collective-permute-start(bf16[8,128,1152]{2,1,0:T(8,128)(2,1)} %get-tuple-element.34), channel_id=1, source_target_pairs={{0,8},{8,0},{16,24},{24,16},{1,9},{9,1},{17,25},{25,17},{2,10},{10... | collective-permute-start | bytes 7077896 | tf_op jit(solution)/shard_map/ppermute | solution.py:748
  98.8 60.6 %all-to-all-start.1 = ((bf16[8,2,37,16,128]{4,3,2,1,0:T(8,128)(2,1)}), bf16[8,2,37,16,128]{4,3,2,1,0:T(8,128)(2,1)S(1)}, u32[]{:S(2)}, u32[]{:S(2)}) async-start(bf16[8,2,37,16,128]{4,3,2,1,0:T(8,128)(2,1)} %get-tuple-element.32), calls=%async_computation.1 | async-start | bytes 4849664 | tf_op jit(solution)/shard_map/all_to_all | solution.py:757
  108.6 50.9 %copy-start.3 = (s32[2,8]{1,0:T(2,128)S(1)}, s32[2,8]{1,0:T(2,128)}, u32[]{:S(2)}) copy-start(s32[2,8]{1,0:T(2,128)} %experts.7) | copy-start | bytes 196
  108.6 50.8 %copy-start.4 = (s32[256]{0:T(256)S(1)}, s32[256]{0:T(256)}, u32[]{:S(2)}) copy-start(s32[256]{0:T(256)} %owner.7) | copy-start | bytes 3076
  113.6 45.8 %copy-start.5 = (f32[8,128]{1,0:T(8,128)S(1)}, f32[8,128]{1,0:T(8,128)}, u32[]{:S(2)}) copy-start(f32[8,128]{1,0:T(8,128)} %get-tuple-element.36.refs_0_) | copy-start | bytes 12292
  113.6 60.5 %collective-permute-start.12 = (bf16[8,128,1152]{2,1,0:T(8,128)(2,1)}, bf16[8,128,1152]{2,1,0:T(8,128)(2,1)}, u32[]{:S(2)}, u32[]{:S(2)}) collective-permute-start(bf16[8,128,1152]{2,1,0:T(8,128)(2,1)} %get-tuple-element.47), channel_id=1, source_target_pairs={{0,8},{8,0},{16,24},{24,16},{1,9},{9,1},{17,25},{25,17},{2,10},{10... | collective-permute-start | bytes 7077896 | tf_op jit(solution)/shard_map/ppermute | solution.py:748
  113.7 60.4 %collective-permute-start.13 = (bf16[8,128,1152]{2,1,0:T(8,128)(2,1)}, bf16[8,128,1152]{2,1,0:T(8,128)(2,1)}, u32[]{:S(2)}, u32[]{:S(2)}) collective-permute-start(bf16[8,128,1152]{2,1,0:T(8,128)(2,1)} %get-tuple-element.48), channel_id=1, source_target_pairs={{0,16},{8,24},{16,0},{24,8},{1,17},{9,25},{17,1},{25,9},{2,18},{10... | collective-permute-start | bytes 7077896 | tf_op jit(solution)/shard_map/ppermute | solution.py:753
  159.4 0.7 copy-start.6
  160.1 14.0 %copy-start = (f32[8,128,1152]{2,1,0:T(8,128)S(1)}, f32[8,128,1152]{2,1,0:T(8,128)}, u32[]{:S(2)}) copy-start(f32[8,128,1152]{2,1,0:T(8,128)} %get-tuple-element.46.refs_0_) | copy-start | bytes 14155780
  162.1 4.8 %collective-permute-start.8 = (bf16[144,128]{1,0:T(8,128)(2,1)S(1)}, bf16[144,128]{1,0:T(8,128)(2,1)S(1)}, u32[]{:S(2)}, u32[]{:S(2)}) collective-permute-start(bf16[144,128]{1,0:T(8,128)(2,1)S(1)} %get-tuple-element.39), channel_id=1, source_target_pairs={{0,8},{8,16},{16,24},{1,9},{9,17},{17,25},{2,10},{10,18},{18,26},{... | collective-permute-start | bytes 110600 | tf_op jit(solution)/shard_map/ppermute | solution.py:744
  163.4 5.9 %collective-permute-start.9 = (bf16[144,128]{1,0:T(8,128)(2,1)S(1)}, bf16[144,128]{1,0:T(8,128)(2,1)S(1)}, u32[]{:S(2)}, u32[]{:S(2)}) collective-permute-start(bf16[144,128]{1,0:T(8,128)(2,1)S(1)} %get-tuple-element.40), channel_id=1, source_target_pairs={{8,0},{16,8},{24,16},{9,1},{17,9},{25,17},{10,2},{18,10},{26,18},{... | collective-permute-start | bytes 110600 | tf_op jit(solution)/shard_map/ppermute | solution.py:744
  169.3 9.0 %collective-permute-start.10 = (bf16[32,128]{1,0:T(8,128)(2,1)S(1)}, bf16[32,128]{1,0:T(8,128)(2,1)S(1)}, u32[]{:S(2)}, u32[]{:S(2)}) collective-permute-start(bf16[32,128]{1,0:T(8,128)(2,1)S(1)} %get-tuple-element.44), channel_id=1, source_target_pairs={{0,1},{1,2},{2,3},{3,4},{4,5},{5,6},{6,7},{7,0},{8,9},{9,10},{10,1... | collective-permute-start | bytes 24584 | tf_op jit(solution)/shard_map/ppermute | solution.py:744
  170.8 7.5 %collective-permute-start.11 = (bf16[32,128]{1,0:T(8,128)(2,1)S(1)}, bf16[32,128]{1,0:T(8,128)(2,1)S(1)}, u32[]{:S(2)}, u32[]{:S(2)}) collective-permute-start(bf16[32,128]{1,0:T(8,128)(2,1)S(1)} %get-tuple-element.45), channel_id=1, source_target_pairs={{0,7},{1,0},{2,1},{3,2},{4,3},{5,4},{6,5},{7,6},{8,15},{9,8},{10,9... | collective-permute-start | bytes 24584 | tf_op jit(solution)/shard_map/ppermute | solution.py:744

commit v4 on v3

--- a/solution.py
+++ b/solution.py
@@ -19,6 +19,7 @@
 NUMBER = 4 * BS + 4
 WINDOW = EDGE + TAIL // BS
 BACK = BS + WINDOW
+SPARE = 8
 GAP = 8
 SPAN = 2 * BS
 GRANT = 59
@@ -254,7 +255,7 @@
         input_output_aliases={7: 0},
         scratch_shapes=[
             pltpu.VMEM((height + 2, width, chans), BF16),
-            pltpu.VMEM(((height + 2) * (width + 2 * GAP), chans), F32),
+            pltpu.VMEM(((height + SPARE) * (width + 2 * GAP), chans), F32),
             pltpu.VMEM((slots, RING, BS, chans), BF16),
         ]
         + tables(columns)
@@ -656,7 +657,7 @@
     return pl.pallas_call(
         functools.partial(canvas_kernel, per, columns, shape, len(after)),
         out_shape=(
-            jax.ShapeDtypeStruct(((height + 2) * stride, chans), F32),
+            jax.ShapeDtypeStruct(((height + SPARE) * stride, chans), F32),
             jax.ShapeDtypeStruct((stride, chans), BF16),
             jax.ShapeDtypeStruct((stride, chans), BF16),
             jax.ShapeDtypeStruct((height, chans), F32),

time: 182 us -> 182 us (level)
  transfers between devices with their start and end apart: 16 -> 16, of which waited for: 5 -> 6; matrix products, arithmetic and copies ran while one was open for 1% -> 1% of each run, Pallas kernels for 18% -> 18%
where the time goes in v4:
time: 182 us; the launch traced here: 179 us
  waiting for transfers between devices  93.8 us (52%)
  Pallas kernels  47.3 us (26%)
  starting transfers between devices  32.5 us (18%)
  local copies, waits for them, and re-layouts  3.52 us (2%)
    all_to_all x2, waiting for transfers between devices, exchange(): return lax.all_to_all(array, 'lon', split_axis=0, concat_axis=0, tiled=True)  52.3 us
    ppermute x2, waiting for transfers between devices, to_chip(): lax.ppermute(array, 'lat', [(i, (i + 2 * shift) % count) for i in range(c...  35.1 us
    pallas_call x3, Pallas kernels, grads(): pl.pallas_call(functools.partial(grads_kernel, piece, per, len(added), le...  17 us
    ppermute x8, starting transfers between devices, across(): return lax.ppermute(array, axis, pairs)  15.7 us
    pallas_call x1, Pallas kernels, taps(): pl.pallas_call(functools.partial(taps_kernel, size, per, wanted, len(bank...  14 us
    all_to_all x2, starting transfers between devices, exchange(): return lax.all_to_all(array, 'lon', split_axis=0, concat_axis=0, tiled=True)  8.5 us
    ppermute x2, starting transfers between devices, to_chip(): lax.ppermute(array, 'lat', [(i, (i + 2 * shift) % count) for i in range(c...  5.97 us
    ppermute x8, waiting for transfers between devices, across(): return lax.ppermute(array, axis, pairs)  5.9 us
  transfers between devices with their start and end apart: 16, of which 6 were waited for; matrix products, arithmetic and copies ran while one was open for 1% of the time, Pallas kernels for 18%

profile of v4, /device:TPU:0, one launch (start us, length us, event | category | flops | bytes accessed | tf_op | source)
XLA Modules:
  0.0 178.9 jit_solution(11371335633612366703)
XLA Ops:
  0.6 0.8 fusion.15
  1.4 2.3 %collective-permute-start = (bf16[1,128,128]{2,1,0:T(8,128)(2,1)S(1)}, bf16[1,128,128]{2,1,0:T(8,128)(2,1)S(1)}, u32[]{:S(2)}, u32[]{:S(2)}) collective-permute-start(bf16[1,128,128]{2,1,0:T(8,128)(2,1)S(1)} %get-tuple-element.54), channel_id=1, source_target_pairs={{0,8},{8,16},{16,24},{1,9},{9,17},{17,25},{2,10},{10,18},{18,26},{... | collective-permute-start | bytes 98312 | tf_op jit(solution)/shard_map/ppermute | solution.py:745
  3.8 1.3 collective-permute-start.1
  5.1 0.9 fusion.14
  6.0 3.0 %collective-permute-done.1.south = bf16[1,128,128]{2,1,0:T(8,128)(2,1)S(1)} collective-permute-done((bf16[1,128,128]{2,1,0:T(8,128)(2,1)S(1)}, bf16[1,128,128]{2,1,0:T(8,128)(2,1)S(1)}, u32[]{:S(2)}, u32[]{:S(2)}) %collective-permute-start.1) | collective-permute-done | bytes 32800 | tf_op jit(solution)/shard_map/ppermute | solution.py:745
  9.0 2.6 %collective-permute-start.5 = (bf16[8,9,128,128]{3,2,1,0:T(8,128)(2,1)}, bf16[8,9,128,128]{3,2,1,0:T(8,128)(2,1)}, u32[]{:S(2)}, u32[]{:S(2)}) collective-permute-start(bf16[8,9,128,128]{3,2,1,0:T(8,128)(2,1)} %refs_0_.1), channel_id=1, source_target_pairs={{0,16},{8,24},{16,0},{24,8},{1,17},{9,25},{17,1},{25,9},{2,18},{10... | collective-permute-start | bytes 7077896 | tf_op jit(solution)/shard_map/ppermute | solution.py:754
  11.6 1.5 collective-permute-start.2
  13.1 3.2 %collective-permute-start.3 = (bf16[34,128]{1,0:T(8,128)(2,1)S(1)}, bf16[34,128]{1,0:T(8,128)(2,1)S(1)}, u32[]{:S(2)}, u32[]{:S(2)}) collective-permute-start(bf16[34,128]{1,0:T(8,128)(2,1)S(1)} %get-tuple-element.28), channel_id=1, source_target_pairs={{0,7},{1,0},{2,1},{3,2},{4,3},{5,4},{6,5},{7,6},{8,15},{9,8},{10,9... | collective-permute-start | bytes 26120 | tf_op jit(solution)/shard_map/ppermute | solution.py:745
  16.3 3.5 %dispatch_own.1 = (bf16[8,2,37,16,128]{4,3,2,1,0:T(8,128)(2,1)}, f32[8,128]{1,0:T(8,128)}) custom-call(s32[2,8]{1,0:T(2,128)} %experts.7, s32[256]{0:T(256)} %owner.7, bf16[32,128,128]{2,1,0:T(8,128)(2,1)} %fields.3, bf16[32,128,128]{2,1,0:T(8,128)(2,1)} %cot.1), custom_call_target="tpu_custom_call" | custom-call | bytes 6000000 | tf_op jit(solution)/shard_map/dispatch_own/pallas_call | solution.py:122
  20.4 3.3 %dispatch_rings.1 = bf16[8,2,37,16,128]{4,3,2,1,0:T(8,128)(2,1)} custom-call(s32[2,8]{1,0:T(2,128)} %experts.7, s32[256]{0:T(256)} %owner.7, bf16[32,128,128]{2,1,0:T(8,128)(2,1)} %fields.3, bf16[1,128,128]{2,1,0:T(8,128)(2,1)} %copy-done.1, bf16[1,128,128]{2,1,0:T(8,128)(2,1)} %copy-done.2, ...), custom_call_target="tpu_custom_call", output_to_operand_aliasing={{}: (7, {})} | custom-call | bytes 3000000 | tf_op jit(solution)/shard_map/dispatch_rings/pallas_call | solution.py:247
  23.7 4.1 %all-to-all-start = ((bf16[8,2,37,16,128]{4,3,2,1,0:T(8,128)(2,1)}), bf16[8,2,37,16,128]{4,3,2,1,0:T(8,128)(2,1)S(1)}, u32[]{:S(2)}, u32[]{:S(2)}) async-start(bf16[8,2,37,16,128]{4,3,2,1,0:T(8,128)(2,1)} %dispatch_rings.1), calls=%async_computation | async-start | bytes 4849664 | tf_op jit(solution)/shard_map/all_to_all | solution.py:758
  27.8 35.1 %collective-permute-done.5.refs_2_ = bf16[8,9,128,128]{3,2,1,0:T(8,128)(2,1)} collective-permute-done((bf16[8,9,128,128]{3,2,1,0:T(8,128)(2,1)}, bf16[8,9,128,128]{3,2,1,0:T(8,128)(2,1)}, u32[]{:S(2)}, u32[]{:S(2)}) %collective-permute-start.5) | collective-permute-done | bytes 2359328 | tf_op jit(solution)/shard_map/ppermute | solution.py:754
  63.0 1.0 collective-permute-start.6
  64.0 18.8 %all-to-all-done.slots_in = bf16[8,2,37,16,128]{4,3,2,1,0:T(8,128)(2,1)S(1)} async-done(((bf16[8,2,37,16,128]{4,3,2,1,0:T(8,128)(2,1)}), bf16[8,2,37,16,128]{4,3,2,1,0:T(8,128)(2,1)S(1)}, u32[]{:S(2)}, u32[]{:S(2)}) %all-to-all-start) | async-done | bytes 2424864 | tf_op jit(solution)/shard_map/all_to_all | solution.py:758
  83.0 0.9 fusion.8.place
  84.2 14.0 %taps.1 = (bf16[8,2,37,16,128]{4,3,2,1,0:T(8,128)(2,1)}, bf16[8,128,1152]{2,1,0:T(8,128)(2,1)}) custom-call(s32[8,2]{1,0:T(8,128)} %fusion.8.place, bf16[8,2,37,16,128]{4,3,2,1,0:T(8,128)(2,1)} %copy-done.7, bf16[8,9,128,128]{3,2,1,0:T(8,128)(2,1)} %refs_0_.1, bf16[8,9,128,128]{3,2,1,0:T(8,128)(2,1)} %collective-permute-done.4.refs_1_, ...), custom_call_target="tpu_custom_call" | custom-call | flops 3200000000 | bytes 12800000 | tf_op jit(solution)/shard_map/taps/pallas_call | solution.py:435
  98.3 4.4 %all-to-all-start.1 = ((bf16[8,2,37,16,128]{4,3,2,1,0:T(8,128)(2,1)}), bf16[8,2,37,16,128]{4,3,2,1,0:T(8,128)(2,1)S(1)}, u32[]{:S(2)}, u32[]{:S(2)}) async-start(bf16[8,2,37,16,128]{4,3,2,1,0:T(8,128)(2,1)} %get-tuple-element.32), calls=%async_computation.1 | async-start | bytes 4849664 | tf_op jit(solution)/shard_map/all_to_all | solution.py:758
  103.1 4.6 %grads.3 = (bf16[8,128,1152]{2,1,0:T(8,128)(2,1)}, f32[8,128]{1,0:T(8,128)}) custom-call(s32[8,2]{1,0:T(8,128)} %fusion.8.place, bf16[8,2,37,16,128]{4,3,2,1,0:T(8,128)(2,1)} %copy-done.7, bf16[8,128,1152]{2,1,0:T(8,128)(2,1)} %collective-permute-done.7.refs_0_), custom_call_target="tpu_custom_call" | custom-call | flops 300000000 | bytes 6000000 | tf_op jit(solution)/shard_map/grads/pallas_call | solution.py:543
  107.8 5.0 %grads.4 = (bf16[8,128,1152]{2,1,0:T(8,128)(2,1)}, f32[8,128]{1,0:T(8,128)}) custom-call(s32[8,2]{1,0:T(8,128)} %fusion.8.place, bf16[8,2,37,16,128]{4,3,2,1,0:T(8,128)(2,1)} %copy-done.7, f32[8,128]{1,0:T(8,128)} %get-tuple-element.35.refs_0_), custom_call_target="tpu_custom_call" | custom-call | flops 300000000 | bytes 6000000 | tf_op jit(solution)/shard_map/grads/pallas_call | solution.py:543
  112.8 1.2 collective-permute-start.12
  114.0 3.4 %collective-permute-start.13 = (bf16[8,128,1152]{2,1,0:T(8,128)(2,1)}, bf16[8,128,1152]{2,1,0:T(8,128)(2,1)}, u32[]{:S(2)}, u32[]{:S(2)}) collective-permute-start(bf16[8,128,1152]{2,1,0:T(8,128)(2,1)} %get-tuple-element.48), channel_id=1, source_target_pairs={{0,16},{8,24},{16,0},{24,8},{1,17},{9,25},{17,1},{25,9},{2,18},{10... | collective-permute-start | bytes 7077896 | tf_op jit(solution)/shard_map/ppermute | solution.py:754
  117.4 7.3 %grads.5 = (f32[8,128,1152]{2,1,0:T(8,128)}, f32[8,128]{1,0:T(8,128)}) custom-call(s32[8,2]{1,0:T(8,128)} %fusion.8.place, bf16[8,2,37,16,128]{4,3,2,1,0:T(8,128)(2,1)} %copy-done.7, f32[8,128]{1,0:T(8,128)} %get-tuple-element.35.refs_0_), custom_call_target="tpu_custom_call" | custom-call | flops 300000000 | bytes 6000000 | tf_op jit(solution)/shard_map/grads/pallas_call | solution.py:543
  124.7 33.5 %all-to-all-done.1.source = bf16[8,2,37,16,128]{4,3,2,1,0:T(8,128)(2,1)S(1)} async-done(((bf16[8,2,37,16,128]{4,3,2,1,0:T(8,128)(2,1)}), bf16[8,2,37,16,128]{4,3,2,1,0:T(8,128)(2,1)S(1)}, u32[]{:S(2)}, u32[]{:S(2)}) %all-to-all-start.1) | async-done | bytes 2424864 | tf_op jit(solution)/shard_map/all_to_all | solution.py:758
  158.9 2.0 %canvas.1 = (f32[5760,128]{1,0:T(8,128)S(1)}, bf16[144,128]{1,0:T(8,128)(2,1)S(1)}, bf16[144,128]{1,0:T(8,128)(2,1)S(1)}, f32[32,128]{1,0:T(8,128)S(1)}, f32[32,128]{1,0:T(8,128)S(1)}) custom-call(s32[2,8]{1,0:T(2,128)S(1)} %copy-done.3, s32[256]{0:T(256)S(1)} %copy-done.4, bf16[8,2,37,16,128]{4,3,2,1,0:T(8,128)(2,1)S(1)} %all-to-all-done.1.source, ...), custom_call_target="tpu_custom_call" | custom-call | bytes 6000000 | tf_op jit(solution)/shard_map/canvas/pallas_call | solution.py:657
  160.9 1.3 collective-permute-start.8
  162.2 1.3 collective-permute-start.9
  163.5 2.2 %outputs.1 = (bf16[32,128,128]{2,1,0:T(8,128)(2,1)}, f32[8,128]{1,0:T(8,128)S(1)}) custom-call(s32[2,8]{1,0:T(2,128)S(1)} %copy-done.3, s32[256]{0:T(256)S(1)} %copy-done.4, bf16[8,2,37,16,128]{4,3,2,1,0:T(8,128)(2,1)S(1)} %all-to-all-done.1.source), custom_call_target="tpu_custom_call" | custom-call | bytes 3000000 | tf_op jit(solution)/shard_map/outputs/pallas_call | solution.py:696
  165.8 2.9 %collective-permute-done.9.below.south = bf16[144,128]{1,0:T(8,128)(2,1)S(1)} collective-permute-done((bf16[144,128]{1,0:T(8,128)(2,1)S(1)}, bf16[144,128]{1,0:T(8,128)(2,1)S(1)}, u32[]{:S(2)}, u32[]{:S(2)}) %collective-permute-start.9) | collective-permute-done | bytes 36896 | tf_op jit(solution)/shard_map/ppermute | solution.py:745
  168.7 1.5 collective-permute-start.10
  170.3 3.2 %collective-permute-start.11 = (bf16[32,128]{1,0:T(8,128)(2,1)S(1)}, bf16[32,128]{1,0:T(8,128)(2,1)S(1)}, u32[]{:S(2)}, u32[]{:S(2)}) collective-permute-start(bf16[32,128]{1,0:T(8,128)(2,1)S(1)} %get-tuple-element.45), channel_id=1, source_target_pairs={{0,7},{1,0},{2,1},{3,2},{4,3},{5,4},{6,5},{7,6},{8,15},{9,8},{10,9... | collective-permute-start | bytes 24584 | tf_op jit(solution)/shard_map/ppermute | solution.py:745
  173.5 4.2 %bank.1 = (f32[8,9,128,128]{3,2,1,0:T(8,128)}, f32[8,128]{1,0:T(8,128)S(1)}) custom-call(f32[8,128,1152]{2,1,0:T(8,128)S(1)} %copy-done, bf16[8,128,1152]{2,1,0:T(8,128)(2,1)} %collective-permute-done.12.refs_1_, bf16[8,128,1152]{2,1,0:T(8,128)(2,1)} %collective-permute-done.13.refs_2_), custom_call_target="tpu_custom_call" | custom-call | bytes 12000000 | tf_op jit(solution)/shard_map/bank/pallas_call | solution.py:596
  177.8 1.1 finish.1
  (39 shorter events, 2.5 us)
Async XLA Ops:
  1.4 4.6 %collective-permute-start = (bf16[1,128,128]{2,1,0:T(8,128)(2,1)S(1)}, bf16[1,128,128]{2,1,0:T(8,128)(2,1)S(1)}, u32[]{:S(2)}, u32[]{:S(2)}) collective-permute-start(bf16[1,128,128]{2,1,0:T(8,128)(2,1)S(1)} %get-tuple-element.54), channel_id=1, source_target_pairs={{0,8},{8,16},{16,24},{1,9},{9,17},{17,25},{2,10},{10,18},{18,26},{... | collective-permute-start | bytes 98312 | tf_op jit(solution)/shard_map/ppermute | solution.py:745
  3.8 5.2 %collective-permute-start.1 = (bf16[1,128,128]{2,1,0:T(8,128)(2,1)S(1)}, bf16[1,128,128]{2,1,0:T(8,128)(2,1)S(1)}, u32[]{:S(2)}, u32[]{:S(2)}) collective-permute-start(bf16[1,128,128]{2,1,0:T(8,128)(2,1)S(1)} %get-tuple-element.53), channel_id=1, source_target_pairs={{8,0},{16,8},{24,16},{9,1},{17,9},{25,17},{10,2},{18,10},{26,18},{... | collective-permute-start | bytes 98312 | tf_op jit(solution)/shard_map/ppermute | solution.py:745
  6.0 13.9 %copy-start.1 = (bf16[1,128,128]{2,1,0:T(8,128)(2,1)}, bf16[1,128,128]{2,1,0:T(8,128)(2,1)S(1)}, u32[]{:S(2)}) copy-start(bf16[1,128,128]{2,1,0:T(8,128)(2,1)S(1)} %collective-permute-done.north) | copy-start | bytes 98308
  9.0 10.9 %copy-start.2 = (bf16[1,128,128]{2,1,0:T(8,128)(2,1)}, bf16[1,128,128]{2,1,0:T(8,128)(2,1)S(1)}, u32[]{:S(2)}) copy-start(bf16[1,128,128]{2,1,0:T(8,128)(2,1)S(1)} %collective-permute-done.1.south) | copy-start | bytes 98308
  9.0 54.0 %collective-permute-start.5 = (bf16[8,9,128,128]{3,2,1,0:T(8,128)(2,1)}, bf16[8,9,128,128]{3,2,1,0:T(8,128)(2,1)}, u32[]{:S(2)}, u32[]{:S(2)}) collective-permute-start(bf16[8,9,128,128]{3,2,1,0:T(8,128)(2,1)} %refs_0_.1), channel_id=1, source_target_pairs={{0,16},{8,24},{16,0},{24,8},{1,17},{9,25},{17,1},{25,9},{2,18},{10... | collective-permute-start | bytes 7077896 | tf_op jit(solution)/shard_map/ppermute | solution.py:754
  11.6 8.2 %collective-permute-start.2 = (bf16[34,128]{1,0:T(8,128)(2,1)S(1)}, bf16[34,128]{1,0:T(8,128)(2,1)S(1)}, u32[]{:S(2)}, u32[]{:S(2)}) collective-permute-start(bf16[34,128]{1,0:T(8,128)(2,1)S(1)} %get-tuple-element.27), channel_id=1, source_target_pairs={{0,1},{1,2},{2,3},{3,4},{4,5},{5,6},{6,7},{7,0},{8,9},{9,10},{10,1... | collective-permute-start | bytes 26120 | tf_op jit(solution)/shard_map/ppermute | solution.py:745
  13.1 6.7 %collective-permute-start.3 = (bf16[34,128]{1,0:T(8,128)(2,1)S(1)}, bf16[34,128]{1,0:T(8,128)(2,1)S(1)}, u32[]{:S(2)}, u32[]{:S(2)}) collective-permute-start(bf16[34,128]{1,0:T(8,128)(2,1)S(1)} %get-tuple-element.28), channel_id=1, source_target_pairs={{0,7},{1,0},{2,1},{3,2},{4,3},{5,4},{6,5},{7,6},{8,15},{9,8},{10,9... | collective-permute-start | bytes 26120 | tf_op jit(solution)/shard_map/ppermute | solution.py:745
  19.8 0.6 copy-start.8
  19.8 0.6 copy-start.9
  23.7 59.1 %all-to-all-start = ((bf16[8,2,37,16,128]{4,3,2,1,0:T(8,128)(2,1)}), bf16[8,2,37,16,128]{4,3,2,1,0:T(8,128)(2,1)S(1)}, u32[]{:S(2)}, u32[]{:S(2)}) async-start(bf16[8,2,37,16,128]{4,3,2,1,0:T(8,128)(2,1)} %dispatch_rings.1), calls=%async_computation | async-start | bytes 4849664 | tf_op jit(solution)/shard_map/all_to_all | solution.py:758
  27.8 56.0 %collective-permute-start.4 = (bf16[8,9,128,128]{3,2,1,0:T(8,128)(2,1)}, bf16[8,9,128,128]{3,2,1,0:T(8,128)(2,1)}, u32[]{:S(2)}, u32[]{:S(2)}) collective-permute-start(bf16[8,9,128,128]{3,2,1,0:T(8,128)(2,1)} %refs_0_.1), channel_id=1, source_target_pairs={{0,8},{8,0},{16,24},{24,16},{1,9},{9,1},{17,25},{25,17},{2,10},{10... | collective-permute-start | bytes 7077896 | tf_op jit(solution)/shard_map/ppermute | solution.py:749
  63.0 20.9 %collective-permute-start.6 = (bf16[8,9,128,128]{3,2,1,0:T(8,128)(2,1)}, bf16[8,9,128,128]{3,2,1,0:T(8,128)(2,1)}, u32[]{:S(2)}, u32[]{:S(2)}) collective-permute-start(bf16[8,9,128,128]{3,2,1,0:T(8,128)(2,1)} %collective-permute-done.5.refs_2_), channel_id=1, source_target_pairs={{0,8},{8,0},{16,24},{24,16},{1,9},{9,1},{17,25},{25,17},{2,10},{10... | collective-permute-start | bytes 7077896 | tf_op jit(solution)/shard_map/ppermute | solution.py:749
  82.8 1.4 copy-start.7
  98.2 4.9 %collective-permute-start.7 = (bf16[8,128,1152]{2,1,0:T(8,128)(2,1)}, bf16[8,128,1152]{2,1,0:T(8,128)(2,1)}, u32[]{:S(2)}, u32[]{:S(2)}) collective-permute-start(bf16[8,128,1152]{2,1,0:T(8,128)(2,1)} %get-tuple-element.34), channel_id=1, source_target_pairs={{0,8},{8,0},{16,24},{24,16},{1,9},{9,1},{17,25},{25,17},{2,10},{10... | collective-permute-start | bytes 7077896 | tf_op jit(solution)/shard_map/ppermute | solution.py:749
  98.3 60.0 %all-to-all-start.1 = ((bf16[8,2,37,16,128]{4,3,2,1,0:T(8,128)(2,1)}), bf16[8,2,37,16,128]{4,3,2,1,0:T(8,128)(2,1)S(1)}, u32[]{:S(2)}, u32[]{:S(2)}) async-start(bf16[8,2,37,16,128]{4,3,2,1,0:T(8,128)(2,1)} %get-tuple-element.32), calls=%async_computation.1 | async-start | bytes 4849664 | tf_op jit(solution)/shard_map/all_to_all | solution.py:758
  107.8 50.5 %copy-start.3 = (s32[2,8]{1,0:T(2,128)S(1)}, s32[2,8]{1,0:T(2,128)}, u32[]{:S(2)}) copy-start(s32[2,8]{1,0:T(2,128)} %experts.7) | copy-start | bytes 196
  107.8 50.5 %copy-start.4 = (s32[256]{0:T(256)S(1)}, s32[256]{0:T(256)}, u32[]{:S(2)}) copy-start(s32[256]{0:T(256)} %owner.7) | copy-start | bytes 3076
  112.8 45.4 %copy-start.5 = (f32[8,128]{1,0:T(8,128)S(1)}, f32[8,128]{1,0:T(8,128)}, u32[]{:S(2)}) copy-start(f32[8,128]{1,0:T(8,128)} %get-tuple-element.36.refs_0_) | copy-start | bytes 12292
  112.8 60.7 %collective-permute-start.12 = (bf16[8,128,1152]{2,1,0:T(8,128)(2,1)}, bf16[8,128,1152]{2,1,0:T(8,128)(2,1)}, u32[]{:S(2)}, u32[]{:S(2)}) collective-permute-start(bf16[8,128,1152]{2,1,0:T(8,128)(2,1)} %get-tuple-element.47), channel_id=1, source_target_pairs={{0,8},{8,0},{16,24},{24,16},{1,9},{9,1},{17,25},{25,17},{2,10},{10... | collective-permute-start | bytes 7077896 | tf_op jit(solution)/shard_map/ppermute | solution.py:749
  114.0 59.5 %collective-permute-start.13 = (bf16[8,128,1152]{2,1,0:T(8,128)(2,1)}, bf16[8,128,1152]{2,1,0:T(8,128)(2,1)}, u32[]{:S(2)}, u32[]{:S(2)}) collective-permute-start(bf16[8,128,1152]{2,1,0:T(8,128)(2,1)} %get-tuple-element.48), channel_id=1, source_target_pairs={{0,16},{8,24},{16,0},{24,8},{1,17},{9,25},{17,1},{25,9},{2,18},{10... | collective-permute-start | bytes 7077896 | tf_op jit(solution)/shard_map/ppermute | solution.py:754
  158.2 0.7 copy-start.6
  158.9 14.6 %copy-start = (f32[8,128,1152]{2,1,0:T(8,128)S(1)}, f32[8,128,1152]{2,1,0:T(8,128)}, u32[]{:S(2)}) copy-start(f32[8,128,1152]{2,1,0:T(8,128)} %get-tuple-element.46.refs_0_) | copy-start | bytes 14155780
  160.9 4.8 %collective-permute-start.8 = (bf16[144,128]{1,0:T(8,128)(2,1)S(1)}, bf16[144,128]{1,0:T(8,128)(2,1)S(1)}, u32[]{:S(2)}, u32[]{:S(2)}) collective-permute-start(bf16[144,128]{1,0:T(8,128)(2,1)S(1)} %get-tuple-element.39), channel_id=1, source_target_pairs={{0,8},{8,16},{16,24},{1,9},{9,17},{17,25},{2,10},{10,18},{18,26},{... | collective-permute-start | bytes 110600 | tf_op jit(solution)/shard_map/ppermute | solution.py:745
  162.2 6.5 %collective-permute-start.9 = (bf16[144,128]{1,0:T(8,128)(2,1)S(1)}, bf16[144,128]{1,0:T(8,128)(2,1)S(1)}, u32[]{:S(2)}, u32[]{:S(2)}) collective-permute-start(bf16[144,128]{1,0:T(8,128)(2,1)S(1)} %get-tuple-element.40), channel_id=1, source_target_pairs={{8,0},{16,8},{24,16},{9,1},{17,9},{25,17},{10,2},{18,10},{26,18},{... | collective-permute-start | bytes 110600 | tf_op jit(solution)/shard_map/ppermute | solution.py:745
  168.7 9.0 %collective-permute-start.10 = (bf16[32,128]{1,0:T(8,128)(2,1)S(1)}, bf16[32,128]{1,0:T(8,128)(2,1)S(1)}, u32[]{:S(2)}, u32[]{:S(2)}) collective-permute-start(bf16[32,128]{1,0:T(8,128)(2,1)S(1)} %get-tuple-element.44), channel_id=1, source_target_pairs={{0,1},{1,2},{2,3},{3,4},{4,5},{5,6},{6,7},{7,0},{8,9},{9,10},{10,1... | collective-permute-start | bytes 24584 | tf_op jit(solution)/shard_map/ppermute | solution.py:745
  170.3 7.5 %collective-permute-start.11 = (bf16[32,128]{1,0:T(8,128)(2,1)S(1)}, bf16[32,128]{1,0:T(8,128)(2,1)S(1)}, u32[]{:S(2)}, u32[]{:S(2)}) collective-permute-start(bf16[32,128]{1,0:T(8,128)(2,1)S(1)} %get-tuple-element.45), channel_id=1, source_target_pairs={{0,7},{1,0},{2,1},{3,2},{4,3},{5,4},{6,5},{7,6},{8,15},{9,8},{10,9... | collective-permute-start | bytes 24584 | tf_op jit(solution)/shard_map/ppermute | solution.py:745

commit v5 on v4

--- a/solution.py
+++ b/solution.py
@@ -798,30 +798,27 @@
         distant = to_chip(tied(kernel_bank, (first, last)), -k)
         banks += [distant, to_other_core(distant)]
 
-    results, beside = taps(
-        place, arrived, banks, tuple(2 * k + 1 for k in range(1, chips))
-    )
+    results, beside = taps(place, arrived, banks, tuple(range(1, 2 * chips, 2)))
     results = exchange(results)
     beside = [to_other_core(part) for part in beside]
-    chip_parts, tokens = [], []
+    terms, tokens = [], []
     for k in range(1, chips):
-        part, token = grads(*slots, 2 * k, shape, [beside[k - 1]], tokens, BF16)
-        chip_parts.append(to_chip(part, k))
+        part, token = grads(*slots, 2 * k, shape, [beside[k]], tokens, BF16)
+        terms.append(to_chip(part, k))
         tokens = [token]
-    core_part, core_token = grads(*slots, 1, shape, [], tokens, BF16)
-    own_part, own_token = grads(*slots, 0, shape, [], tokens, F32)
-    terms = [own_part, to_other_core(core_part)] + chip_parts
+    own_part, token = grads(*slots, 0, shape, [], tokens, F32)
+    terms = [own_part, beside[0]] + terms
 
     canvas, top, bottom, left, right = canvas_of(
-        block_expert, owner, results, [core_token, own_token], fields.shape, per
+        block_expert, owner, results, [token], fields.shape, per
     )
     above = across(bottom, "lat", 1, False)
     below = across(top, "lat", -1, False)
-    outputs, token = outputs_of(block_expert, owner, results, fields.shape, per)
+    grad_bank, token = bank_of(terms, shape)
     left, right = corners_of(above, below, left, right, token)
     from_west = across(right, "lon", 1, True)
     from_east = across(left, "lon", -1, True)
-    grad_bank, token = bank_of(terms, shape)
+    outputs, token = outputs_of(block_expert, owner, results, fields.shape, per)
     grad_fields = finish(canvas, above, below, from_west, from_east, token, fields.shape)
     return (outputs, grad_fields, grad_bank)
 

time: 182 us -> 185 us (1.016)
  waiting for transfers between devices: 93.8 us -> 97.7 us
  Pallas kernels: 47.3 us -> 44.1 us
  local copies, waits for them, and re-layouts: 3.52 us -> 5.83 us
    all_to_all x2, waiting for transfers between devices: 52.3 us -> 59.6 us  [exchange(): return lax.all_to_all(array, 'lon', split_axis=0, concat_axis=0, tiled=True)]
    pallas_call x3 -> x2, Pallas kernels: 17 us -> 10.6 us  [grads(): pl.pallas_call(functools.partial(grads_kernel, piece, per, len(added), le...]
    pallas_call x1, Pallas kernels: 14 us -> 17.2 us  [taps(): pl.pallas_call(functools.partial(taps_kernel, size, per, wanted, len(bank...]
    ppermute x8, waiting for transfers between devices: 5.9 us -> 2.98 us  [across(): return lax.ppermute(array, axis, pairs)]
    unnamed x20 -> x18, local copies, waits for them, and re-layouts: 1.66 us -> 3.96 us
  transfers between devices with their start and end apart: 16 -> 16, of which waited for: 6 -> 4; matrix products, arithmetic and copies ran while one was open for 1% -> 1% of each run, Pallas kernels for 18% -> 14%
where the time goes in v5:
time: 185 us; the launch traced here: 182 us
  waiting for transfers between devices  97.7 us (53%)
  Pallas kernels  44.1 us (24%)
  starting transfers between devices  32.4 us (18%)
  local copies, waits for them, and re-layouts  5.83 us (3%)
    all_to_all x2, waiting for transfers between devices, exchange(): return lax.all_to_all(array, 'lon', split_axis=0, concat_axis=0, tiled=True)  59.6 us
    ppermute x2, waiting for transfers between devices, to_chip(): lax.ppermute(array, 'lat', [(i, (i + 2 * shift) % count) for i in range(c...  35.1 us
    pallas_call x1, Pallas kernels, taps(): pl.pallas_call(functools.partial(taps_kernel, size, per, wanted, len(bank...  17.2 us
    ppermute x8, starting transfers between devices, across(): return lax.ppermute(array, axis, pairs)  15.7 us
    pallas_call x2, Pallas kernels, grads(): pl.pallas_call(functools.partial(grads_kernel, piece, per, len(added), le...  10.6 us
    all_to_all x2, starting transfers between devices, exchange(): return lax.all_to_all(array, 'lon', split_axis=0, concat_axis=0, tiled=True)  8.97 us
    ppermute x2, starting transfers between devices, to_chip(): lax.ppermute(array, 'lat', [(i, (i + 2 * shift) % count) for i in range(c...  6.59 us
    pallas_call x1, Pallas kernels, bank_of(): pl.pallas_call(functools.partial(bank_kernel, len(terms)), out_shape=[jax...  4.21 us
  transfers between devices with their start and end apart: 16, of which 4 were waited for; matrix products, arithmetic and copies ran while one was open for 1% of the time, Pallas kernels for 14%

profile of v5, /device:TPU:0, one launch (start us, length us, event | category | flops | bytes accessed | tf_op | source)
XLA Modules:
  0.0 181.8 jit_solution(11467777084254977732)
XLA Ops:
  0.6 0.8 fusion.15
  1.4 2.3 %collective-permute-start = (bf16[1,128,128]{2,1,0:T(8,128)(2,1)S(1)}, bf16[1,128,128]{2,1,0:T(8,128)(2,1)S(1)}, u32[]{:S(2)}, u32[]{:S(2)}) collective-permute-start(bf16[1,128,128]{2,1,0:T(8,128)(2,1)S(1)} %get-tuple-element.52), channel_id=1, source_target_pairs={{0,8},{8,16},{16,24},{1,9},{9,17},{17,25},{2,10},{10,18},{18,26},{... | collective-permute-start | bytes 98312 | tf_op jit(solution)/shard_map/ppermute | solution.py:745
  3.8 1.3 collective-permute-start.1
  5.1 0.9 fusion.14
  6.0 3.0 %collective-permute-done.1.south = bf16[1,128,128]{2,1,0:T(8,128)(2,1)S(1)} collective-permute-done((bf16[1,128,128]{2,1,0:T(8,128)(2,1)S(1)}, bf16[1,128,128]{2,1,0:T(8,128)(2,1)S(1)}, u32[]{:S(2)}, u32[]{:S(2)}) %collective-permute-start.1) | collective-permute-done | bytes 32800 | tf_op jit(solution)/shard_map/ppermute | solution.py:745
  9.0 2.6 %collective-permute-start.5 = (bf16[8,9,128,128]{3,2,1,0:T(8,128)(2,1)}, bf16[8,9,128,128]{3,2,1,0:T(8,128)(2,1)}, u32[]{:S(2)}, u32[]{:S(2)}) collective-permute-start(bf16[8,9,128,128]{3,2,1,0:T(8,128)(2,1)} %refs_0_.1), channel_id=1, source_target_pairs={{0,16},{8,24},{16,0},{24,8},{1,17},{9,25},{17,1},{25,9},{2,18},{10... | collective-permute-start | bytes 7077896 | tf_op jit(solution)/shard_map/ppermute | solution.py:754
  11.6 1.5 collective-permute-start.2
  13.1 3.2 %collective-permute-start.3 = (bf16[34,128]{1,0:T(8,128)(2,1)S(1)}, bf16[34,128]{1,0:T(8,128)(2,1)S(1)}, u32[]{:S(2)}, u32[]{:S(2)}) collective-permute-start(bf16[34,128]{1,0:T(8,128)(2,1)S(1)} %get-tuple-element.27), channel_id=1, source_target_pairs={{0,7},{1,0},{2,1},{3,2},{4,3},{5,4},{6,5},{7,6},{8,15},{9,8},{10,9... | collective-permute-start | bytes 26120 | tf_op jit(solution)/shard_map/ppermute | solution.py:745
  16.3 3.5 %dispatch_own.1 = (bf16[8,2,37,16,128]{4,3,2,1,0:T(8,128)(2,1)}, f32[8,128]{1,0:T(8,128)}) custom-call(s32[2,8]{1,0:T(2,128)} %experts.7, s32[256]{0:T(256)} %owner.7, bf16[32,128,128]{2,1,0:T(8,128)(2,1)} %fields.3, bf16[32,128,128]{2,1,0:T(8,128)(2,1)} %cot.1), custom_call_target="tpu_custom_call" | custom-call | bytes 6000000 | tf_op jit(solution)/shard_map/dispatch_own/pallas_call | solution.py:122
  19.9 0.5 copy-done.7
  20.4 3.3 %dispatch_rings.1 = bf16[8,2,37,16,128]{4,3,2,1,0:T(8,128)(2,1)} custom-call(s32[2,8]{1,0:T(2,128)} %experts.7, s32[256]{0:T(256)} %owner.7, bf16[32,128,128]{2,1,0:T(8,128)(2,1)} %fields.3, bf16[1,128,128]{2,1,0:T(8,128)(2,1)} %copy-done.1, bf16[1,128,128]{2,1,0:T(8,128)(2,1)} %copy-done.2, ...), custom_call_target="tpu_custom_call", output_to_operand_aliasing={{}: (7, {})} | custom-call | bytes 3000000 | tf_op jit(solution)/shard_map/dispatch_rings/pallas_call | solution.py:247
  23.7 4.1 %all-to-all-start = ((bf16[8,2,37,16,128]{4,3,2,1,0:T(8,128)(2,1)}), bf16[8,2,37,16,128]{4,3,2,1,0:T(8,128)(2,1)S(1)}, u32[]{:S(2)}, u32[]{:S(2)}) async-start(bf16[8,2,37,16,128]{4,3,2,1,0:T(8,128)(2,1)} %dispatch_rings.1), calls=%async_computation | async-start | bytes 4849664 | tf_op jit(solution)/shard_map/all_to_all | solution.py:758
  27.8 35.1 %collective-permute-done.5.refs_2_ = bf16[8,9,128,128]{3,2,1,0:T(8,128)(2,1)} collective-permute-done((bf16[8,9,128,128]{3,2,1,0:T(8,128)(2,1)}, bf16[8,9,128,128]{3,2,1,0:T(8,128)(2,1)}, u32[]{:S(2)}, u32[]{:S(2)}) %collective-permute-start.5) | collective-permute-done | bytes 2359328 | tf_op jit(solution)/shard_map/ppermute | solution.py:754
  63.0 1.0 collective-permute-start.6
  64.0 18.8 %all-to-all-done.slots_in = bf16[8,2,37,16,128]{4,3,2,1,0:T(8,128)(2,1)S(1)} async-done(((bf16[8,2,37,16,128]{4,3,2,1,0:T(8,128)(2,1)}), bf16[8,2,37,16,128]{4,3,2,1,0:T(8,128)(2,1)S(1)}, u32[]{:S(2)}, u32[]{:S(2)}) %all-to-all-start) | async-done | bytes 2424864 | tf_op jit(solution)/shard_map/all_to_all | solution.py:758
  83.0 0.9 fusion.8.place
  84.2 17.2 %taps.1 = (bf16[8,2,37,16,128]{4,3,2,1,0:T(8,128)(2,1)}, bf16[8,128,1152]{2,1,0:T(8,128)(2,1)}, bf16[8,128,1152]{2,1,0:T(8,128)(2,1)}) custom-call(s32[8,2]{1,0:T(8,128)} %fusion.8.place, bf16[8,2,37,16,128]{4,3,2,1,0:T(8,128)(2,1)} %copy-done.6, bf16[8,9,128,128]{3,2,1,0:T(8,128)(2,1)} %refs_0_.1, bf16[8,9,128,128]{3,2,1,0:T(8,128)(2,1)} %collective-permute-done.4.refs_1_, ...), custom_call_target="tpu_custom_call" | custom-call | flops 3200000000 | bytes 12800000 | tf_op jit(solution)/shard_map/taps/pallas_call | solution.py:435
  101.5 4.9 %all-to-all-start.1 = ((bf16[8,2,37,16,128]{4,3,2,1,0:T(8,128)(2,1)}), bf16[8,2,37,16,128]{4,3,2,1,0:T(8,128)(2,1)S(1)}, u32[]{:S(2)}, u32[]{:S(2)}) async-start(bf16[8,2,37,16,128]{4,3,2,1,0:T(8,128)(2,1)} %get-tuple-element.31), calls=%async_computation.1 | async-start | bytes 4849664 | tf_op jit(solution)/shard_map/all_to_all | solution.py:758
  106.4 4.6 %grads.2 = (bf16[8,128,1152]{2,1,0:T(8,128)(2,1)}, f32[8,128]{1,0:T(8,128)}) custom-call(s32[8,2]{1,0:T(8,128)} %fusion.8.place, bf16[8,2,37,16,128]{4,3,2,1,0:T(8,128)(2,1)} %copy-done.6, bf16[8,128,1152]{2,1,0:T(8,128)(2,1)} %collective-permute-done.7.refs_0_), custom_call_target="tpu_custom_call" | custom-call | flops 300000000 | bytes 6000000 | tf_op jit(solution)/shard_map/grads/pallas_call | solution.py:543
  110.9 4.0 %collective-permute-start.11 = (bf16[8,128,1152]{2,1,0:T(8,128)(2,1)}, bf16[8,128,1152]{2,1,0:T(8,128)(2,1)}, u32[]{:S(2)}, u32[]{:S(2)}) collective-permute-start(bf16[8,128,1152]{2,1,0:T(8,128)(2,1)} %get-tuple-element.43), channel_id=1, source_target_pairs={{0,16},{8,24},{16,0},{24,8},{1,17},{9,25},{17,1},{25,9},{2,18},{10... | collective-permute-start | bytes 7077896 | tf_op jit(solution)/shard_map/ppermute | solution.py:754
  114.9 6.0 %grads.3 = (f32[8,128,1152]{2,1,0:T(8,128)}, f32[8,128]{1,0:T(8,128)}) custom-call(s32[8,2]{1,0:T(8,128)} %fusion.8.place, bf16[8,2,37,16,128]{4,3,2,1,0:T(8,128)(2,1)} %copy-done.6, f32[8,128]{1,0:T(8,128)} %get-tuple-element.34.refs_0_), custom_call_target="tpu_custom_call" | custom-call | flops 300000000 | bytes 6000000 | tf_op jit(solution)/shard_map/grads/pallas_call | solution.py:543
  121.0 40.8 %all-to-all-done.1.source = bf16[8,2,37,16,128]{4,3,2,1,0:T(8,128)(2,1)S(1)} async-done(((bf16[8,2,37,16,128]{4,3,2,1,0:T(8,128)(2,1)}), bf16[8,2,37,16,128]{4,3,2,1,0:T(8,128)(2,1)S(1)}, u32[]{:S(2)}, u32[]{:S(2)}) %all-to-all-start.1) | async-done | bytes 2424864 | tf_op jit(solution)/shard_map/all_to_all | solution.py:758
  161.8 0.7 copy-done.5
  162.5 2.0 %canvas.1 = (f32[5760,128]{1,0:T(8,128)S(1)}, bf16[144,128]{1,0:T(8,128)(2,1)S(1)}, bf16[144,128]{1,0:T(8,128)(2,1)S(1)}, f32[32,128]{1,0:T(8,128)S(1)}, f32[32,128]{1,0:T(8,128)S(1)}) custom-call(s32[2,8]{1,0:T(2,128)S(1)} %copy-done.3, s32[256]{0:T(256)S(1)} %copy-done.4, bf16[8,2,37,16,128]{4,3,2,1,0:T(8,128)(2,1)S(1)} %all-to-all-done.1.source, ...), custom_call_target="tpu_custom_call" | custom-call | bytes 6000000 | tf_op jit(solution)/shard_map/canvas/pallas_call | solution.py:657
  164.5 1.3 collective-permute-start.8
  165.8 1.3 collective-permute-start.9
  167.1 2.3 %copy-done = f32[8,128,1152]{2,1,0:T(8,128)S(1)} copy-done((f32[8,128,1152]{2,1,0:T(8,128)S(1)}, f32[8,128,1152]{2,1,0:T(8,128)}, u32[]{:S(2)}) %copy-start) | copy-done | bytes 4718616
  169.4 4.2 %bank.1 = (f32[8,9,128,128]{3,2,1,0:T(8,128)}, f32[8,128]{1,0:T(8,128)S(1)}) custom-call(f32[8,128,1152]{2,1,0:T(8,128)S(1)} %copy-done, bf16[8,128,1152]{2,1,0:T(8,128)(2,1)} %collective-permute-done.10.refs_1_, bf16[8,128,1152]{2,1,0:T(8,128)(2,1)} %collective-permute-done.11.refs_2_), custom_call_target="tpu_custom_call" | custom-call | bytes 12000000 | tf_op jit(solution)/shard_map/bank/pallas_call | solution.py:596
  173.7 1.5 collective-permute-start.12
  175.2 3.3 %collective-permute-start.13 = (bf16[32,128]{1,0:T(8,128)(2,1)S(1)}, bf16[32,128]{1,0:T(8,128)(2,1)S(1)}, u32[]{:S(2)}, u32[]{:S(2)}) collective-permute-start(bf16[32,128]{1,0:T(8,128)(2,1)S(1)} %get-tuple-element.46), channel_id=1, source_target_pairs={{0,7},{1,0},{2,1},{3,2},{4,3},{5,4},{6,5},{7,6},{8,15},{9,8},{10,9... | collective-permute-start | bytes 24584 | tf_op jit(solution)/shard_map/ppermute | solution.py:745
  178.5 2.2 %outputs.1 = (bf16[32,128,128]{2,1,0:T(8,128)(2,1)}, f32[8,128]{1,0:T(8,128)S(1)}) custom-call(s32[2,8]{1,0:T(2,128)S(1)} %copy-done.3, s32[256]{0:T(256)S(1)} %copy-done.4, bf16[8,2,37,16,128]{4,3,2,1,0:T(8,128)(2,1)S(1)} %all-to-all-done.1.source), custom_call_target="tpu_custom_call" | custom-call | bytes 3000000 | tf_op jit(solution)/shard_map/outputs/pallas_call | solution.py:696
  180.7 1.1 finish.1
  (36 shorter events, 0.7 us)
Async XLA Ops:
  1.4 4.6 %collective-permute-start = (bf16[1,128,128]{2,1,0:T(8,128)(2,1)S(1)}, bf16[1,128,128]{2,1,0:T(8,128)(2,1)S(1)}, u32[]{:S(2)}, u32[]{:S(2)}) collective-permute-start(bf16[1,128,128]{2,1,0:T(8,128)(2,1)S(1)} %get-tuple-element.52), channel_id=1, source_target_pairs={{0,8},{8,16},{16,24},{1,9},{9,17},{17,25},{2,10},{10,18},{18,26},{... | collective-permute-start | bytes 98312 | tf_op jit(solution)/shard_map/ppermute | solution.py:745
  3.8 5.2 %collective-permute-start.1 = (bf16[1,128,128]{2,1,0:T(8,128)(2,1)S(1)}, bf16[1,128,128]{2,1,0:T(8,128)(2,1)S(1)}, u32[]{:S(2)}, u32[]{:S(2)}) collective-permute-start(bf16[1,128,128]{2,1,0:T(8,128)(2,1)S(1)} %get-tuple-element.51), channel_id=1, source_target_pairs={{8,0},{16,8},{24,16},{9,1},{17,9},{25,17},{10,2},{18,10},{26,18},{... | collective-permute-start | bytes 98312 | tf_op jit(solution)/shard_map/ppermute | solution.py:745
  6.0 13.9 %copy-start.1 = (bf16[1,128,128]{2,1,0:T(8,128)(2,1)}, bf16[1,128,128]{2,1,0:T(8,128)(2,1)S(1)}, u32[]{:S(2)}) copy-start(bf16[1,128,128]{2,1,0:T(8,128)(2,1)S(1)} %collective-permute-done.north) | copy-start | bytes 98308
  9.0 10.9 %copy-start.2 = (bf16[1,128,128]{2,1,0:T(8,128)(2,1)}, bf16[1,128,128]{2,1,0:T(8,128)(2,1)S(1)}, u32[]{:S(2)}) copy-start(bf16[1,128,128]{2,1,0:T(8,128)(2,1)S(1)} %collective-permute-done.1.south) | copy-start | bytes 98308
  9.0 54.0 %collective-permute-start.5 = (bf16[8,9,128,128]{3,2,1,0:T(8,128)(2,1)}, bf16[8,9,128,128]{3,2,1,0:T(8,128)(2,1)}, u32[]{:S(2)}, u32[]{:S(2)}) collective-permute-start(bf16[8,9,128,128]{3,2,1,0:T(8,128)(2,1)} %refs_0_.1), channel_id=1, source_target_pairs={{0,16},{8,24},{16,0},{24,8},{1,17},{9,25},{17,1},{25,9},{2,18},{10... | collective-permute-start | bytes 7077896 | tf_op jit(solution)/shard_map/ppermute | solution.py:754
  11.6 8.2 %collective-permute-start.2 = (bf16[34,128]{1,0:T(8,128)(2,1)S(1)}, bf16[34,128]{1,0:T(8,128)(2,1)S(1)}, u32[]{:S(2)}, u32[]{:S(2)}) collective-permute-start(bf16[34,128]{1,0:T(8,128)(2,1)S(1)} %get-tuple-element.26), channel_id=1, source_target_pairs={{0,1},{1,2},{2,3},{3,4},{4,5},{5,6},{6,7},{7,0},{8,9},{9,10},{10,1... | collective-permute-start | bytes 26120 | tf_op jit(solution)/shard_map/ppermute | solution.py:745
  13.1 6.7 %collective-permute-start.3 = (bf16[34,128]{1,0:T(8,128)(2,1)S(1)}, bf16[34,128]{1,0:T(8,128)(2,1)S(1)}, u32[]{:S(2)}, u32[]{:S(2)}) collective-permute-start(bf16[34,128]{1,0:T(8,128)(2,1)S(1)} %get-tuple-element.27), channel_id=1, source_target_pairs={{0,7},{1,0},{2,1},{3,2},{4,3},{5,4},{6,5},{7,6},{8,15},{9,8},{10,9... | collective-permute-start | bytes 26120 | tf_op jit(solution)/shard_map/ppermute | solution.py:745
  19.8 0.6 copy-start.7
  19.8 0.6 copy-start.8
  23.7 59.1 %all-to-all-start = ((bf16[8,2,37,16,128]{4,3,2,1,0:T(8,128)(2,1)}), bf16[8,2,37,16,128]{4,3,2,1,0:T(8,128)(2,1)S(1)}, u32[]{:S(2)}, u32[]{:S(2)}) async-start(bf16[8,2,37,16,128]{4,3,2,1,0:T(8,128)(2,1)} %dispatch_rings.1), calls=%async_computation | async-start | bytes 4849664 | tf_op jit(solution)/shard_map/all_to_all | solution.py:758
  27.8 56.0 %collective-permute-start.4 = (bf16[8,9,128,128]{3,2,1,0:T(8,128)(2,1)}, bf16[8,9,128,128]{3,2,1,0:T(8,128)(2,1)}, u32[]{:S(2)}, u32[]{:S(2)}) collective-permute-start(bf16[8,9,128,128]{3,2,1,0:T(8,128)(2,1)} %refs_0_.1), channel_id=1, source_target_pairs={{0,8},{8,0},{16,24},{24,16},{1,9},{9,1},{17,25},{25,17},{2,10},{10... | collective-permute-start | bytes 7077896 | tf_op jit(solution)/shard_map/ppermute | solution.py:749
  63.0 20.9 %collective-permute-start.6 = (bf16[8,9,128,128]{3,2,1,0:T(8,128)(2,1)}, bf16[8,9,128,128]{3,2,1,0:T(8,128)(2,1)}, u32[]{:S(2)}, u32[]{:S(2)}) collective-permute-start(bf16[8,9,128,128]{3,2,1,0:T(8,128)(2,1)} %collective-permute-done.5.refs_2_), channel_id=1, source_target_pairs={{0,8},{8,0},{16,24},{24,16},{1,9},{9,1},{17,25},{25,17},{2,10},{10... | collective-permute-start | bytes 7077896 | tf_op jit(solution)/shard_map/ppermute | solution.py:749
  82.8 1.4 copy-start.6
  101.4 5.0 %collective-permute-start.7 = (bf16[8,128,1152]{2,1,0:T(8,128)(2,1)}, bf16[8,128,1152]{2,1,0:T(8,128)(2,1)}, u32[]{:S(2)}, u32[]{:S(2)}) collective-permute-start(bf16[8,128,1152]{2,1,0:T(8,128)(2,1)} %get-tuple-element.33), channel_id=1, source_target_pairs={{0,8},{8,0},{16,24},{24,16},{1,9},{9,1},{17,25},{25,17},{2,10},{10... | collective-permute-start | bytes 7077896 | tf_op jit(solution)/shard_map/ppermute | solution.py:749
  101.5 60.3 %all-to-all-start.1 = ((bf16[8,2,37,16,128]{4,3,2,1,0:T(8,128)(2,1)}), bf16[8,2,37,16,128]{4,3,2,1,0:T(8,128)(2,1)S(1)}, u32[]{:S(2)}, u32[]{:S(2)}) async-start(bf16[8,2,37,16,128]{4,3,2,1,0:T(8,128)(2,1)} %get-tuple-element.31), calls=%async_computation.1 | async-start | bytes 4849664 | tf_op jit(solution)/shard_map/all_to_all | solution.py:758
  106.3 60.8 %collective-permute-start.10 = (bf16[8,128,1152]{2,1,0:T(8,128)(2,1)}, bf16[8,128,1152]{2,1,0:T(8,128)(2,1)}, u32[]{:S(2)}, u32[]{:S(2)}) collective-permute-start(bf16[8,128,1152]{2,1,0:T(8,128)(2,1)} %get-tuple-element.42), channel_id=1, source_target_pairs={{0,8},{8,0},{16,24},{24,16},{1,9},{9,1},{17,25},{25,17},{2,10},{10... | collective-permute-start | bytes 7077896 | tf_op jit(solution)/shard_map/ppermute | solution.py:749
  110.9 50.9 %copy-start.3 = (s32[2,8]{1,0:T(2,128)S(1)}, s32[2,8]{1,0:T(2,128)}, u32[]{:S(2)}) copy-start(s32[2,8]{1,0:T(2,128)} %experts.7) | copy-start | bytes 196
  110.9 50.9 %copy-start.4 = (s32[256]{0:T(256)S(1)}, s32[256]{0:T(256)}, u32[]{:S(2)}) copy-start(s32[256]{0:T(256)} %owner.7) | copy-start | bytes 3076
  110.9 56.2 %collective-permute-start.11 = (bf16[8,128,1152]{2,1,0:T(8,128)(2,1)}, bf16[8,128,1152]{2,1,0:T(8,128)(2,1)}, u32[]{:S(2)}, u32[]{:S(2)}) collective-permute-start(bf16[8,128,1152]{2,1,0:T(8,128)(2,1)} %get-tuple-element.43), channel_id=1, source_target_pairs={{0,16},{8,24},{16,0},{24,8},{1,17},{9,25},{17,1},{25,9},{2,18},{10... | collective-permute-start | bytes 7077896 | tf_op jit(solution)/shard_map/ppermute | solution.py:754
  161.8 0.7 copy-start.5
  164.5 9.2 %collective-permute-start.8 = (bf16[144,128]{1,0:T(8,128)(2,1)S(1)}, bf16[144,128]{1,0:T(8,128)(2,1)S(1)}, u32[]{:S(2)}, u32[]{:S(2)}) collective-permute-start(bf16[144,128]{1,0:T(8,128)(2,1)S(1)} %get-tuple-element.37), channel_id=1, source_target_pairs={{0,8},{8,16},{16,24},{1,9},{9,17},{17,25},{2,10},{10,18},{18,26},{... | collective-permute-start | bytes 110600 | tf_op jit(solution)/shard_map/ppermute | solution.py:745
  165.8 7.9 %collective-permute-start.9 = (bf16[144,128]{1,0:T(8,128)(2,1)S(1)}, bf16[144,128]{1,0:T(8,128)(2,1)S(1)}, u32[]{:S(2)}, u32[]{:S(2)}) collective-permute-start(bf16[144,128]{1,0:T(8,128)(2,1)S(1)} %get-tuple-element.38), channel_id=1, source_target_pairs={{8,0},{16,8},{24,16},{9,1},{17,9},{25,17},{10,2},{18,10},{26,18},{... | collective-permute-start | bytes 110600 | tf_op jit(solution)/shard_map/ppermute | solution.py:745
  167.1 2.3 %copy-start = (f32[8,128,1152]{2,1,0:T(8,128)S(1)}, f32[8,128,1152]{2,1,0:T(8,128)}, u32[]{:S(2)}) copy-start(f32[8,128,1152]{2,1,0:T(8,128)} %get-tuple-element.41.refs_0_) | copy-start | bytes 14155780
  173.7 7.0 %collective-permute-start.12 = (bf16[32,128]{1,0:T(8,128)(2,1)S(1)}, bf16[32,128]{1,0:T(8,128)(2,1)S(1)}, u32[]{:S(2)}, u32[]{:S(2)}) collective-permute-start(bf16[32,128]{1,0:T(8,128)(2,1)S(1)} %get-tuple-element.45), channel_id=1, source_target_pairs={{0,1},{1,2},{2,3},{3,4},{4,5},{5,6},{6,7},{7,0},{8,9},{9,10},{10,1... | collective-permute-start | bytes 24584 | tf_op jit(solution)/shard_map/ppermute | solution.py:745
  175.2 5.5 %collective-permute-start.13 = (bf16[32,128]{1,0:T(8,128)(2,1)S(1)}, bf16[32,128]{1,0:T(8,128)(2,1)S(1)}, u32[]{:S(2)}, u32[]{:S(2)}) collective-permute-start(bf16[32,128]{1,0:T(8,128)(2,1)S(1)} %get-tuple-element.46), channel_id=1, source_target_pairs={{0,7},{1,0},{2,1},{3,2},{4,3},{5,4},{6,5},{7,6},{8,15},{9,8},{10,9... | collective-permute-start | bytes 24584 | tf_op jit(solution)/shard_map/ppermute | solution.py:745
